TPU v7x, 32 devices: a whole 2x2x4 slice. The times are simulated.
32 devices in a mesh: pipe: 4 (over x, core), dp: 2 (over y), tensor: 4 (over z).
Axes of the slice: x: 2, y: 2, z: 4, core: 2. Of those that a mesh axis runs over, the one named last changes fastest.
Arguments:
- tokens: bfloat16 [4, 512, 5120], P('pipe', 'dp', 'tensor'), may hold values from -6 to 6
- norm_gain: bfloat16 [4, 5120], P('pipe'), may hold values from 0.099609375 to 1.8984375
- w_query: bfloat16 [4, 5120, 4096], P('pipe', None, 'tensor'), may hold values from -0.078125 to 0.078125
- key_value_weight: bfloat16 [4, 5120, 1024], P('pipe', None, 'tensor'), may hold values from -0.078125 to 0.078125
- w_out: bfloat16 [4, 4096, 5120], P('pipe', 'tensor'), may hold values from -0.5 to 0.5
- cache_kv: bfloat16 [4, 2048, 4, 256], P('pipe', 'dp', 'tensor'), may hold values from -80 to 80
- cache_lengths: int32 [4, 4], P('pipe'), may hold values from 1 to 1024, 2048 in all within a row
- row_lengths: int32 [4, 4], P('pipe'), may hold values from 1 to 256, 512 in all within a row
- block_owner: int32 [4, 4, 1], P('pipe'), may hold values from 0 to 1; in each aligned block of 2 rows (0 to 1, 2 to 3, ..., all dimensions but the last counted through in order) no two rows name the same one
Outputs:
- handed: bfloat16 [4, 512, 5120], P('pipe', 'dp', 'tensor')
- blocks_held: float32 [4, 2], P('pipe', 'dp')
Inputs may be any that keep to these rules, and one draw needn't show every extreme that they name: `block_owner`: the 2 aligned row blocks of one data rank at one section hand at most 1 block to any one data rank. `cache_lengths`: each section's documents hold 2048 cached positions in all; the longest exactly 1024. `row_lengths`: each section's documents hold 512 rows in all; the longest exactly 256.
All inputs are finite; a program needn't handle non-finite values.
Results may differ from a plain program's by a relative error of at most 0.012.
The roundings to bfloat16 on the way count: a program that leaves them out, or rounds other values in their place, can miss the bound.
Values may be sent and summed in bfloat16 or wider, within the bound.
No kernel may reach another device: no remote copies, remote signals or barrier semaphores. Data moves between devices by JAX's collectives and lax.ppermute only.
A program may use at most 192 MiB of HBM per device.

v0:
```python
import jax
import jax.numpy as jnp
from jax import lax
from jax.sharding import PartitionSpec as P

HEAD_SIZE = 128
BLOCK_ROWS = 128


EPS = 1e-06
NEG = -1e30


def from_behind(block, axis, distance):
    devices = range(lax.axis_size(axis))
    route = [((i - distance) % len(devices), i) for i in devices]
    return lax.ppermute(block, axis, route)


def doc_ids(lengths, amount):
    bounds = jnp.cumsum(lengths)
    places = jnp.arange(amount, dtype=jnp.int32)
    return jnp.sum((places[:, None] >= bounds[None, :]).astype(jnp.int32), axis=1)


def block_loads(row_len, cache_len, amount, block_size):
    row_doc = doc_ids(row_len, amount)
    bounds = jnp.cumsum(row_len)
    starts = bounds - row_len
    offsets = cache_len - starts + 1
    doc_numbers = jnp.arange(row_len.shape[0], dtype=jnp.int32)
    matches = (row_doc[:, None] == doc_numbers[None, :]).astype(jnp.int32)
    per_row = jnp.sum(matches * offsets[None, :], axis=1) + jnp.arange(amount, dtype=jnp.int32)
    return jnp.sum(per_row.reshape(amount // block_size, block_size), axis=1)


def on_device(
    tokens,
    norm_gain,
    w_query,
    key_value_weight,
    w_out,
    cache_kv,
    cache_lengths,
    row_lengths,
    block_owner,
):
    rank_count = lax.axis_size("dp")
    my_rank = lax.axis_index("dp")
    own_rows = tokens[0]
    row_count = own_rows.shape[0]
    blocks_here = row_count // BLOCK_ROWS
    pair_slots = (blocks_here + rank_count - 1) // rank_count
    slot_count = rank_count * pair_slots
    head_width = w_query.shape[2]
    kv_heads = key_value_weight.shape[2] // (2 * HEAD_SIZE)
    group_list = head_width // HEAD_SIZE // kv_heads
    cache_rows = cache_kv.shape[1]
    shard_span = cache_rows + row_count
    cache_doc = doc_ids(cache_lengths[0], cache_rows * rank_count)
    row_doc = doc_ids(row_lengths[0], row_count * rank_count)
    full_rows = lax.all_gather(own_rows, "tensor", axis=1, tiled=True)
    widened = full_rows.astype(jnp.float32)
    factor = lax.rsqrt(jnp.mean(widened * widened, axis=1, keepdims=True) + EPS)
    normed = (widened * factor * norm_gain[0].astype(jnp.float32)).astype(jnp.bfloat16)
    query_rows = jnp.dot(normed, w_query[0], preferred_element_type=jnp.float32).astype(
        jnp.bfloat16
    )
    key_value_rows = jnp.dot(
        normed, key_value_weight[0], preferred_element_type=jnp.float32
    ).astype(jnp.bfloat16)
    owners = block_owner[0, :, 0]
    owner_grid = owners.reshape(rank_count, blocks_here)
    block_ids = jnp.arange(blocks_here, dtype=jnp.int32)
    earlier = block_ids[None, :] < block_ids[:, None]
    same_owner = owner_grid[:, :, None] == owner_grid[:, None, :]
    order_in = jnp.sum((same_owner & earlier[None]).astype(jnp.int32), axis=2)
    mine_owner = lax.dynamic_index_in_dim(owner_grid, my_rank, 0, keepdims=False)
    mine_order = lax.dynamic_index_in_dim(order_in, my_rank, 0, keepdims=False)
    mine_slot = mine_owner * pair_slots + mine_order
    slot_ids = jnp.arange(slot_count, dtype=jnp.int32)
    choose = (mine_slot[:, None] == slot_ids[None, :]).astype(jnp.bfloat16)
    outgoing = jnp.einsum(
        "jr,jqe->rqe",
        choose,
        query_rows.reshape(blocks_here, BLOCK_ROWS, head_width),
        preferred_element_type=jnp.float32,
    ).astype(jnp.bfloat16)
    arrived = lax.all_to_all(outgoing, "dp", split_axis=0, concat_axis=0, tiled=True)
    pair_ids = jnp.arange(pair_slots, dtype=jnp.int32)
    slot_hits = (owner_grid == my_rank)[:, :, None] & (
        order_in[:, :, None] == pair_ids[None, None, :]
    )
    slot_live = jnp.any(slot_hits, axis=1).reshape(slot_count)
    which_block = jnp.sum(slot_hits.astype(jnp.int32) * block_ids[None, :, None], axis=1)
    source_ids = jnp.arange(rank_count, dtype=jnp.int32)
    slot_start = ((source_ids[:, None] * blocks_here + which_block) * BLOCK_ROWS).reshape(
        slot_count
    )
    slot_rows = slot_start[:, None] + jnp.arange(BLOCK_ROWS, dtype=jnp.int32)[None, :]
    slot_docs = jnp.take(row_doc, slot_rows)
    history_rows = jnp.concatenate(
        [cache_kv[0].reshape(cache_rows, kv_heads * 2 * HEAD_SIZE), key_value_rows], axis=0
    )
    start_state = (
        jnp.full((slot_count, BLOCK_ROWS, kv_heads, group_list), NEG, jnp.float32),
        jnp.zeros((slot_count, BLOCK_ROWS, kv_heads, group_list), jnp.float32),
        jnp.zeros((slot_count, BLOCK_ROWS, kv_heads, group_list, HEAD_SIZE), jnp.float32),
    )
    piece = lax.all_gather(history_rows, "dp", axis=0, tiled=True)
    length = piece.shape[0]
    places = jnp.arange(length, dtype=jnp.int32)
    shard_of = places // shard_span
    offset = places - shard_of * shard_span
    in_cache = offset < cache_rows
    cache_index = jnp.clip(shard_of * cache_rows + offset, 0, cache_rows * rank_count - 1)
    row_index = jnp.clip(shard_of * row_count + offset - cache_rows, 0, row_count * rank_count - 1)
    key_doc = jnp.where(in_cache, jnp.take(cache_doc, cache_index), jnp.take(row_doc, row_index))
    key_row = jnp.where(in_cache, -1, row_index)
    shaped = piece.reshape(length, kv_heads, 2 * HEAD_SIZE)
    key_part = shaped[:, :, :HEAD_SIZE]
    value_part = shaped[:, :, HEAD_SIZE:]

    def per_slot(slot_index, carried):
        visible = (slot_docs[slot_index][:, None] == key_doc[None, :]) & (
            key_row[None, :] <= slot_rows[slot_index][:, None]
        )

        def update(carried_in):
            old_max, old_sum, old_acc = carried_in
            query_slot = arrived[slot_index].reshape(BLOCK_ROWS, kv_heads, group_list, HEAD_SIZE)
            scores = jnp.einsum(
                "qkgd,nkd->qkgn", query_slot, key_part, preferred_element_type=jnp.float32
            ) * HEAD_SIZE ** (-0.5)
            visible_wide = visible[:, None, None, :]
            scores = jnp.where(visible_wide, scores, NEG)
            prior = old_max[slot_index]
            newest = jnp.maximum(prior, jnp.max(scores, axis=3))
            weights = jnp.where(visible_wide, jnp.exp(scores - newest[..., None]), 0.0)
            rescale = jnp.exp(prior - newest)
            summed = old_sum[slot_index] * rescale + jnp.sum(weights, axis=3)
            product = jnp.einsum(
                "qkgn,nkd->qkgd",
                weights.astype(jnp.bfloat16),
                value_part,
                preferred_element_type=jnp.float32,
            )
            accrued = old_acc[slot_index] * rescale[..., None] + product
            return (
                old_max.at[slot_index].set(newest),
                old_sum.at[slot_index].set(summed),
                old_acc.at[slot_index].set(accrued),
            )

        def keep_state(carried_in):
            return carried_in

        return lax.cond(slot_live[slot_index] & jnp.any(visible), update, keep_state, carried)

    final_max, final_sum, final_acc = lax.fori_loop(0, slot_count, per_slot, start_state)
    safe_sum = jnp.where(final_sum > 0.0, final_sum, 1.0)
    attended = (
        (final_acc / safe_sum[..., None])
        .astype(jnp.bfloat16)
        .reshape(slot_count, BLOCK_ROWS, head_width)
    )
    splits = lax.axis_size("tensor")
    width_split = w_out.shape[2] // splits
    split_weight = w_out[0].reshape(head_width, splits, width_split)
    by_pair = attended.reshape(rank_count, pair_slots, BLOCK_ROWS, head_width)
    partial_value = jnp.einsum(
        "dpqe,etf->dtpqf", by_pair, split_weight, preferred_element_type=jnp.float32
    ).astype(jnp.bfloat16)
    flat_parts = partial_value.reshape(rank_count * splits * pair_slots, BLOCK_ROWS, width_split)
    came = lax.all_to_all(flat_parts, ("dp", "tensor"), split_axis=0, concat_axis=0, tiled=True)
    came = came.reshape(rank_count, splits, pair_slots, BLOCK_ROWS, width_split)
    reduced = jnp.sum(came.astype(jnp.float32), axis=1).reshape(slot_count, BLOCK_ROWS, width_split)
    summed_rows = jnp.take(reduced, mine_slot, axis=0).reshape(row_count, width_split)
    section_out = (own_rows.astype(jnp.float32) + summed_rows).astype(jnp.bfloat16)
    handed = from_behind(section_out[None], "pipe", 1)
    loads = block_loads(row_lengths[0], cache_lengths[0], row_count * rank_count, BLOCK_ROWS)
    work_sum = jnp.sum((owners == my_rank).astype(jnp.int32) * loads)
    divisor = BLOCK_ROWS * (cache_rows * rank_count // 2 + row_count * rank_count // 2)
    blocks_held = (work_sum.astype(jnp.float32) / jnp.float32(divisor)).reshape(1, 1)
    return (handed, blocks_held)


def solution(mesh):
    placed = (
        P("pipe", "dp", "tensor"),
        P("pipe", None),
        P("pipe", None, "tensor"),
        P("pipe", None, "tensor"),
        P("pipe", "tensor", None),
        P("pipe", "dp", "tensor", None),
        P("pipe", None),
        P("pipe", None),
        P("pipe", None, None),
    )
    return jax.shard_map(
        on_device,
        mesh=mesh,
        in_specs=placed,
        out_specs=(P("pipe", "dp", "tensor"), P("pipe", "dp")),
        check_vma=False,
    )
```

profile of v0, /device:TPU:0, one launch (start us, length us, event | category | flops | bytes accessed | tf_op | source)
XLA Modules:
  0.0 274.8 jit_solution(4989024712115714808)
XLA Ops:
  16.0 51.1 %all-gather.6.cloned.1.call-done = bf16[1,256,5120]{2,1,0:T(8,128)(2,1)} async-done(((bf16[1,256,1280]{2,1,0:T(8,128)(2,1)}), bf16[1,256,5120]{2,1,0:T(8,128)(2,1)}) %all-gather.6.cloned.1.call-update) | async-done | bytes 2621456 | tf_op jit(solution)/shard_map/all_gather | solution.py:62
  67.1 2.3 fusion.46
  69.4 2.6 fusion.59
  73.0 7.7 %fusion.56 = bf16[256,1024]{1,0:T(8,128)(2,1)S(1)} fusion(bf16[1,5120,1024]{2,1,0:T(8,128)(2,1)} %param.21, bf16[1,256,5120]{2,1,0:T(8,128)(2,1)} %all-gather.6.cloned.1.call-done, f32[5120]{0:T(1024)S(1)} %bitcast.198, f32[256]{0:T(256)S(1)} %add_rsqrt_fusion), kind=kOutput, calls=%fused_computation.70 | convolution fusion | flops 2689859584 | bytes 13652992 | tf_op jit(solution)/shard_map/dot_general | solution.py:66
  82.4 3.7 %all-to-all-start = ((bf16[2,128,1024]{2,1,0:T(8,128)(2,1)}), bf16[2,128,1024]{2,1,0:T(8,128)(2,1)S(1)}, u32[]{:S(2)}, u32[]{:S(2)}) async-start(bf16[2,128,1024]{2,1,0:T(8,128)(2,1)} %copy.29), calls=%async_computation | async-start | bytes 1048576 | tf_op jit(solution)/shard_map/all_to_all | solution.py:89
  86.2 15.4 %gather_fusion.2 = s32[2560]{0:T(1024)S(1)} fusion(s32[512]{0:T(512)S(1)} %convert_reduce_fusion.2, s32[3072]{0:T(1024)S(1)} %pad_clamp_fusion), kind=kCustom, calls=%fused_computation.2 | custom fusion | bytes 30720 | tf_op jit(solution)/shard_map/jit(_take)/gather | solution.py:118
  101.6 19.4 %reshape_squeeze.11 = bf16[1024,4,1280]{2,1,0:T(4,128)(2,1)} reshape(bf16[1,1024,5120]{2,1,0:T(8,128)(2,1)} %param.23) | data formatting | bytes 20971520 | tf_op jit(solution)/shard_map/reshape;squeeze | solution.py:169
  121.0 13.6 %gather_fusion.1 = s32[2560]{0:T(1024)S(1)} fusion(s32[2048]{0:T(1024)S(1)} %convert_reduce_fusion.1, s32[3072]{0:T(1024)S(1)} %pad_clamp_fusion.1), kind=kCustom, calls=%fused_computation.1 | custom fusion | bytes 30720 | tf_op jit(solution)/shard_map/jit(_take)/gather | solution.py:118
  134.9 2.2 fusion.84
  137.2 35.7 %while.21 = (s32[]{:T(128)}, f32[2,128,1,8]{1,3,2,0:T(8,128)S(1)}, f32[2,128,1,8]{1,3,2,0:T(8,128)S(1)}, f32[2,128,1,8,128]{4,1,3,2,0:T(8,128)S(1)}, pred[2]{0:T...) while((s32[]{:T(128)}, f32[2,128,1,8]{1,3,2,0:T(8,128)S(1)}, ...), condition=%wide.region_16.17_spmd.clone, body=%wide.region_8.16_spmd.clone.sunk | while | flops 1378007040 | bytes 79001232 | solution.py:160
  140.2 14.8 %conditional.3 = ((f32[2,128,1,8]{1,3,2,0:T(8,128)S(1)}, f32[2,128,1,8]{1,3,2,0:T(8,128)S(1)}, f32[2,128,1,8,128]{4,1,3,2,0:T(8,128)S(1)})) conditional(s32[]{:T(128)} %convert_element_type.132, (f32[2,128,1,8]{1,3,2,0:T(8,128)S(1)}, f32[2,128,1,8]{1,3,2,0:T(8,128)S(1)}, f32[2,128,1,8,128]{4,1,3,2,0:T(8,128)S(1)}) %tuple.74, (s32[]{:T(128)}, ...), branch_computations={%region_10.10_spmd, %region_11.15_spmd} | conditional | flops 1376655360 | bytes 78639528 | solution.py:158
  142.4 3.1 %fusion.4 = f32[128,8]{0,1:T(8,128)S(1)} fusion(f32[128,8,2560]{2,0,1:T(8,128)S(1)} %get-tuple-element.381, f32[128,8]{0,1:T(8,128)S(1)} %get-tuple-element.373, pred[128,2560]{1,0:T(8,128)(4,1)S(1)} %get-tuple-element.251), kind=kLoop, calls=%fused_computation.9 | loop fusion | flops 13106176 | bytes 10821632 | tf_op jit(solution)/shard_map/while/body/eval_jaxpr/cond/branch_1_fun/reduce_sum | solution.py:141
  148.5 6.4 %fusion.21 = f32[2,128,1,8,128]{4,1,3,2,0:T(8,128)S(1)} fusion(f32[2,128,1,8,128]{4,1,3,2,0:T(8,128)S(1)} %get-tuple-element.255, s32[]{:T(128)} %select_n.131, f32[1,128,1,8,128]{4,1,3,2,0:T(8,128)S(1)} %constant_dynamic-slice_fusion, f32[128,8,2560]{2,0,1:T(8,128)} %copy-done.2, f32[128,8]{0,1:T(8,128)S(1)} %get-tuple-element.373, ...), kind=kOutput, calls=%fused_computation.17 | convolution fusion | flops 684589056 | bytes 12525573 | tf_op jit(solution)/shard_map/while/body/eval_jaxpr/cond/branch_1_fun/qkgn,nkd->qkgd/dot_general | solution.py:142
  157.9 14.8 %conditional.3 = ((f32[2,128,1,8]{1,3,2,0:T(8,128)S(1)}, f32[2,128,1,8]{1,3,2,0:T(8,128)S(1)}, f32[2,128,1,8,128]{4,1,3,2,0:T(8,128)S(1)})) conditional(s32[]{:T(128)} %convert_element_type.132, (f32[2,128,1,8]{1,3,2,0:T(8,128)S(1)}, f32[2,128,1,8]{1,3,2,0:T(8,128)S(1)}, f32[2,128,1,8,128]{4,1,3,2,0:T(8,128)S(1)}) %tuple.74, (s32[]{:T(128)}, ...), branch_computations={%region_10.10_spmd, %region_11.15_spmd} | conditional | flops 1376655360 | bytes 78639528 | solution.py:158
  158.0 2.1 fusion.2
  160.1 3.1 %fusion.4 = f32[128,8]{0,1:T(8,128)S(1)} fusion(f32[128,8,2560]{2,0,1:T(8,128)S(1)} %get-tuple-element.381, f32[128,8]{0,1:T(8,128)S(1)} %get-tuple-element.373, pred[128,2560]{1,0:T(8,128)(4,1)S(1)} %get-tuple-element.251), kind=kLoop, calls=%fused_computation.9 | loop fusion | flops 13106176 | bytes 10821632 | tf_op jit(solution)/shard_map/while/body/eval_jaxpr/cond/branch_1_fun/reduce_sum | solution.py:141
  166.2 6.4 %fusion.21 = f32[2,128,1,8,128]{4,1,3,2,0:T(8,128)S(1)} fusion(f32[2,128,1,8,128]{4,1,3,2,0:T(8,128)S(1)} %get-tuple-element.255, s32[]{:T(128)} %select_n.131, f32[1,128,1,8,128]{4,1,3,2,0:T(8,128)S(1)} %constant_dynamic-slice_fusion, f32[128,8,2560]{2,0,1:T(8,128)} %copy-done.2, f32[128,8]{0,1:T(8,128)S(1)} %get-tuple-element.373, ...), kind=kOutput, calls=%fused_computation.17 | convolution fusion | flops 684589056 | bytes 12525573 | tf_op jit(solution)/shard_map/while/body/eval_jaxpr/cond/branch_1_fun/qkgn,nkd->qkgd/dot_general | solution.py:142
  173.4 8.5 %fusion.49 = bf16[2,128,4,1280]{3,1,2,0:T(8,128)(2,1)} fusion(bf16[2,128,1024,1]{1,2,3,0:T(8,128)(2,1)S(1)} %bitcast.195, bf16[1024,4,1280]{2,1,0:T(4,128)(2,1)} %reshape_squeeze.11), kind=kOutput, calls=%fused_computation.64 | convolution fusion | flops 2685665280 | bytes 13631488 | tf_op jit(solution)/shard_map/dpqe,etf->dtpqf/dot_general | solution.py:171
  181.9 4.5 %all-to-all-start.1 = ((bf16[8,128,1280]{2,1,0:T(8,128)(2,1)}), bf16[8,128,1280]{2,1,0:T(8,128)(2,1)}, u32[]{:S(2)}, u32[]{:S(2)}) async-start(bf16[8,128,1280]{2,1,0:T(8,128)(2,1)} %bitcast.43), calls=%async_computation.1 | async-start | bytes 5242880 | tf_op jit(solution)/shard_map/all_to_all | solution.py:175
  186.6 60.5 %all-to-all-done.1 = bf16[8,128,1280]{2,1,0:T(8,128)(2,1)} async-done(((bf16[8,128,1280]{2,1,0:T(8,128)(2,1)}), bf16[8,128,1280]{2,1,0:T(8,128)(2,1)}, u32[]{:S(2)}, u32[]{:S(2)}) %all-to-all-start.1) | async-done | bytes 2621472 | tf_op jit(solution)/shard_map/all_to_all | solution.py:175
  247.0 3.4 %convert_reduce_fusion = f32[2,128,1280]{2,1,0:T(8,128)} fusion(bf16[8,128,1280]{2,1,0:T(8,128)(2,1)} %all-to-all-done.1), kind=kLoop, calls=%fused_computation.63 | loop fusion | flops 2293760 | bytes 3932160 | tf_op jit(solution)/shard_map/reduce_sum | solution.py:177
  250.4 3.0 %gather_fusion.3 = f32[2,128,1280]{2,1,0:T(8,128)} fusion(f32[2,128,1280]{2,1,0:T(8,128)} %convert_reduce_fusion, s32[1024]{0:T(1024)S(1)} %pad_clamp_fusion.2), kind=kCustom, calls=%fused_computation.3 | custom fusion | bytes 2621448 | tf_op jit(solution)/shard_map/jit(_take)/gather | solution.py:178
  253.4 2.4 fusion.55
  257.3 8.7 %collective-permute-done = bf16[1,256,1280]{2,1,0:T(8,128)(2,1)S(1)} collective-permute-done((bf16[1,256,1280]{2,1,0:T(8,128)(2,1)}, bf16[1,256,1280]{2,1,0:T(8,128)(2,1)S(1)}, u32[]{:S(2)}, u32[]{:S(2)}) %collective-permute-start) | collective-permute-done | bytes 655392 | tf_op jit(solution)/shard_map/ppermute | solution.py:17
  (100 shorter events, 25.7 us)
Async XLA Ops:
  7.2 62.3 %copy-start = (bf16[1,5120,256]{2,1,0:T(8,128)(2,1)S(1)}, bf16[1,5120,256]{2,1,0:T(8,128)(2,1)}, u32[]{:S(2)}) copy-start(bf16[1,5120,256]{2,1,0:T(8,128)(2,1)} %param.22) | copy-start | bytes 7864324
  7.2 59.9 %all-gather.6.cloned.1.call-start = ((), (), s32[]{:S(2)}) async-start(), calls=%async_computation.3 | async-start | bytes 3276800 | tf_op jit(solution)/shard_map/all_gather | solution.py:62
  7.9 127.0 %all-gather.4.cloned.1.call-start = ((), (), s32[]{:S(2)}) async-start(), calls=%async_computation.2 | async-start | bytes 1966080 | tf_op jit(solution)/shard_map/all_gather | solution.py:110
  16.0 56.1 %copy-start.4 = (bf16[1,1024,1,256]{3,1,2,0:T(8,128)(2,1)S(1)}, bf16[1,1024,1,256]{3,1,2,0:T(8,128)(2,1)}, u32[]{:S(2)}) copy-start(bf16[1,1024,1,256]{3,1,2,0:T(8,128)(2,1)} %param.24) | copy-start | bytes 1572868
  82.4 52.3 %all-to-all-start = ((bf16[2,128,1024]{2,1,0:T(8,128)(2,1)}), bf16[2,128,1024]{2,1,0:T(8,128)(2,1)S(1)}, u32[]{:S(2)}, u32[]{:S(2)}) async-start(bf16[2,128,1024]{2,1,0:T(8,128)(2,1)} %copy.29), calls=%async_computation | async-start | bytes 1048576 | tf_op jit(solution)/shard_map/all_to_all | solution.py:89
  142.3 3.8 %copy-start.2 = (f32[128,8,2560]{2,0,1:T(8,128)}, f32[128,8,2560]{2,0,1:T(8,128)S(1)}, u32[]{:S(2)}) copy-start(f32[128,8,2560]{2,0,1:T(8,128)S(1)} %get-tuple-element.381) | copy-start | bytes 31457284 | tf_op jit(solution)/shard_map/while/body/eval_jaxpr/cond
  142.4 3.8 %copy-start.5 = (s32[4]{0:T(128)S(1)}, s32[4]{0:T(128)}, u32[]{:S(2)}) copy-start(s32[4]{0:T(128)} %constant.191.clone) | copy-start | bytes 52 | tf_op jit(solution)/shard_map/while/body/eval_jaxpr/cond
  142.4 5.4 %copy-start.9 = (s32[5]{0:T(128)S(1)}, s32[5]{0:T(128)}, u32[]{:S(2)}) copy-start(s32[5]{0:T(128)} %constant.197.clone) | copy-start | bytes 64 | tf_op jit(solution)/shard_map/while/body/eval_jaxpr/cond
  160.1 3.8 %copy-start.2 = (f32[128,8,2560]{2,0,1:T(8,128)}, f32[128,8,2560]{2,0,1:T(8,128)S(1)}, u32[]{:S(2)}) copy-start(f32[128,8,2560]{2,0,1:T(8,128)S(1)} %get-tuple-element.381) | copy-start | bytes 31457284 | tf_op jit(solution)/shard_map/while/body/eval_jaxpr/cond
  160.1 3.8 %copy-start.5 = (s32[4]{0:T(128)S(1)}, s32[4]{0:T(128)}, u32[]{:S(2)}) copy-start(s32[4]{0:T(128)} %constant.191.clone) | copy-start | bytes 52 | tf_op jit(solution)/shard_map/while/body/eval_jaxpr/cond
  160.1 5.4 %copy-start.9 = (s32[5]{0:T(128)S(1)}, s32[5]{0:T(128)}, u32[]{:S(2)}) copy-start(s32[5]{0:T(128)} %constant.197.clone) | copy-start | bytes 64 | tf_op jit(solution)/shard_map/while/body/eval_jaxpr/cond
  181.9 71.5 %copy-start.3 = (bf16[1,256,1280]{2,1,0:T(8,128)(2,1)S(1)}, bf16[1,256,1280]{2,1,0:T(8,128)(2,1)}, u32[]{:S(2)}) copy-start(bf16[1,256,1280]{2,1,0:T(8,128)(2,1)} %param.19) | copy-start | bytes 1966084
  181.9 65.1 %all-to-all-start.1 = ((bf16[8,128,1280]{2,1,0:T(8,128)(2,1)}), bf16[8,128,1280]{2,1,0:T(8,128)(2,1)}, u32[]{:S(2)}, u32[]{:S(2)}) async-start(bf16[8,128,1280]{2,1,0:T(8,128)(2,1)} %bitcast.43), calls=%async_computation.1 | async-start | bytes 5242880 | tf_op jit(solution)/shard_map/all_to_all | solution.py:175
  186.4 69.4 %copy-start.6 = (s32[1,4]{1,0:T(1,128)S(1)}, s32[1,4]{1,0:T(1,128)}, u32[]{:S(2)}) copy-start(s32[1,4]{1,0:T(1,128)} %param.26) | copy-start | bytes 52
  186.4 69.3 %copy-start.7 = (s32[1,4]{1,0:T(1,128)S(1)}, s32[1,4]{1,0:T(1,128)}, u32[]{:S(2)}) copy-start(s32[1,4]{1,0:T(1,128)} %param.25) | copy-start | bytes 52
  186.4 69.6 %copy-start.8 = (s32[1,4,1]{1,2,0:T(1,128)S(1)}, s32[1,4,1]{1,2,0:T(1,128)}, u32[]{:S(2)}) copy-start(s32[1,4,1]{1,2,0:T(1,128)} %param.27) | copy-start | bytes 52
  186.5 80.4 %copy-start.1 = (bf16[1,5120,256]{2,1,0:T(8,128)(2,1)S(1)}, bf16[1,5120,256]{2,1,0:T(8,128)(2,1)}, u32[]{:S(2)}) copy-start(bf16[1,5120,256]{2,1,0:T(8,128)(2,1)} %param.22) | copy-start | bytes 7864324
  255.8 10.2 %collective-permute-start = (bf16[1,256,1280]{2,1,0:T(8,128)(2,1)}, bf16[1,256,1280]{2,1,0:T(8,128)(2,1)S(1)}, u32[]{:S(2)}, u32[]{:S(2)}) collective-permute-start(bf16[1,256,1280]{2,1,0:T(8,128)(2,1)} %fusion.55), channel_id=1, source_target_pairs={{24,0},{0,8},{8,16},{16,24},{25,1},{1,9},{9,17},{17,25},{26,2},{2,... | collective-permute-start | bytes 1966088 | tf_op jit(solution)/shard_map/ppermute | solution.py:17
Sparse Core Ops, SparseCore 0:
  9.6 57.4 all-gather.5
  73.1 28.6 all-gather.3
where the time goes:
time: 276 us; the launch traced here: 275 us
  waiting for transfers between devices  121 us (44%)
  local copies, waits for them, and re-layouts  61.9 us (22%)
  matrix products  36.6 us (13%)
  other arithmetic  28 us (10%)
  between operations  16.1 us (6%)
  starting transfers between devices  8.26 us (3%)
  loops' own time  2.9 us (1%)
    all_to_all x1, waiting for transfers between devices, on_device(): lax.all_to_all(flat_parts, ('dp', 'tensor'), split_axis=0, concat_axis=0,...  60.5 us
    all_gather x1, waiting for transfers between devices, on_device(): full_rows = lax.all_gather(own_rows, 'tensor', axis=1, tiled=True)  51.1 us
    another operation x1, local copies, waits for them, and re-layouts, on_device(): split_weight = w_out[0].reshape(head_width, splits, width_split)  19.4 us
    gather x1, local copies, waits for them, and re-layouts, on_device(): jnp.take(row_doc, row_index)  15.4 us
    gather x1, local copies, waits for them, and re-layouts, on_device(): jnp.take(cache_doc, cache_index)  13.6 us
    dot_general x2, matrix products, update(): jnp.einsum('qkgn,nkd->qkgd', weights.astype(jnp.bfloat16), value_part, pr...  12.9 us
    ppermute x1, waiting for transfers between devices, from_behind(): return lax.ppermute(block, axis, route)  8.7 us
    dot_general x1, matrix products, on_device(): jnp.einsum('dpqe,etf->dtpqf', by_pair, split_weight, preferred_element_ty...  8.48 us
  transfers between devices with their start and end apart: 5, of which 3 were waited for; matrix products, arithmetic and copies ran while one was open for 24% of the time, Pallas kernels for 0%

commit v1 on v0

v1 whole, which is shorter than its diff:
```python
import functools

import jax
import jax.numpy as jnp
from jax import lax
from jax.experimental import pallas as pl
from jax.experimental.pallas import tpu as pltpu
from jax.sharding import PartitionSpec as P

HEAD_SIZE = 128
BLOCK_ROWS = 128
EPS = 1e-06
NEG = -1e30
LOG2E = 1.4426950408889634
MIB = 1024 * 1024
SCORE_BYTES = 13 * MIB
PARTS = 4
WEIGHT_CUTS = 4
KEY_TILE = 384


def swap(block, axis, pairs):
    return lax.ppermute(block, axis, pairs)


def xor_pairs(count, mask, among=None):
    return [(i, i ^ mask) for i in range(count) if among is None or i in among]


def after(value, *others):
    return lax.optimization_barrier((value, *others))[0]


def in_vmem(x):
    return pltpu.with_memory_space_constraint(x, pltpu.VMEM)


def in_hbm(x):
    return pltpu.with_memory_space_constraint(x, pltpu.HBM)


def resident(kernel, name, outs, args, scalars=(), weights=(), scratch=(), limit=16, moved=0):
    spaces = [pl.BlockSpec(memory_space=pltpu.SMEM)] * len(scalars)
    spaces += [pl.BlockSpec(memory_space=pltpu.VMEM)] * len(args)
    spaces += [pl.BlockSpec(memory_space=pl.ANY)] * len(weights)
    return pl.pallas_call(
        kernel,
        in_specs=spaces,
        out_specs=[pl.BlockSpec(memory_space=pltpu.VMEM)] * len(outs),
        out_shape=[
            jax.ShapeDtypeStruct(shape, dtype) if shape == (1, 1) else pltpu.VMEM(shape, dtype)
            for shape, dtype in outs
        ],
        scratch_shapes=list(scratch),
        compiler_params=pltpu.CompilerParams(vmem_limit_bytes=limit * MIB),
        cost_estimate=pl.CostEstimate(flops=0, bytes_accessed=moved, transcendentals=0),
        name=name,
    )(*scalars, *[in_vmem(x) for x in args], *[in_hbm(w) for w in weights])


def start_copies(copies):
    for copy in copies:
        copy.start()


def wait_copies(copies):
    for copy in copies:
        copy.wait()


def row_copies(w_ref, start, held, sems):
    cuts = sems.shape[0]
    rows = held.shape[0] // cuts
    return [
        pltpu.make_async_copy(
            w_ref.at[pl.ds(pl.multiple_of(start + at * rows, 16), rows)],
            held.at[pl.ds(at * rows, rows)],
            sems.at[at],
        )
        for at in range(cuts)
    ]


def column_copies(w_ref, start, held, sems):
    cuts = sems.shape[0]
    rows, width = held.shape
    rows = rows // cuts
    return [
        pltpu.make_async_copy(
            w_ref.at[pl.ds(at * rows, rows), pl.ds(pl.multiple_of(start, 128), width)],
            held.at[pl.ds(at * rows, rows)],
            sems.at[at],
        )
        for at in range(cuts)
    ]


def store_normed(out_ref, x_ref, factor_ref, gain_ref, place):
    width = x_ref.shape[1]
    gain = gain_ref[:, pl.ds(pl.multiple_of(place * width, 128), width)].astype(jnp.float32)
    for c in range(0, width, 128):
        wide = x_ref[:, c : c + 128].astype(jnp.float32)
        out_ref[:, c : c + 128] = (wide * factor_ref[...] * gain[:, c : c + 128]).astype(jnp.bfloat16)


def documents(lengths, docs):
    starts, ends, last = [], [], jnp.int32(0)
    for d in range(docs):
        starts.append(last)
        last = last + lengths[0, d]
        ends.append(last)
    return starts, ends


def early_kernel(
    own, near, far, rest_ref, gain_ref, wq_ref, wkv_ref,
    q_ref, kv_ref, factor_ref, wq_held, wkv_held, normed, sems_q, sems_kv,
):
    place = lax.axis_index("tensor")
    width = own.shape[1]
    shards = (own, near, far)
    copies = []
    for at in range(len(shards)):
        first, spot = (place ^ at) * width, pl.ds(at * width, width)
        copies += row_copies(wkv_ref, first, wkv_held.at[spot], sems_kv.at[at])
        copies += row_copies(wq_ref, first, wq_held.at[spot], sems_q.at[at])
    start_copies(copies)
    squares = rest_ref[:, :1]
    for x_ref in shards:
        wide = x_ref[...].astype(jnp.float32)
        squares += jnp.sum(wide * wide, axis=1, keepdims=True)
    factor = lax.rsqrt(squares / (width * (len(shards) + 1)) + EPS)
    factor_ref[...] = jnp.broadcast_to(factor, factor_ref.shape)
    for at, x_ref in enumerate(shards):
        store_normed(normed.at[:, pl.ds(at * width, width)], x_ref, factor_ref, gain_ref, place ^ at)
    wait_copies(copies)
    kv_ref[...] = jnp.dot(normed[...], wkv_held[...], preferred_element_type=jnp.float32)
    q_ref[...] = jnp.dot(normed[...], wq_held[...], preferred_element_type=jnp.float32)


def early_projection(own, near, far, rest, gain, wq, wkv):
    rows, width = own.shape
    heads, kv_width = wq.shape[1], wkv.shape[1]
    return resident(
        early_kernel,
        "early_projection",
        [((rows, heads), jnp.float32), ((rows, kv_width), jnp.float32), ((rows, 128), jnp.float32)],
        [own, near, far, rest, gain],
        weights=[wq, wkv],
        scratch=[
            pltpu.VMEM((3 * width, heads), jnp.bfloat16),
            pltpu.VMEM((3 * width, kv_width), jnp.bfloat16),
            pltpu.VMEM((rows, 3 * width), jnp.bfloat16),
            pltpu.SemaphoreType.DMA((3, WEIGHT_CUTS)),
            pltpu.SemaphoreType.DMA((3, 1)),
        ],
        limit=24,
    )


def last_kv_kernel(
    cross, relayed, factor_ref, gain_ref, acc_ref, w_ref, kv_ref, normed, w_held, x, sems
):
    place = lax.axis_index("tensor")
    copies = row_copies(w_ref, (place ^ 3) * x.shape[1], w_held, sems)
    start_copies(copies)
    is_inner = (place > 0) & (place < PARTS - 1)

    @pl.when(is_inner)
    def _():
        store_normed(normed, cross, factor_ref, gain_ref, place ^ 3)

    @pl.when(jnp.logical_not(is_inner))
    def _():
        store_normed(normed, relayed, factor_ref, gain_ref, place ^ 3)

    wait_copies(copies)
    part = jnp.dot(normed[...], w_held[...], preferred_element_type=jnp.float32)
    kv_ref[...] = (acc_ref[...] + part).astype(jnp.bfloat16)


def last_kv(cross, relayed, factor, gain, acc, w):
    rows, columns = acc.shape
    width = relayed.shape[1]
    return resident(
        last_kv_kernel,
        "last_kv",
        [((rows, columns), jnp.bfloat16), ((rows, width), jnp.bfloat16)],
        [cross, relayed, factor, gain, acc],
        weights=[w],
        scratch=[
            pltpu.VMEM((width, columns), jnp.bfloat16),
            pltpu.VMEM((rows, width), jnp.bfloat16),
            pltpu.SemaphoreType.DMA((2,)),
        ],
        limit=8,
    )


def last_q_kernel(normed, acc_ref, w_ref, q_ref, w_held, sems):
    place = lax.axis_index("tensor")
    copies = row_copies(w_ref, (place ^ 3) * normed.shape[1], w_held, sems)
    start_copies(copies)
    wait_copies(copies)
    part = jnp.dot(normed[...], w_held[...], preferred_element_type=jnp.float32)
    q_ref[...] = (acc_ref[...] + part).astype(jnp.bfloat16)


def last_q(normed, acc, w):
    rows, width = normed.shape
    columns = w.shape[1]
    return resident(
        last_q_kernel,
        "last_q",
        [((rows, columns), jnp.bfloat16)],
        [normed, acc],
        weights=[w],
        scratch=[pltpu.VMEM((width, columns), jnp.bfloat16), pltpu.SemaphoreType.DMA((WEIGHT_CUTS,))],
        limit=8,
    )[0]


def attend_kernel(
    row_lengths, cache_lengths, owners, *refs, count, places, sub_rows, heads, tile, divisor
):
    cache, pieces = refs[0], refs[1 : 1 + count]
    q_ref, w_ref, attended_rows, part_ref, held_ref = refs[1 + count : 6 + count]
    w_held, fresh, scores, top, total, acc, sems, w_sems = refs[6 + count :]
    rank = lax.axis_index("dp")
    place = lax.axis_index("tensor")
    row_count = q_ref.shape[0]
    width = part_ref.shape[1]
    docs = row_lengths.shape[1]
    copies = []
    for at, (piece, own) in enumerate(zip(pieces, places)):
        size = piece.shape[0]
        start = 0 if own is None else (rank if own else 1 - rank) * size
        target = fresh.at[pl.ds(pl.multiple_of(start, 16), size)]
        copies.append(pltpu.make_async_copy(piece, target, sems.at[at]))
    w_copies = column_copies(w_ref, (place ^ 3) * width, w_held, w_sems)
    start_copies(copies + w_copies)

    row_start, row_end = documents(row_lengths, docs)
    cache_start, cache_end = documents(cache_lengths, docs)
    stacked = heads * sub_rows
    lanes = 128

    def by_doc(row, values):
        found = values[0]
        for d in range(1, docs):
            found = jnp.where(row >= row_start[d], values[d], found)
        return found

    pairs = jnp.int32(0)
    for block in range(owners.shape[1]):
        found = jnp.int32(0)
        for d in range(docs):
            low = jnp.maximum(row_start[d], block * BLOCK_ROWS)
            high = jnp.maximum(jnp.minimum(row_end[d], (block + 1) * BLOCK_ROWS), low)
            amount = high - low
            found += amount * (cache_lengths[0, d] + 1 - row_start[d])
            found += lax.shift_right_arithmetic((low + high - 1) * amount, 1)
        pairs += jnp.where(owners[0, block] == rank, found, 0)
    held_ref[...] = jnp.full(held_ref.shape, pairs, jnp.int32).astype(jnp.float32) / divisor

    def span(start, end):
        start = lax.div(start, 16) * 16
        return start, lax.div(end - start + tile - 1, tile)

    def tile_start(source, first, t):
        start = first + t * tile
        return start, pl.multiple_of(jnp.minimum(start, source.shape[0] - tile), 16)

    for step in range(row_count // sub_rows):
        spots = slice(step * sub_rows, (step + 1) * sub_rows)
        first_row = rank * row_count + step * sub_rows
        last_row = first_row + sub_rows - 1
        rows = first_row + lax.broadcasted_iota(jnp.int32, (sub_rows, 1), 0)
        queries = jnp.concatenate(
            [q_ref[spots, h * HEAD_SIZE : (h + 1) * HEAD_SIZE] for h in range(heads)], axis=0
        )
        top[...] = jnp.full(top.shape, NEG, jnp.float32)
        total[...] = jnp.zeros(total.shape, jnp.float32)
        acc[...] = jnp.zeros(acc.shape, jnp.float32)

        def score(source, first, base, low, high):
            def body(t, _):
                begin, start = tile_start(source, first, t)
                found = lax.dot_general(
                    queries,
                    source[pl.ds(start, tile), :HEAD_SIZE],
                    (((1,), (1,)), ((), ())),
                    preferred_element_type=jnp.float32,
                )
                spot = start + lax.broadcasted_iota(jnp.int32, (1, tile), 1)
                seen = (spot >= jnp.maximum(low, begin)) & (spot < high)
                found = jnp.where(seen[None], found.reshape(heads, sub_rows, tile), NEG)
                found = found.reshape(stacked, tile)
                scores[base + t] = found
                best = found[:, :lanes]
                for c in range(1, tile // lanes):
                    best = jnp.maximum(best, found[:, c * lanes : (c + 1) * lanes])
                top[...] = jnp.maximum(top[...], best)
                return 0

            return body

        cache_from, cache_tiles = span(by_doc(first_row, cache_start), by_doc(last_row, cache_end))
        new_from, new_tiles = span(by_doc(first_row, row_start), last_row + 1)
        low, high = by_doc(rows, cache_start), by_doc(rows, cache_end)
        lax.fori_loop(0, cache_tiles, score(cache, cache_from, 0, low, high), 0)
        if step == 0:
            wait_copies(copies)
        low, high = by_doc(rows, row_start), rows + 1
        lax.fori_loop(0, new_tiles, score(fresh, new_from, cache_tiles, low, high), 0)
        highest = jnp.max(top[...], axis=1, keepdims=True)

        def weigh(source, first, base):
            def body(t, _):
                _, start = tile_start(source, first, t)
                weights = jnp.exp2((scores[base + t] - highest) * (HEAD_SIZE**-0.5 * LOG2E))
                part = weights[:, :lanes]
                for c in range(1, tile // lanes):
                    part = part + weights[:, c * lanes : (c + 1) * lanes]
                total[...] += part
                acc[...] += jnp.dot(
                    weights.astype(jnp.bfloat16),
                    source[pl.ds(start, tile), HEAD_SIZE:],
                    preferred_element_type=jnp.float32,
                )
                return 0

            return body

        lax.fori_loop(0, cache_tiles, weigh(cache, cache_from, 0), 0)
        lax.fori_loop(0, new_tiles, weigh(fresh, new_from, cache_tiles), 0)
        attended = (acc[...] / jnp.sum(total[...], axis=1, keepdims=True)).astype(jnp.bfloat16)
        for h in range(heads):
            attended_rows[spots, h * HEAD_SIZE : (h + 1) * HEAD_SIZE] = attended[
                h * sub_rows : (h + 1) * sub_rows
            ]
    wait_copies(w_copies)
    part_ref[...] = jnp.dot(
        attended_rows[...], w_held[...], preferred_element_type=jnp.float32
    ).astype(jnp.bfloat16)


def attention(scalars, queries, cache, pieces, places, fresh, w, divisor):
    rows, width = queries.shape
    heads = width // HEAD_SIZE
    tiles = sum(pl.cdiv(amount, KEY_TILE) for amount in (cache.shape[0], fresh))
    sub_rows = BLOCK_ROWS
    while sub_rows > 32 and heads * sub_rows * tiles * KEY_TILE * 4 > SCORE_BYTES:
        sub_rows //= 2
    stacked = heads * sub_rows
    out_width = w.shape[1] // PARTS
    return resident(
        functools.partial(
            attend_kernel,
            count=len(pieces),
            places=places,
            sub_rows=sub_rows,
            heads=heads,
            tile=KEY_TILE,
            divisor=divisor,
        ),
        "attention",
        [((rows, width), jnp.bfloat16), ((rows, out_width), jnp.bfloat16), ((1, 1), jnp.float32)],
        [cache, *pieces, queries],
        scalars,
        weights=[w],
        scratch=[
            pltpu.VMEM((width, out_width), jnp.bfloat16),
            pltpu.VMEM((fresh, 2 * HEAD_SIZE), jnp.bfloat16),
            pltpu.VMEM((tiles, stacked, KEY_TILE), jnp.float32),
            pltpu.VMEM((stacked, 128), jnp.float32),
            pltpu.VMEM((stacked, 128), jnp.float32),
            pltpu.VMEM((stacked, HEAD_SIZE), jnp.float32),
            pltpu.SemaphoreType.DMA((len(pieces),)),
            pltpu.SemaphoreType.DMA((WEIGHT_CUTS,)),
        ],
        limit=26,
        moved=2 * w.size,
    )


def out_kernel(a_ref, w_ref, *refs, masks):
    outs, (w_held, sems) = refs[: len(masks)], refs[len(masks) :]
    place = lax.axis_index("tensor")
    width = outs[0].shape[1]
    copies = [
        column_copies(w_ref, (place ^ mask) * width, w_held.at[at], sems.at[at])
        for at, mask in enumerate(masks)
    ]
    for some in copies:
        start_copies(some)
    for at, out_ref in enumerate(outs):
        wait_copies(copies[at])
        out_ref[...] = jnp.dot(
            a_ref[...], w_held[at], preferred_element_type=jnp.float32
        ).astype(jnp.bfloat16)


def out_projection(attended, w, masks):
    rows, depth = attended.shape
    width = w.shape[1] // PARTS
    return resident(
        functools.partial(out_kernel, masks=masks),
        "out_projection",
        [((rows, width), jnp.bfloat16)] * len(masks),
        [attended],
        weights=[w],
        scratch=[
            pltpu.VMEM((len(masks), depth, width), jnp.bfloat16),
            pltpu.SemaphoreType.DMA((len(masks), WEIGHT_CUTS)),
        ],
        limit=16,
    )


def on_device(
    tokens, norm_gain, w_query, key_value_weight, w_out, cache_kv, cache_lengths, row_lengths, block_owner
):
    ranks = lax.axis_size("dp")
    splits = lax.axis_size("tensor")
    sections = lax.axis_size("pipe")
    rank = lax.axis_index("dp")
    own = tokens[0]
    row_count = own.shape[0]
    cache_rows = cache_kv.shape[1]
    gain, wq, wkv, wo = norm_gain, w_query[0], key_value_weight[0], w_out[0]
    assert splits == PARTS and row_count % BLOCK_ROWS == 0
    inner_pairs = xor_pairs(splits, 3, range(1, splits - 1))
    pair = [(0, 1), (1, 0)] if ranks == 2 else None

    def onwards(block, pairs):
        route = [
            (p * splits + a, (p + 1) % sections * splits + b) for p in range(sections) for a, b in pairs
        ]
        return swap(block, ("pipe", "tensor"), route)

    far = swap(own, "tensor", xor_pairs(splits, 2))
    near = swap(own, "tensor", xor_pairs(splits, 1))
    square = jnp.sum(jnp.square(own.astype(jnp.float32)), axis=1)[None]
    rest = swap(square, "tensor", xor_pairs(splits, 3))
    cross = swap(own, "tensor", inner_pairs)
    far, near, rest = lax.optimization_barrier((far, near, rest))
    relayed = swap(far, "tensor", [(1, 0), (2, 3)])
    cache = after(cache_kv.reshape(cache_rows, 2 * HEAD_SIZE), far)
    if pair:
        other = swap(cache, "dp", pair)
        cache = jnp.where(
            rank == 0, jnp.concatenate([cache, other]), jnp.concatenate([other, cache])
        )
    else:
        cache = lax.all_gather(cache, "dp", axis=0, tiled=True)

    rest = jnp.broadcast_to(rest[0][:, None], (row_count, 128))
    divisor = BLOCK_ROWS * (cache_rows * ranks // 2 + row_count * ranks // 2)
    early_q, early_kv, factor = early_projection(own, near, far, rest, gain, wq, wkv)
    kv, normed = last_kv(cross, relayed, factor, gain, early_kv, wkv)
    if pair:
        pieces, places = [kv, swap(kv, "dp", pair)], (1, 0)
    else:
        pieces, places = [lax.all_gather(kv, "dp", axis=0, tiled=True)], (None,)
    queries = last_q(normed, early_q, wq)
    home = onwards(after(own, kv), xor_pairs(splits, 0))

    scalars = (row_lengths, cache_lengths, block_owner[:, :, 0])
    attended, third, blocks_held = attention(
        scalars, queries, cache, pieces, places, ranks * row_count, wo, float(divisor)
    )
    from_outer = swap(third, "tensor", [(0, 1), (3, 2)])
    from_cross = onwards(third, inner_pairs)
    attended, home = lax.optimization_barrier((attended, home))
    second, first, same = out_projection(attended, wo, (2, 1, 0))
    from_far = onwards(second, [(0, 2), (3, 1)])
    summed = (second.astype(jnp.float32) + from_outer.astype(jnp.float32)).astype(jnp.bfloat16)
    first, same, summed = lax.optimization_barrier((first, same, summed))
    from_near = onwards(first, xor_pairs(splits, 1))
    from_same = onwards(same, xor_pairs(splits, 0))
    from_sum = onwards(summed, [(1, 3), (2, 0)])
    total = from_same.astype(jnp.float32)
    for block in (from_near, from_far, from_cross, from_sum):
        total = total + block.astype(jnp.float32)
    handed = (home.astype(jnp.float32) + total).astype(jnp.bfloat16)[None]
    return handed, blocks_held


def solution(mesh):
    placed = (
        P("pipe", "dp", "tensor"),
        P("pipe", None),
        P("pipe", None, "tensor"),
        P("pipe", None, "tensor"),
        P("pipe", "tensor", None),
        P("pipe", "dp", "tensor", None),
        P("pipe", None),
        P("pipe", None),
        P("pipe", None, None),
    )
    return jax.shard_map(
        on_device,
        mesh=mesh,
        in_specs=placed,
        out_specs=(P("pipe", "dp", "tensor"), P("pipe", "dp")),
        check_vma=False,
    )
```

time: 276 us -> 121 us (0.44)
  local copies, waits for them, and re-layouts: 61.9 us -> 0.84 us
  waiting for transfers between devices: 121 us -> 68.5 us
  matrix products: 36.6 us -> 0 us
  Pallas kernels: 0 us -> 28.2 us
  other arithmetic: 28 us -> 3.12 us
  between operations: 16.1 us -> 0.83 us
  starting transfers between devices: 8.26 us -> 19.5 us
  loops' own time: 2.9 us -> 0 us
    all_to_all x2 -> x0, waiting for transfers between devices: 60.5 us -> none  [the longest x1 60.5 us: on_device(): lax.all_to_all(flat_parts, ('dp', 'tensor'), split_axis=0, concat_axis=0,...]
    ppermute x1 -> x14, waiting for transfers between devices: 8.7 us -> 68.5 us  [swap(): return lax.ppermute(block, axis, pairs)]
    all_gather x2 -> x0, waiting for transfers between devices: 51.1 us -> none  [the longest x1 51.1 us: on_device(): full_rows = lax.all_gather(own_rows, 'tensor', axis=1, tiled=True)]
    dot_general x8 -> x0, matrix products: 36.6 us -> none  [the longest x2 12.9 us: update(): jnp.einsum('qkgn,nkd->qkgd', weights.astype(jnp.bfloat16), value_part, pr...]
    gather x4 -> x0, local copies, waits for them, and re-layouts: 34 us -> none  [the longest x1 15.4 us: on_device(): jnp.take(row_doc, row_index)]
    pallas_call x0 -> x5, Pallas kernels: none -> 28.2 us  [resident(): pl.pallas_call(kernel, in_specs=spaces, out_specs=[pl.BlockSpec(memory_sp...]
    another operation x5 -> x0, local copies, waits for them, and re-layouts: 19.6 us -> none  [the longest x1 19.4 us: on_device(): split_weight = w_out[0].reshape(head_width, splits, width_split)]
    ppermute x1 -> x14, starting transfers between devices: 0.01 us -> 19.5 us  [swap(): return lax.ppermute(block, axis, pairs)]
  transfers between devices with their start and end apart: 5 -> 14, of which waited for: 3 -> 8; matrix products, arithmetic and copies ran while one was open for 24% -> 2% of each run, Pallas kernels for 0% -> 23%
where the time goes in v1:
time: 121 us
  waiting for transfers between devices  68.5 us (57%)
  Pallas kernels  28.2 us (23%)
  starting transfers between devices  19.5 us (16%)
  other arithmetic  3.12 us (3%)
    ppermute x14, waiting for transfers between devices, swap(): return lax.ppermute(block, axis, pairs)  68.5 us
    pallas_call x5, Pallas kernels, resident(): pl.pallas_call(kernel, in_specs=spaces, out_specs=[pl.BlockSpec(memory_sp...  28.2 us
    ppermute x14, starting transfers between devices, swap(): return lax.ppermute(block, axis, pairs)  19.5 us
  transfers between devices with their start and end apart: 14, of which 8 were waited for; matrix products, arithmetic and copies ran while one was open for 2% of the time, Pallas kernels for 23%

profile of v1, /device:TPU:0, one launch (start us, length us, event | category | flops | bytes accessed | tf_op | source)
XLA Modules:
  0.0 121.0 jit_solution(11190132287308641459)
XLA Ops:
  0.6 3.1 %collective-permute-start.1 = (bf16[256,1280]{1,0:T(8,128)(2,1)}, bf16[256,1280]{1,0:T(8,128)(2,1)S(1)}, u32[]{:S(2)}, u32[]{:S(2)}) collective-permute-start(bf16[256,1280]{1,0:T(8,128)(2,1)} %bitcast.2.own), channel_id=1, source_target_pairs={{0,1},{1,0},{2,3},{3,2},{4,5},{5,4},{6,7},{7,6},{8,9},{9,8},{10,11... | collective-permute-start | bytes 1966088 | tf_op jit(solution)/shard_map/ppermute | solution.py:23
  3.7 2.6 %collective-permute-start = (bf16[256,1280]{1,0:T(8,128)(2,1)}, bf16[256,1280]{1,0:T(8,128)(2,1)S(1)}, u32[]{:S(2)}, u32[]{:S(2)}) collective-permute-start(bf16[256,1280]{1,0:T(8,128)(2,1)} %bitcast.2.own), channel_id=1, source_target_pairs={{0,2},{1,3},{2,0},{3,1},{4,6},{5,7},{6,4},{7,5},{8,10},{9,11},{10,... | collective-permute-start | bytes 1966088 | tf_op jit(solution)/shard_map/ppermute | solution.py:23
  6.3 1.3 %multiply_reduce_fusion = f32[256]{0:T(256)S(1)} fusion(bf16[1,256,1280]{2,1,0:T(8,128)(2,1)} %param.9), kind=kLoop, calls=%fused_computation.2 | loop fusion | flops 982784 | bytes 656384 | tf_op jit(solution)/shard_map/reduce_sum | solution.py:444
  8.4 26.6 %collective-permute-done.2 = f32[1,256]{1,0:T(1,128)S(1)} collective-permute-done((f32[1,256]{1,0:T(1,128)S(1)}, f32[1,256]{1,0:T(1,128)S(1)}, u32[]{:S(2)}, u32[]{:S(2)}) %collective-permute-start.2) | collective-permute-done | bytes 1056 | tf_op jit(solution)/shard_map/ppermute | solution.py:23
  35.0 1.5 %collective-permute-done.far = bf16[256,1280]{1,0:T(8,128)(2,1)S(1)} collective-permute-done((bf16[256,1280]{1,0:T(8,128)(2,1)}, bf16[256,1280]{1,0:T(8,128)(2,1)S(1)}, u32[]{:S(2)}, u32[]{:S(2)}) %collective-permute-start) | collective-permute-done | bytes 655392 | tf_op jit(solution)/shard_map/ppermute | solution.py:23
  36.6 1.3 %collective-permute-start.5 = (bf16[256,1280]{1,0:T(8,128)(2,1)S(1)}, bf16[256,1280]{1,0:T(8,128)(2,1)S(1)}, u32[]{:S(2)}, u32[]{:S(2)}) collective-permute-start(bf16[256,1280]{1,0:T(8,128)(2,1)S(1)} %collective-permute-done.far), channel_id=1, source_target_pairs={{1,0},{2,3},{5,4},{6,7},{9,8},{10,11},{13,12},{14,15},{17,16},{18,... | collective-permute-start | bytes 1966088 | tf_op jit(solution)/shard_map/ppermute | solution.py:23
  37.8 1.6 %collective-permute-start.3 = (bf16[1024,256]{1,0:T(8,128)(2,1)}, bf16[1024,256]{1,0:T(8,128)(2,1)S(1)}, u32[]{:S(2)}, u32[]{:S(2)}) collective-permute-start(bf16[1024,256]{1,0:T(8,128)(2,1)} %bitcast.18), channel_id=1, source_target_pairs={{0,4},{4,0},{1,5},{5,1},{2,6},{6,2},{3,7},{7,3},{8,12},{12,8},{9,1... | collective-permute-start | bytes 1572872 | tf_op jit(solution)/shard_map/ppermute | solution.py:23
  40.3 8.2 %early_projection.1 = (f32[256,1024]{1,0:T(8,128)S(1)}, f32[256,256]{1,0:T(8,128)S(1)}, f32[256,128]{1,0:T(8,128)S(1)}) custom-call(bf16[256,1280]{1,0:T(8,128)(2,1)} %bitcast.2.own, bf16[256,1280]{1,0:T(8,128)(2,1)S(1)} %collective-permute-done.1.near, bf16[256,1280]{1,0:T(8,128)(2,1)S(1)} %collective-permute-done.far, ...), custom_call_target="tpu_custom_call" | custom-call | tf_op jit(solution)/shard_map/early_projection/pallas_call | solution.py:46
  48.5 3.7 %collective-permute-done.5.relayed = bf16[256,1280]{1,0:T(8,128)(2,1)S(1)} collective-permute-done((bf16[256,1280]{1,0:T(8,128)(2,1)S(1)}, bf16[256,1280]{1,0:T(8,128)(2,1)S(1)}, u32[]{:S(2)}, u32[]{:S(2)}) %collective-permute-start.5) | collective-permute-done | bytes 655392 | tf_op jit(solution)/shard_map/ppermute | solution.py:23
  52.2 1.5 %last_kv.1 = (bf16[256,256]{1,0:T(8,128)(2,1)S(1)}, bf16[256,1280]{1,0:T(8,128)(2,1)S(1)}) custom-call(bf16[256,1280]{1,0:T(8,128)(2,1)S(1)} %collective-permute-done.4.cross, bf16[256,1280]{1,0:T(8,128)(2,1)S(1)} %collective-permute-done.5.relayed, f32[256,128]{1,0:T(8,128)S(1)} %get-tuple-element.27.factor_ref, bf16[1,5120]{1,0:T(2,128)(2,1)S(1)} %copy-done, ...), custom_call_target="tpu_custom_call" | custom-call | tf_op jit(solution)/shard_map/last_kv/pallas_call | solution.py:46
  53.7 1.6 %collective-permute-start.6 = (bf16[256,256]{1,0:T(8,128)(2,1)S(1)}, bf16[256,256]{1,0:T(8,128)(2,1)S(1)}, u32[]{:S(2)}, u32[]{:S(2)}) collective-permute-start(bf16[256,256]{1,0:T(8,128)(2,1)S(1)} %get-tuple-element.29.refs_1_), channel_id=1, source_target_pairs={{0,4},{4,0},{1,5},{5,1},{2,6},{6,2},{3,7},{7,3},{8,12},{12,8},{9,1... | collective-permute-start | bytes 393224 | tf_op jit(solution)/shard_map/ppermute | solution.py:23
  55.7 2.6 %last_q.1.refs_3_ = bf16[256,1024]{1,0:T(8,128)(2,1)S(1)} custom-call(bf16[256,1280]{1,0:T(8,128)(2,1)S(1)} %get-tuple-element.30.normed, f32[256,1024]{1,0:T(8,128)S(1)} %get-tuple-element.31.acc_ref, bf16[5120,1024]{1,0:T(8,128)(2,1)} %bitcast.13), custom_call_target="tpu_custom_call" | custom-call | tf_op jit(solution)/shard_map/last_q/pallas_call | solution.py:46
  58.7 11.2 %attention.1 = (bf16[256,1024]{1,0:T(8,128)(2,1)S(1)}, bf16[256,1280]{1,0:T(8,128)(2,1)S(1)}, f32[1,1]{1,0:T(1,128)}) custom-call(s32[1,4]{1,0:T(1,128)S(1)} %copy-done.1, s32[1,4]{1,0:T(1,128)S(1)} %copy-done.2, s32[1,4]{1,0:T(1,128)S(1)} %bitcast.11, bf16[2048,256]{1,0:T(8,128)(2,1)S(1)} %maximum_select_fusion.refs_0_, ...), custom_call_target="tpu_custom_call" | custom-call | bytes 10485760 | tf_op jit(solution)/shard_map/attention/pallas_call | solution.py:46
  70.0 1.5 %collective-permute-start.8 = (bf16[256,1280]{1,0:T(8,128)(2,1)S(1)}, bf16[256,1280]{1,0:T(8,128)(2,1)S(1)}, u32[]{:S(2)}, u32[]{:S(2)}) collective-permute-start(bf16[256,1280]{1,0:T(8,128)(2,1)S(1)} %get-tuple-element.39), channel_id=1, source_target_pairs={{0,1},{3,2},{4,5},{7,6},{8,9},{11,10},{12,13},{15,14},{16,17},{19,... | collective-permute-start | bytes 1966088 | tf_op jit(solution)/shard_map/ppermute | solution.py:23
  71.5 0.9 collective-permute-start.12
  72.4 4.6 %out_projection.1 = (bf16[256,1280]{1,0:T(8,128)(2,1)S(1)}, bf16[256,1280]{1,0:T(8,128)(2,1)S(1)}, bf16[256,1280]{1,0:T(8,128)(2,1)S(1)}) custom-call(bf16[256,1024]{1,0:T(8,128)(2,1)S(1)} %get-tuple-element.35.a_ref, bf16[1024,5120]{1,0:T(8,128)(2,1)} %bitcast.15), custom_call_target="tpu_custom_call" | custom-call | tf_op jit(solution)/shard_map/out_projection/pallas_call | solution.py:46
  77.0 3.0 %collective-permute-start.11 = (bf16[256,1280]{1,0:T(8,128)(2,1)S(1)}, bf16[256,1280]{1,0:T(8,128)(2,1)S(1)}, u32[]{:S(2)}, u32[]{:S(2)}) collective-permute-start(bf16[256,1280]{1,0:T(8,128)(2,1)S(1)} %get-tuple-element.38), channel_id=1, source_target_pairs={{0,10},{3,9},{8,18},{11,17},{16,26},{19,25},{24,2},{27,1},{4,14},{... | collective-permute-start | bytes 1966088 | tf_op jit(solution)/shard_map/ppermute | solution.py:23
  80.0 6.6 %collective-permute-done.8 = bf16[256,1280]{1,0:T(8,128)(2,1)S(1)} collective-permute-done((bf16[256,1280]{1,0:T(8,128)(2,1)S(1)}, bf16[256,1280]{1,0:T(8,128)(2,1)S(1)}, u32[]{:S(2)}, u32[]{:S(2)}) %collective-permute-start.8) | collective-permute-done | bytes 655392 | tf_op jit(solution)/shard_map/ppermute | solution.py:23
  86.8 1.8 %collective-permute-start.10 = (bf16[256,1280]{1,0:T(8,128)(2,1)S(1)}, bf16[256,1280]{1,0:T(8,128)(2,1)S(1)}, u32[]{:S(2)}, u32[]{:S(2)}) collective-permute-start(bf16[256,1280]{1,0:T(8,128)(2,1)S(1)} %get-tuple-element.41), channel_id=1, source_target_pairs={{0,9},{1,8},{2,11},{3,10},{8,17},{9,16},{10,19},{11,18},{16,25},{1... | collective-permute-start | bytes 1966088 | tf_op jit(solution)/shard_map/ppermute | solution.py:23
  88.6 1.3 %collective-permute-start.13 = (bf16[256,1280]{1,0:T(8,128)(2,1)S(1)}, bf16[256,1280]{1,0:T(8,128)(2,1)S(1)}, u32[]{:S(2)}, u32[]{:S(2)}) collective-permute-start(bf16[256,1280]{1,0:T(8,128)(2,1)S(1)} %add_convert_fusion.1), channel_id=1, source_target_pairs={{1,11},{2,8},{9,19},{10,16},{17,27},{18,24},{25,3},{26,0},{5,15},{... | collective-permute-start | bytes 1966088 | tf_op jit(solution)/shard_map/ppermute | solution.py:23
  89.9 10.8 %collective-permute-done.11 = bf16[256,1280]{1,0:T(8,128)(2,1)S(1)} collective-permute-done((bf16[256,1280]{1,0:T(8,128)(2,1)S(1)}, bf16[256,1280]{1,0:T(8,128)(2,1)S(1)}, u32[]{:S(2)}, u32[]{:S(2)}) %collective-permute-start.11) | collective-permute-done | bytes 655392 | tf_op jit(solution)/shard_map/ppermute | solution.py:23
  100.7 1.2 %collective-permute-done.9 = bf16[256,1280]{1,0:T(8,128)(2,1)S(1)} collective-permute-done((bf16[256,1280]{1,0:T(8,128)(2,1)S(1)}, bf16[256,1280]{1,0:T(8,128)(2,1)S(1)}, u32[]{:S(2)}, u32[]{:S(2)}) %collective-permute-start.9) | collective-permute-done | bytes 655392 | tf_op jit(solution)/shard_map/ppermute | solution.py:23
  101.9 17.7 %collective-permute-done.10 = bf16[256,1280]{1,0:T(8,128)(2,1)S(1)} collective-permute-done((bf16[256,1280]{1,0:T(8,128)(2,1)S(1)}, bf16[256,1280]{1,0:T(8,128)(2,1)S(1)}, u32[]{:S(2)}, u32[]{:S(2)}) %collective-permute-start.10) | collective-permute-done | bytes 655392 | tf_op jit(solution)/shard_map/ppermute | solution.py:23
  119.6 1.4 %fusion = bf16[1,256,1280]{2,1,0:T(8,128)(2,1)} fusion(bf16[256,1280]{1,0:T(8,128)(2,1)S(1)} %collective-permute-done.13, bf16[256,1280]{1,0:T(8,128)(2,1)S(1)} %collective-permute-done.12, bf16[256,1280]{1,0:T(8,128)(2,1)S(1)} %collective-permute-done.11, bf16[256,1280]{1,0:T(8,128)(2,1)S(1)} %collective-permute-done.10, ...), kind=kLoop, calls=%fused_computation.4 | loop fusion | flops 3932160 | bytes 4587520 | tf_op jit(solution)/shard_map/broadcast_in_dim | solution.py:486
  (24 shorter events, 2.6 us)
Async XLA Ops:
  0.6 34.4 %collective-permute-start.1 = (bf16[256,1280]{1,0:T(8,128)(2,1)}, bf16[256,1280]{1,0:T(8,128)(2,1)S(1)}, u32[]{:S(2)}, u32[]{:S(2)}) collective-permute-start(bf16[256,1280]{1,0:T(8,128)(2,1)} %bitcast.2.own), channel_id=1, source_target_pairs={{0,1},{1,0},{2,3},{3,2},{4,5},{5,4},{6,7},{7,6},{8,9},{9,8},{10,11... | collective-permute-start | bytes 1966088 | tf_op jit(solution)/shard_map/ppermute | solution.py:23
  3.7 32.8 %collective-permute-start = (bf16[256,1280]{1,0:T(8,128)(2,1)}, bf16[256,1280]{1,0:T(8,128)(2,1)S(1)}, u32[]{:S(2)}, u32[]{:S(2)}) collective-permute-start(bf16[256,1280]{1,0:T(8,128)(2,1)} %bitcast.2.own), channel_id=1, source_target_pairs={{0,2},{1,3},{2,0},{3,1},{4,6},{5,7},{6,4},{7,5},{8,10},{9,11},{10,... | collective-permute-start | bytes 1966088 | tf_op jit(solution)/shard_map/ppermute | solution.py:23
  7.6 27.4 %collective-permute-start.2 = (f32[1,256]{1,0:T(1,128)S(1)}, f32[1,256]{1,0:T(1,128)S(1)}, u32[]{:S(2)}, u32[]{:S(2)}) collective-permute-start(f32[1,256]{1,0:T(1,128)S(1)} %bitcast.21), channel_id=1, source_target_pairs={{0,3},{1,2},{2,1},{3,0},{4,7},{5,6},{6,5},{7,4},{8,11},{9,10},{10,... | collective-permute-start | bytes 3080 | tf_op jit(solution)/shard_map/ppermute | solution.py:23
  7.7 40.8 %collective-permute-start.4 = (bf16[256,1280]{1,0:T(8,128)(2,1)}, bf16[256,1280]{1,0:T(8,128)(2,1)S(1)}, u32[]{:S(2)}, u32[]{:S(2)}) collective-permute-start(bf16[256,1280]{1,0:T(8,128)(2,1)} %bitcast.2.own), channel_id=1, source_target_pairs={{1,2},{2,1},{5,6},{6,5},{9,10},{10,9},{13,14},{14,13},{17,18},{18,... | collective-permute-start | bytes 1966088 | tf_op jit(solution)/shard_map/ppermute | solution.py:23
  36.6 15.7 %collective-permute-start.5 = (bf16[256,1280]{1,0:T(8,128)(2,1)S(1)}, bf16[256,1280]{1,0:T(8,128)(2,1)S(1)}, u32[]{:S(2)}, u32[]{:S(2)}) collective-permute-start(bf16[256,1280]{1,0:T(8,128)(2,1)S(1)} %collective-permute-done.far), channel_id=1, source_target_pairs={{1,0},{2,3},{5,4},{6,7},{9,8},{10,11},{13,12},{14,15},{17,16},{18,... | collective-permute-start | bytes 1966088 | tf_op jit(solution)/shard_map/ppermute | solution.py:23
  37.8 17.5 %collective-permute-start.3 = (bf16[1024,256]{1,0:T(8,128)(2,1)}, bf16[1024,256]{1,0:T(8,128)(2,1)S(1)}, u32[]{:S(2)}, u32[]{:S(2)}) collective-permute-start(bf16[1024,256]{1,0:T(8,128)(2,1)} %bitcast.18), channel_id=1, source_target_pairs={{0,4},{4,0},{1,5},{5,1},{2,6},{6,2},{3,7},{7,3},{8,12},{12,8},{9,1... | collective-permute-start | bytes 1572872 | tf_op jit(solution)/shard_map/ppermute | solution.py:23
  39.5 0.7 copy-start
  52.2 3.1 %copy-start.4 = (bf16[1,1024,1,256]{3,1,2,0:T(8,128)(2,1)S(1)}, bf16[1,1024,1,256]{3,1,2,0:T(8,128)(2,1)}, u32[]{:S(2)}) copy-start(bf16[1,1024,1,256]{3,1,2,0:T(8,128)(2,1)} %param.14) | copy-start | bytes 1572868
  53.7 5.0 %collective-permute-start.6 = (bf16[256,256]{1,0:T(8,128)(2,1)S(1)}, bf16[256,256]{1,0:T(8,128)(2,1)S(1)}, u32[]{:S(2)}, u32[]{:S(2)}) collective-permute-start(bf16[256,256]{1,0:T(8,128)(2,1)S(1)} %get-tuple-element.29.refs_1_), channel_id=1, source_target_pairs={{0,4},{4,0},{1,5},{5,1},{2,6},{6,2},{3,7},{7,3},{8,12},{12,8},{9,1... | collective-permute-start | bytes 393224 | tf_op jit(solution)/shard_map/ppermute | solution.py:23
  55.6 16.8 %collective-permute-start.7 = (bf16[256,1280]{1,0:T(8,128)(2,1)}, bf16[256,1280]{1,0:T(8,128)(2,1)S(1)}, u32[]{:S(2)}, u32[]{:S(2)}) collective-permute-start(bf16[256,1280]{1,0:T(8,128)(2,1)} %bitcast.2.own), channel_id=1, source_target_pairs={{0,8},{1,9},{2,10},{3,11},{8,16},{9,17},{10,18},{11,19},{16,24},{1... | collective-permute-start | bytes 1966088 | tf_op jit(solution)/shard_map/ppermute | solution.py:23
  55.7 3.1 %copy-start.1 = (s32[1,4]{1,0:T(1,128)S(1)}, s32[1,4]{1,0:T(1,128)}, u32[]{:S(2)}) copy-start(s32[1,4]{1,0:T(1,128)} %row_lengths.1) | copy-start | bytes 52
  55.7 3.1 %copy-start.2 = (s32[1,4]{1,0:T(1,128)S(1)}, s32[1,4]{1,0:T(1,128)}, u32[]{:S(2)}) copy-start(s32[1,4]{1,0:T(1,128)} %cache_lengths.1) | copy-start | bytes 52
  55.7 3.1 %copy-start.3 = (s32[1,4,1]{1,2,0:T(1,128)S(1)}, s32[1,4,1]{1,2,0:T(1,128)}, u32[]{:S(2)}) copy-start(s32[1,4,1]{1,2,0:T(1,128)} %param.17) | copy-start | bytes 52
  70.0 16.6 %collective-permute-start.8 = (bf16[256,1280]{1,0:T(8,128)(2,1)S(1)}, bf16[256,1280]{1,0:T(8,128)(2,1)S(1)}, u32[]{:S(2)}, u32[]{:S(2)}) collective-permute-start(bf16[256,1280]{1,0:T(8,128)(2,1)S(1)} %get-tuple-element.39), channel_id=1, source_target_pairs={{0,1},{3,2},{4,5},{7,6},{8,9},{11,10},{12,13},{15,14},{16,17},{19,... | collective-permute-start | bytes 1966088 | tf_op jit(solution)/shard_map/ppermute | solution.py:23
  71.5 18.4 %collective-permute-start.12 = (bf16[256,1280]{1,0:T(8,128)(2,1)S(1)}, bf16[256,1280]{1,0:T(8,128)(2,1)S(1)}, u32[]{:S(2)}, u32[]{:S(2)}) collective-permute-start(bf16[256,1280]{1,0:T(8,128)(2,1)S(1)} %get-tuple-element.39), channel_id=1, source_target_pairs={{1,10},{2,9},{9,18},{10,17},{17,26},{18,25},{25,2},{26,1},{5,14},{... | collective-permute-start | bytes 1966088 | tf_op jit(solution)/shard_map/ppermute | solution.py:23
  77.0 23.7 %collective-permute-start.11 = (bf16[256,1280]{1,0:T(8,128)(2,1)S(1)}, bf16[256,1280]{1,0:T(8,128)(2,1)S(1)}, u32[]{:S(2)}, u32[]{:S(2)}) collective-permute-start(bf16[256,1280]{1,0:T(8,128)(2,1)S(1)} %get-tuple-element.38), channel_id=1, source_target_pairs={{0,10},{3,9},{8,18},{11,17},{16,26},{19,25},{24,2},{27,1},{4,14},{... | collective-permute-start | bytes 1966088 | tf_op jit(solution)/shard_map/ppermute | solution.py:23
  86.7 15.2 %collective-permute-start.9 = (bf16[256,1280]{1,0:T(8,128)(2,1)S(1)}, bf16[256,1280]{1,0:T(8,128)(2,1)S(1)}, u32[]{:S(2)}, u32[]{:S(2)}) collective-permute-start(bf16[256,1280]{1,0:T(8,128)(2,1)S(1)} %get-tuple-element.40), channel_id=1, source_target_pairs={{0,8},{1,9},{2,10},{3,11},{8,16},{9,17},{10,18},{11,19},{16,24},{1... | collective-permute-start | bytes 1966088 | tf_op jit(solution)/shard_map/ppermute | solution.py:23
  86.8 32.8 %collective-permute-start.10 = (bf16[256,1280]{1,0:T(8,128)(2,1)S(1)}, bf16[256,1280]{1,0:T(8,128)(2,1)S(1)}, u32[]{:S(2)}, u32[]{:S(2)}) collective-permute-start(bf16[256,1280]{1,0:T(8,128)(2,1)S(1)} %get-tuple-element.41), channel_id=1, source_target_pairs={{0,9},{1,8},{2,11},{3,10},{8,17},{9,16},{10,19},{11,18},{16,25},{1... | collective-permute-start | bytes 1966088 | tf_op jit(solution)/shard_map/ppermute | solution.py:23
  88.6 31.0 %collective-permute-start.13 = (bf16[256,1280]{1,0:T(8,128)(2,1)S(1)}, bf16[256,1280]{1,0:T(8,128)(2,1)S(1)}, u32[]{:S(2)}, u32[]{:S(2)}) collective-permute-start(bf16[256,1280]{1,0:T(8,128)(2,1)S(1)} %add_convert_fusion.1), channel_id=1, source_target_pairs={{1,11},{2,8},{9,19},{10,16},{17,27},{18,24},{25,3},{26,0},{5,15},{... | collective-permute-start | bytes 1966088 | tf_op jit(solution)/shard_map/ppermute | solution.py:23

commit v2 on v1

--- a/solution.py
+++ b/solution.py
@@ -112,16 +112,21 @@
     return starts, ends
 
 
+def by_position(place, for_inner, for_outer):
+    return jnp.where((place > 0) & (place < PARTS - 1), for_inner, for_outer)
+
+
 def early_kernel(
-    own, near, far, rest_ref, gain_ref, wq_ref, wkv_ref,
+    own, one, two, rest_ref, gain_ref, wq_ref, wkv_ref,
     q_ref, kv_ref, factor_ref, wq_held, wkv_held, normed, sems_q, sems_kv,
 ):
     place = lax.axis_index("tensor")
     width = own.shape[1]
-    shards = (own, near, far)
+    shards = (own, one, two)
+    spots = (place, place ^ by_position(place, 2, 1), place ^ by_position(place, 1, 2))
     copies = []
     for at in range(len(shards)):
-        first, spot = (place ^ at) * width, pl.ds(at * width, width)
+        first, spot = spots[at] * width, pl.ds(at * width, width)
         copies += row_copies(wkv_ref, first, wkv_held.at[spot], sems_kv.at[at])
         copies += row_copies(wq_ref, first, wq_held.at[spot], sems_q.at[at])
     start_copies(copies)
@@ -132,20 +137,20 @@
     factor = lax.rsqrt(squares / (width * (len(shards) + 1)) + EPS)
     factor_ref[...] = jnp.broadcast_to(factor, factor_ref.shape)
     for at, x_ref in enumerate(shards):
-        store_normed(normed.at[:, pl.ds(at * width, width)], x_ref, factor_ref, gain_ref, place ^ at)
+        store_normed(normed.at[:, pl.ds(at * width, width)], x_ref, factor_ref, gain_ref, spots[at])
     wait_copies(copies)
     kv_ref[...] = jnp.dot(normed[...], wkv_held[...], preferred_element_type=jnp.float32)
     q_ref[...] = jnp.dot(normed[...], wq_held[...], preferred_element_type=jnp.float32)
 
 
-def early_projection(own, near, far, rest, gain, wq, wkv):
+def early_projection(own, one, two, rest, gain, wq, wkv):
     rows, width = own.shape
     heads, kv_width = wq.shape[1], wkv.shape[1]
     return resident(
         early_kernel,
         "early_projection",
         [((rows, heads), jnp.float32), ((rows, kv_width), jnp.float32), ((rows, 128), jnp.float32)],
-        [own, near, far, rest, gain],
+        [own, one, two, rest, gain],
         weights=[wq, wkv],
         scratch=[
             pltpu.VMEM((3 * width, heads), jnp.bfloat16),
@@ -384,13 +389,13 @@
     )
 
 
-def out_kernel(a_ref, w_ref, *refs, masks):
-    outs, (w_held, sems) = refs[: len(masks)], refs[len(masks) :]
+def out_kernel(a_ref, w_ref, one, two, same, w_held, sems):
+    outs = (one, two, same)
     place = lax.axis_index("tensor")
-    width = outs[0].shape[1]
+    spots = (place ^ by_position(place, 1, 2), place ^ by_position(place, 2, 1), place)
+    width = same.shape[1]
     copies = [
-        column_copies(w_ref, (place ^ mask) * width, w_held.at[at], sems.at[at])
-        for at, mask in enumerate(masks)
+        column_copies(w_ref, spot * width, w_held.at[at], sems.at[at]) for at, spot in enumerate(spots)
     ]
     for some in copies:
         start_copies(some)
@@ -401,18 +406,18 @@
         ).astype(jnp.bfloat16)
 
 
-def out_projection(attended, w, masks):
+def out_projection(attended, w):
     rows, depth = attended.shape
     width = w.shape[1] // PARTS
     return resident(
-        functools.partial(out_kernel, masks=masks),
+        out_kernel,
         "out_projection",
-        [((rows, width), jnp.bfloat16)] * len(masks),
+        [((rows, width), jnp.bfloat16)] * 3,
         [attended],
         weights=[w],
         scratch=[
-            pltpu.VMEM((len(masks), depth, width), jnp.bfloat16),
-            pltpu.SemaphoreType.DMA((len(masks), WEIGHT_CUTS)),
+            pltpu.VMEM((3, depth, width), jnp.bfloat16),
+            pltpu.SemaphoreType.DMA((3, WEIGHT_CUTS)),
         ],
         limit=16,
     )
@@ -439,14 +444,14 @@
         ]
         return swap(block, ("pipe", "tensor"), route)
 
-    far = swap(own, "tensor", xor_pairs(splits, 2))
-    near = swap(own, "tensor", xor_pairs(splits, 1))
+    one = swap(own, "tensor", [(0, 2), (3, 1), (1, 0), (2, 3)])
     square = jnp.sum(jnp.square(own.astype(jnp.float32)), axis=1)[None]
     rest = swap(square, "tensor", xor_pairs(splits, 3))
-    cross = swap(own, "tensor", inner_pairs)
-    far, near, rest = lax.optimization_barrier((far, near, rest))
-    relayed = swap(far, "tensor", [(1, 0), (2, 3)])
-    cache = after(cache_kv.reshape(cache_rows, 2 * HEAD_SIZE), far)
+    one, rest, late = lax.optimization_barrier((one, rest, own))
+    two = swap(late, "tensor", [(0, 1), (3, 2), (1, 3), (2, 0)])
+    relayed = swap(one, "tensor", [(1, 0), (2, 3)])
+    cross = swap(late, "tensor", inner_pairs)
+    cache = after(cache_kv.reshape(cache_rows, 2 * HEAD_SIZE), rest)
     if pair:
         other = swap(cache, "dp", pair)
         cache = jnp.where(
@@ -457,7 +462,7 @@
 
     rest = jnp.broadcast_to(rest[0][:, None], (row_count, 128))
     divisor = BLOCK_ROWS * (cache_rows * ranks // 2 + row_count * ranks // 2)
-    early_q, early_kv, factor = early_projection(own, near, far, rest, gain, wq, wkv)
+    early_q, early_kv, factor = early_projection(own, one, two, rest, gain, wq, wkv)
     kv, normed = last_kv(cross, relayed, factor, gain, early_kv, wkv)
     if pair:
         pieces, places = [kv, swap(kv, "dp", pair)], (1, 0)
@@ -473,15 +478,13 @@
     from_outer = swap(third, "tensor", [(0, 1), (3, 2)])
     from_cross = onwards(third, inner_pairs)
     attended, home = lax.optimization_barrier((attended, home))
-    second, first, same = out_projection(attended, wo, (2, 1, 0))
-    from_far = onwards(second, [(0, 2), (3, 1)])
+    first, second, same = out_projection(attended, wo)
+    from_one = onwards(first, [(0, 2), (3, 1), (1, 0), (2, 3)])
+    from_same = onwards(same, xor_pairs(splits, 0))
     summed = (second.astype(jnp.float32) + from_outer.astype(jnp.float32)).astype(jnp.bfloat16)
-    first, same, summed = lax.optimization_barrier((first, same, summed))
-    from_near = onwards(first, xor_pairs(splits, 1))
-    from_same = onwards(same, xor_pairs(splits, 0))
-    from_sum = onwards(summed, [(1, 3), (2, 0)])
+    from_two = onwards(summed, [(0, 1), (3, 2), (1, 3), (2, 0)])
     total = from_same.astype(jnp.float32)
-    for block in (from_near, from_far, from_cross, from_sum):
+    for block in (from_one, from_two, from_cross):
         total = total + block.astype(jnp.float32)
     handed = (home.astype(jnp.float32) + total).astype(jnp.bfloat16)[None]
     return handed, blocks_held

time: 121 us -> 119 us (0.983); the launches traced: 121 us -> 118 us
  starting transfers between devices: 19.5 us -> 24.1 us
  waiting for transfers between devices: 68.5 us -> 64 us
  Pallas kernels: 28.2 us -> 24.9 us
    ppermute x14 -> x13, starting transfers between devices: 19.5 us -> 24.1 us  [swap(): return lax.ppermute(block, axis, pairs)]
    ppermute x14 -> x13, waiting for transfers between devices: 68.5 us -> 64 us  [swap(): return lax.ppermute(block, axis, pairs)]
    pallas_call x5, Pallas kernels: 28.2 us -> 24.9 us  [resident(): pl.pallas_call(kernel, in_specs=spaces, out_specs=[pl.BlockSpec(memory_sp...]
  transfers between devices with their start and end apart: 14 -> 13, of which waited for: 8 -> 8; matrix products, arithmetic and copies ran while one was open for 2% -> 2% of each run, Pallas kernels for 23% -> 21%
where the time goes in v2:
time: 119 us; the launch traced here: 118 us
  waiting for transfers between devices  64 us (54%)
  Pallas kernels  24.9 us (21%)
  starting transfers between devices  24.1 us (20%)
  other arithmetic  3.04 us (3%)
    ppermute x13, waiting for transfers between devices, swap(): return lax.ppermute(block, axis, pairs)  64 us
    pallas_call x5, Pallas kernels, resident(): pl.pallas_call(kernel, in_specs=spaces, out_specs=[pl.BlockSpec(memory_sp...  24.9 us
    ppermute x13, starting transfers between devices, swap(): return lax.ppermute(block, axis, pairs)  24.1 us
  transfers between devices with their start and end apart: 13, of which 8 were waited for; matrix products, arithmetic and copies ran while one was open for 2% of the time, Pallas kernels for 21%

profile of v2, /device:TPU:0, one launch (start us, length us, event | category | flops | bytes accessed | tf_op | source)
XLA Modules:
  0.0 117.7 jit_solution(14007397715301648758)
XLA Ops:
  0.6 4.1 %collective-permute-start = (bf16[256,1280]{1,0:T(8,128)(2,1)}, bf16[256,1280]{1,0:T(8,128)(2,1)S(1)}, u32[]{:S(2)}, u32[]{:S(2)}) collective-permute-start(bf16[256,1280]{1,0:T(8,128)(2,1)} %bitcast.2.own), channel_id=1, source_target_pairs={{0,2},{3,1},{1,0},{2,3},{4,6},{7,5},{5,4},{6,7},{8,10},{11,9},{9,8... | collective-permute-start | bytes 1966088 | tf_op jit(solution)/shard_map/ppermute | solution.py:23
  4.7 1.3 %multiply_reduce_fusion = f32[256]{0:T(256)S(1)} fusion(bf16[1,256,1280]{2,1,0:T(8,128)(2,1)} %param.9), kind=kLoop, calls=%fused_computation.2 | loop fusion | flops 982784 | bytes 656384 | tf_op jit(solution)/shard_map/reduce_sum | solution.py:448
  6.0 1.4 %collective-permute-start.1 = (f32[1,256]{1,0:T(1,128)S(1)}, f32[1,256]{1,0:T(1,128)S(1)}, u32[]{:S(2)}, u32[]{:S(2)}) collective-permute-start(f32[1,256]{1,0:T(1,128)S(1)} %bitcast.21), channel_id=1, source_target_pairs={{0,3},{1,2},{2,1},{3,0},{4,7},{5,6},{6,5},{7,4},{8,11},{9,10},{10,... | collective-permute-start | bytes 3080 | tf_op jit(solution)/shard_map/ppermute | solution.py:23
  7.5 13.3 %collective-permute-done.1 = f32[1,256]{1,0:T(1,128)S(1)} collective-permute-done((f32[1,256]{1,0:T(1,128)S(1)}, f32[1,256]{1,0:T(1,128)S(1)}, u32[]{:S(2)}, u32[]{:S(2)}) %collective-permute-start.1) | collective-permute-done | bytes 1056 | tf_op jit(solution)/shard_map/ppermute | solution.py:23
  22.0 1.3 %collective-permute-start.4 = (bf16[256,1280]{1,0:T(8,128)(2,1)S(1)}, bf16[256,1280]{1,0:T(8,128)(2,1)S(1)}, u32[]{:S(2)}, u32[]{:S(2)}) collective-permute-start(bf16[256,1280]{1,0:T(8,128)(2,1)S(1)} %collective-permute-done.one), channel_id=1, source_target_pairs={{1,0},{2,3},{5,4},{6,7},{9,8},{10,11},{13,12},{14,15},{17,16},{18,... | collective-permute-start | bytes 1966088 | tf_op jit(solution)/shard_map/ppermute | solution.py:23
  23.3 1.6 %collective-permute-start.2 = (bf16[1024,256]{1,0:T(8,128)(2,1)}, bf16[1024,256]{1,0:T(8,128)(2,1)S(1)}, u32[]{:S(2)}, u32[]{:S(2)}) collective-permute-start(bf16[1024,256]{1,0:T(8,128)(2,1)} %bitcast.18), channel_id=1, source_target_pairs={{0,4},{4,0},{1,5},{5,1},{2,6},{6,2},{3,7},{7,3},{8,12},{12,8},{9,1... | collective-permute-start | bytes 1572872 | tf_op jit(solution)/shard_map/ppermute | solution.py:23
  24.9 14.7 %collective-permute-done.5.two = bf16[256,1280]{1,0:T(8,128)(2,1)S(1)} collective-permute-done((bf16[256,1280]{1,0:T(8,128)(2,1)}, bf16[256,1280]{1,0:T(8,128)(2,1)S(1)}, u32[]{:S(2)}, u32[]{:S(2)}) %collective-permute-start.5) | collective-permute-done | bytes 655392 | tf_op jit(solution)/shard_map/ppermute | solution.py:23
  40.4 8.2 %early_projection.1 = (f32[256,1024]{1,0:T(8,128)S(1)}, f32[256,256]{1,0:T(8,128)S(1)}, f32[256,128]{1,0:T(8,128)S(1)}) custom-call(bf16[256,1280]{1,0:T(8,128)(2,1)} %bitcast.2.own, bf16[256,1280]{1,0:T(8,128)(2,1)S(1)} %collective-permute-done.one, bf16[256,1280]{1,0:T(8,128)(2,1)S(1)} %collective-permute-done.5.two, ...), custom_call_target="tpu_custom_call" | custom-call | tf_op jit(solution)/shard_map/early_projection/pallas_call | solution.py:46
  48.7 2.6 %collective-permute-done.4.relayed = bf16[256,1280]{1,0:T(8,128)(2,1)S(1)} collective-permute-done((bf16[256,1280]{1,0:T(8,128)(2,1)S(1)}, bf16[256,1280]{1,0:T(8,128)(2,1)S(1)}, u32[]{:S(2)}, u32[]{:S(2)}) %collective-permute-start.4) | collective-permute-done | bytes 655392 | tf_op jit(solution)/shard_map/ppermute | solution.py:23
  51.2 1.5 %last_kv.1 = (bf16[256,256]{1,0:T(8,128)(2,1)S(1)}, bf16[256,1280]{1,0:T(8,128)(2,1)S(1)}) custom-call(bf16[256,1280]{1,0:T(8,128)(2,1)S(1)} %collective-permute-done.3.cross, bf16[256,1280]{1,0:T(8,128)(2,1)S(1)} %collective-permute-done.4.relayed, f32[256,128]{1,0:T(8,128)S(1)} %get-tuple-element.24.factor_ref, bf16[1,5120]{1,0:T(2,128)(2,1)S(1)} %copy-done, ...), custom_call_target="tpu_custom_call" | custom-call | tf_op jit(solution)/shard_map/last_kv/pallas_call | solution.py:46
  52.7 1.6 %collective-permute-start.6 = (bf16[256,256]{1,0:T(8,128)(2,1)S(1)}, bf16[256,256]{1,0:T(8,128)(2,1)S(1)}, u32[]{:S(2)}, u32[]{:S(2)}) collective-permute-start(bf16[256,256]{1,0:T(8,128)(2,1)S(1)} %get-tuple-element.26.refs_1_), channel_id=1, source_target_pairs={{0,4},{4,0},{1,5},{5,1},{2,6},{6,2},{3,7},{7,3},{8,12},{12,8},{9,1... | collective-permute-start | bytes 393224 | tf_op jit(solution)/shard_map/ppermute | solution.py:23
  54.7 2.6 %last_q.1.refs_3_ = bf16[256,1024]{1,0:T(8,128)(2,1)S(1)} custom-call(bf16[256,1280]{1,0:T(8,128)(2,1)S(1)} %get-tuple-element.27.normed, f32[256,1024]{1,0:T(8,128)S(1)} %get-tuple-element.28.acc_ref, bf16[5120,1024]{1,0:T(8,128)(2,1)} %bitcast.13), custom_call_target="tpu_custom_call" | custom-call | tf_op jit(solution)/shard_map/last_q/pallas_call | solution.py:46
  58.2 7.9 %attention.1 = (bf16[256,1024]{1,0:T(8,128)(2,1)S(1)}, bf16[256,1280]{1,0:T(8,128)(2,1)S(1)}, f32[1,1]{1,0:T(1,128)}) custom-call(s32[1,4]{1,0:T(1,128)S(1)} %copy-done.1, s32[1,4]{1,0:T(1,128)S(1)} %copy-done.2, s32[1,4]{1,0:T(1,128)S(1)} %bitcast.11, bf16[2048,256]{1,0:T(8,128)(2,1)S(1)} %maximum_select_fusion.refs_0_, ...), custom_call_target="tpu_custom_call" | custom-call | bytes 10485760 | tf_op jit(solution)/shard_map/attention/pallas_call | solution.py:46
  66.1 2.1 %collective-permute-start.10 = (bf16[256,1280]{1,0:T(8,128)(2,1)S(1)}, bf16[256,1280]{1,0:T(8,128)(2,1)S(1)}, u32[]{:S(2)}, u32[]{:S(2)}) collective-permute-start(bf16[256,1280]{1,0:T(8,128)(2,1)S(1)} %get-tuple-element.36), channel_id=1, source_target_pairs={{0,1},{3,2},{4,5},{7,6},{8,9},{11,10},{12,13},{15,14},{16,17},{19,... | collective-permute-start | bytes 1966088 | tf_op jit(solution)/shard_map/ppermute | solution.py:23
  68.2 0.9 collective-permute-start.12
  69.1 4.7 %out_projection.1 = (bf16[256,1280]{1,0:T(8,128)(2,1)S(1)}, bf16[256,1280]{1,0:T(8,128)(2,1)S(1)}, bf16[256,1280]{1,0:T(8,128)(2,1)S(1)}) custom-call(bf16[256,1024]{1,0:T(8,128)(2,1)S(1)} %get-tuple-element.32.a_ref, bf16[1024,5120]{1,0:T(8,128)(2,1)} %bitcast.15), custom_call_target="tpu_custom_call" | custom-call | tf_op jit(solution)/shard_map/out_projection/pallas_call | solution.py:46
  73.8 1.8 %collective-permute-start.8 = (bf16[256,1280]{1,0:T(8,128)(2,1)S(1)}, bf16[256,1280]{1,0:T(8,128)(2,1)S(1)}, u32[]{:S(2)}, u32[]{:S(2)}) collective-permute-start(bf16[256,1280]{1,0:T(8,128)(2,1)S(1)} %get-tuple-element.33), channel_id=1, source_target_pairs={{0,8},{1,9},{2,10},{3,11},{8,16},{9,17},{10,18},{11,19},{16,24},{1... | collective-permute-start | bytes 1966088 | tf_op jit(solution)/shard_map/ppermute | solution.py:23
  75.6 3.8 %collective-permute-start.9 = (bf16[256,1280]{1,0:T(8,128)(2,1)S(1)}, bf16[256,1280]{1,0:T(8,128)(2,1)S(1)}, u32[]{:S(2)}, u32[]{:S(2)}) collective-permute-start(bf16[256,1280]{1,0:T(8,128)(2,1)S(1)} %get-tuple-element.34), channel_id=1, source_target_pairs={{0,10},{3,9},{1,8},{2,11},{8,18},{11,17},{9,16},{10,19},{16,26},{1... | collective-permute-start | bytes 1966088 | tf_op jit(solution)/shard_map/ppermute | solution.py:23
  79.3 2.9 %collective-permute-done.10 = bf16[256,1280]{1,0:T(8,128)(2,1)S(1)} collective-permute-done((bf16[256,1280]{1,0:T(8,128)(2,1)S(1)}, bf16[256,1280]{1,0:T(8,128)(2,1)S(1)}, u32[]{:S(2)}, u32[]{:S(2)}) %collective-permute-start.10) | collective-permute-done | bytes 655392 | tf_op jit(solution)/shard_map/ppermute | solution.py:23
  82.4 4.4 %collective-permute-start.11 = (bf16[256,1280]{1,0:T(8,128)(2,1)S(1)}, bf16[256,1280]{1,0:T(8,128)(2,1)S(1)}, u32[]{:S(2)}, u32[]{:S(2)}) collective-permute-start(bf16[256,1280]{1,0:T(8,128)(2,1)S(1)} %add_convert_fusion.1), channel_id=1, source_target_pairs={{0,9},{3,10},{1,11},{2,8},{8,17},{11,18},{9,19},{10,16},{16,25},{1... | collective-permute-start | bytes 1966088 | tf_op jit(solution)/shard_map/ppermute | solution.py:23
  86.8 5.1 %collective-permute-done.8 = bf16[256,1280]{1,0:T(8,128)(2,1)S(1)} collective-permute-done((bf16[256,1280]{1,0:T(8,128)(2,1)S(1)}, bf16[256,1280]{1,0:T(8,128)(2,1)S(1)}, u32[]{:S(2)}, u32[]{:S(2)}) %collective-permute-start.8) | collective-permute-done | bytes 655392 | tf_op jit(solution)/shard_map/ppermute | solution.py:23
  91.9 4.4 %collective-permute-done.9 = bf16[256,1280]{1,0:T(8,128)(2,1)S(1)} collective-permute-done((bf16[256,1280]{1,0:T(8,128)(2,1)S(1)}, bf16[256,1280]{1,0:T(8,128)(2,1)S(1)}, u32[]{:S(2)}, u32[]{:S(2)}) %collective-permute-start.9) | collective-permute-done | bytes 655392 | tf_op jit(solution)/shard_map/ppermute | solution.py:23
  96.3 20.1 %collective-permute-done.11 = bf16[256,1280]{1,0:T(8,128)(2,1)S(1)} collective-permute-done((bf16[256,1280]{1,0:T(8,128)(2,1)S(1)}, bf16[256,1280]{1,0:T(8,128)(2,1)S(1)}, u32[]{:S(2)}, u32[]{:S(2)}) %collective-permute-start.11) | collective-permute-done | bytes 655392 | tf_op jit(solution)/shard_map/ppermute | solution.py:23
  116.4 1.3 %fusion = bf16[1,256,1280]{2,1,0:T(8,128)(2,1)} fusion(bf16[256,1280]{1,0:T(8,128)(2,1)S(1)} %collective-permute-done.12, bf16[256,1280]{1,0:T(8,128)(2,1)S(1)} %collective-permute-done.11, bf16[256,1280]{1,0:T(8,128)(2,1)S(1)} %collective-permute-done.9, bf16[256,1280]{1,0:T(8,128)(2,1)S(1)} %collective-permute-done.8, ...), kind=kLoop, calls=%fused_computation.4 | loop fusion | flops 3276800 | bytes 3932160 | tf_op jit(solution)/shard_map/broadcast_in_dim | solution.py:489
  (22 shorter events, 3.5 us)
Async XLA Ops:
  0.6 20.1 %collective-permute-start = (bf16[256,1280]{1,0:T(8,128)(2,1)}, bf16[256,1280]{1,0:T(8,128)(2,1)S(1)}, u32[]{:S(2)}, u32[]{:S(2)}) collective-permute-start(bf16[256,1280]{1,0:T(8,128)(2,1)} %bitcast.2.own), channel_id=1, source_target_pairs={{0,2},{3,1},{1,0},{2,3},{4,6},{7,5},{5,4},{6,7},{8,10},{11,9},{9,8... | collective-permute-start | bytes 1966088 | tf_op jit(solution)/shard_map/ppermute | solution.py:23
  6.0 14.7 %collective-permute-start.1 = (f32[1,256]{1,0:T(1,128)S(1)}, f32[1,256]{1,0:T(1,128)S(1)}, u32[]{:S(2)}, u32[]{:S(2)}) collective-permute-start(f32[1,256]{1,0:T(1,128)S(1)} %bitcast.21), channel_id=1, source_target_pairs={{0,3},{1,2},{2,1},{3,0},{4,7},{5,6},{6,5},{7,4},{8,11},{9,10},{10,... | collective-permute-start | bytes 3080 | tf_op jit(solution)/shard_map/ppermute | solution.py:23
  20.8 18.8 %collective-permute-start.5 = (bf16[256,1280]{1,0:T(8,128)(2,1)}, bf16[256,1280]{1,0:T(8,128)(2,1)S(1)}, u32[]{:S(2)}, u32[]{:S(2)}) collective-permute-start(bf16[256,1280]{1,0:T(8,128)(2,1)} %bitcast.2.own), channel_id=1, source_target_pairs={{0,1},{3,2},{1,3},{2,0},{4,5},{7,6},{5,7},{6,4},{8,9},{11,10},{9,1... | collective-permute-start | bytes 1966088 | tf_op jit(solution)/shard_map/ppermute | solution.py:23
  21.3 27.3 %collective-permute-start.3 = (bf16[256,1280]{1,0:T(8,128)(2,1)}, bf16[256,1280]{1,0:T(8,128)(2,1)S(1)}, u32[]{:S(2)}, u32[]{:S(2)}) collective-permute-start(bf16[256,1280]{1,0:T(8,128)(2,1)} %bitcast.2.own), channel_id=1, source_target_pairs={{1,2},{2,1},{5,6},{6,5},{9,10},{10,9},{13,14},{14,13},{17,18},{18,... | collective-permute-start | bytes 1966088 | tf_op jit(solution)/shard_map/ppermute | solution.py:23
  22.0 29.2 %collective-permute-start.4 = (bf16[256,1280]{1,0:T(8,128)(2,1)S(1)}, bf16[256,1280]{1,0:T(8,128)(2,1)S(1)}, u32[]{:S(2)}, u32[]{:S(2)}) collective-permute-start(bf16[256,1280]{1,0:T(8,128)(2,1)S(1)} %collective-permute-done.one), channel_id=1, source_target_pairs={{1,0},{2,3},{5,4},{6,7},{9,8},{10,11},{13,12},{14,15},{17,16},{18,... | collective-permute-start | bytes 1966088 | tf_op jit(solution)/shard_map/ppermute | solution.py:23
  23.3 31.0 %collective-permute-start.2 = (bf16[1024,256]{1,0:T(8,128)(2,1)}, bf16[1024,256]{1,0:T(8,128)(2,1)S(1)}, u32[]{:S(2)}, u32[]{:S(2)}) collective-permute-start(bf16[1024,256]{1,0:T(8,128)(2,1)} %bitcast.18), channel_id=1, source_target_pairs={{0,4},{4,0},{1,5},{5,1},{2,6},{6,2},{3,7},{7,3},{8,12},{12,8},{9,1... | collective-permute-start | bytes 1572872 | tf_op jit(solution)/shard_map/ppermute | solution.py:23
  39.7 0.7 copy-start
  51.2 3.1 %copy-start.4 = (bf16[1,1024,1,256]{3,1,2,0:T(8,128)(2,1)S(1)}, bf16[1,1024,1,256]{3,1,2,0:T(8,128)(2,1)}, u32[]{:S(2)}) copy-start(bf16[1,1024,1,256]{3,1,2,0:T(8,128)(2,1)} %param.14) | copy-start | bytes 1572868
  52.7 5.5 %collective-permute-start.6 = (bf16[256,256]{1,0:T(8,128)(2,1)S(1)}, bf16[256,256]{1,0:T(8,128)(2,1)S(1)}, u32[]{:S(2)}, u32[]{:S(2)}) collective-permute-start(bf16[256,256]{1,0:T(8,128)(2,1)S(1)} %get-tuple-element.26.refs_1_), channel_id=1, source_target_pairs={{0,4},{4,0},{1,5},{5,1},{2,6},{6,2},{3,7},{7,3},{8,12},{12,8},{9,1... | collective-permute-start | bytes 393224 | tf_op jit(solution)/shard_map/ppermute | solution.py:23
  54.6 14.5 %collective-permute-start.7 = (bf16[256,1280]{1,0:T(8,128)(2,1)}, bf16[256,1280]{1,0:T(8,128)(2,1)S(1)}, u32[]{:S(2)}, u32[]{:S(2)}) collective-permute-start(bf16[256,1280]{1,0:T(8,128)(2,1)} %bitcast.2.own), channel_id=1, source_target_pairs={{0,8},{1,9},{2,10},{3,11},{8,16},{9,17},{10,18},{11,19},{16,24},{1... | collective-permute-start | bytes 1966088 | tf_op jit(solution)/shard_map/ppermute | solution.py:23
  54.7 3.5 %copy-start.1 = (s32[1,4]{1,0:T(1,128)S(1)}, s32[1,4]{1,0:T(1,128)}, u32[]{:S(2)}) copy-start(s32[1,4]{1,0:T(1,128)} %row_lengths.1) | copy-start | bytes 52
  54.7 3.5 %copy-start.2 = (s32[1,4]{1,0:T(1,128)S(1)}, s32[1,4]{1,0:T(1,128)}, u32[]{:S(2)}) copy-start(s32[1,4]{1,0:T(1,128)} %cache_lengths.1) | copy-start | bytes 52
  54.7 3.5 %copy-start.3 = (s32[1,4,1]{1,2,0:T(1,128)S(1)}, s32[1,4,1]{1,2,0:T(1,128)}, u32[]{:S(2)}) copy-start(s32[1,4,1]{1,2,0:T(1,128)} %param.17) | copy-start | bytes 52
  66.1 16.1 %collective-permute-start.10 = (bf16[256,1280]{1,0:T(8,128)(2,1)S(1)}, bf16[256,1280]{1,0:T(8,128)(2,1)S(1)}, u32[]{:S(2)}, u32[]{:S(2)}) collective-permute-start(bf16[256,1280]{1,0:T(8,128)(2,1)S(1)} %get-tuple-element.36), channel_id=1, source_target_pairs={{0,1},{3,2},{4,5},{7,6},{8,9},{11,10},{12,13},{15,14},{16,17},{19,... | collective-permute-start | bytes 1966088 | tf_op jit(solution)/shard_map/ppermute | solution.py:23
  68.2 18.5 %collective-permute-start.12 = (bf16[256,1280]{1,0:T(8,128)(2,1)S(1)}, bf16[256,1280]{1,0:T(8,128)(2,1)S(1)}, u32[]{:S(2)}, u32[]{:S(2)}) collective-permute-start(bf16[256,1280]{1,0:T(8,128)(2,1)S(1)} %get-tuple-element.36), channel_id=1, source_target_pairs={{1,10},{2,9},{9,18},{10,17},{17,26},{18,25},{25,2},{26,1},{5,14},{... | collective-permute-start | bytes 1966088 | tf_op jit(solution)/shard_map/ppermute | solution.py:23
  73.8 18.1 %collective-permute-start.8 = (bf16[256,1280]{1,0:T(8,128)(2,1)S(1)}, bf16[256,1280]{1,0:T(8,128)(2,1)S(1)}, u32[]{:S(2)}, u32[]{:S(2)}) collective-permute-start(bf16[256,1280]{1,0:T(8,128)(2,1)S(1)} %get-tuple-element.33), channel_id=1, source_target_pairs={{0,8},{1,9},{2,10},{3,11},{8,16},{9,17},{10,18},{11,19},{16,24},{1... | collective-permute-start | bytes 1966088 | tf_op jit(solution)/shard_map/ppermute | solution.py:23
  75.6 20.7 %collective-permute-start.9 = (bf16[256,1280]{1,0:T(8,128)(2,1)S(1)}, bf16[256,1280]{1,0:T(8,128)(2,1)S(1)}, u32[]{:S(2)}, u32[]{:S(2)}) collective-permute-start(bf16[256,1280]{1,0:T(8,128)(2,1)S(1)} %get-tuple-element.34), channel_id=1, source_target_pairs={{0,10},{3,9},{1,8},{2,11},{8,18},{11,17},{9,16},{10,19},{16,26},{1... | collective-permute-start | bytes 1966088 | tf_op jit(solution)/shard_map/ppermute | solution.py:23
  82.4 34.0 %collective-permute-start.11 = (bf16[256,1280]{1,0:T(8,128)(2,1)S(1)}, bf16[256,1280]{1,0:T(8,128)(2,1)S(1)}, u32[]{:S(2)}, u32[]{:S(2)}) collective-permute-start(bf16[256,1280]{1,0:T(8,128)(2,1)S(1)} %add_convert_fusion.1), channel_id=1, source_target_pairs={{0,9},{3,10},{1,11},{2,8},{8,17},{11,18},{9,19},{10,16},{16,25},{1... | collective-permute-start | bytes 1966088 | tf_op jit(solution)/shard_map/ppermute | solution.py:23

commit v3 on v2

--- a/solution.py
+++ b/solution.py
@@ -16,7 +16,8 @@
 SCORE_BYTES = 13 * MIB
 PARTS = 4
 WEIGHT_CUTS = 4
-KEY_TILE = 384
+CACHE_TILE = 640
+NEW_TILE = 512
 
 
 def swap(block, axis, pairs):
@@ -226,11 +227,11 @@
 
 
 def attend_kernel(
-    row_lengths, cache_lengths, owners, *refs, count, places, sub_rows, heads, tile, divisor
+    row_lengths, cache_lengths, owners, *refs, count, places, sub_rows, heads, divisor
 ):
     cache, pieces = refs[0], refs[1 : 1 + count]
     q_ref, w_ref, attended_rows, part_ref, held_ref = refs[1 + count : 6 + count]
-    w_held, fresh, scores, top, total, acc, sems, w_sems = refs[6 + count :]
+    w_held, fresh, old_scores, new_scores, top, total, acc, sems, w_sems = refs[6 + count :]
     rank = lax.axis_index("dp")
     place = lax.axis_index("tensor")
     row_count = q_ref.shape[0]
@@ -268,13 +269,18 @@
         pairs += jnp.where(owners[0, block] == rank, found, 0)
     held_ref[...] = jnp.full(held_ref.shape, pairs, jnp.int32).astype(jnp.float32) / divisor
 
-    def span(start, end):
+    def span(scores, start, end):
+        tile = scores.shape[2]
         start = lax.div(start, 16) * 16
         return start, lax.div(end - start + tile - 1, tile)
 
-    def tile_start(source, first, t):
+    def tile_start(scores, source, first, t):
+        tile = scores.shape[2]
         start = first + t * tile
         return start, pl.multiple_of(jnp.minimum(start, source.shape[0] - tile), 16)
+
+    def lane_blocks(values):
+        return [values[:, c : c + lanes] for c in range(0, values.shape[1], lanes)]
 
     for step in range(row_count // sub_rows):
         spots = slice(step * sub_rows, (step + 1) * sub_rows)
@@ -288,9 +294,11 @@
         total[...] = jnp.zeros(total.shape, jnp.float32)
         acc[...] = jnp.zeros(acc.shape, jnp.float32)
 
-        def score(source, first, base, low, high):
+        def score(scores, source, first, low, high):
+            tile = scores.shape[2]
+
             def body(t, _):
-                begin, start = tile_start(source, first, t)
+                begin, start = tile_start(scores, source, first, t)
                 found = lax.dot_general(
                     queries,
                     source[pl.ds(start, tile), :HEAD_SIZE],
@@ -301,35 +309,37 @@
                 seen = (spot >= jnp.maximum(low, begin)) & (spot < high)
                 found = jnp.where(seen[None], found.reshape(heads, sub_rows, tile), NEG)
                 found = found.reshape(stacked, tile)
-                scores[base + t] = found
-                best = found[:, :lanes]
-                for c in range(1, tile // lanes):
-                    best = jnp.maximum(best, found[:, c * lanes : (c + 1) * lanes])
-                top[...] = jnp.maximum(top[...], best)
+                scores[t] = found
+                top[...] = functools.reduce(jnp.maximum, lane_blocks(found), top[...])
                 return 0
 
             return body
 
-        cache_from, cache_tiles = span(by_doc(first_row, cache_start), by_doc(last_row, cache_end))
-        new_from, new_tiles = span(by_doc(first_row, row_start), last_row + 1)
+        cache_from, cache_tiles = span(
+            old_scores, by_doc(first_row, cache_start), by_doc(last_row, cache_end)
+        )
+        new_from, new_tiles = span(new_scores, by_doc(first_row, row_start), last_row + 1)
         low, high = by_doc(rows, cache_start), by_doc(rows, cache_end)
-        lax.fori_loop(0, cache_tiles, score(cache, cache_from, 0, low, high), 0)
+        lax.fori_loop(0, cache_tiles, score(old_scores, cache, cache_from, low, high), 0)
         if step == 0:
             wait_copies(copies)
         low, high = by_doc(rows, row_start), rows + 1
-        lax.fori_loop(0, new_tiles, score(fresh, new_from, cache_tiles, low, high), 0)
-        highest = jnp.max(top[...], axis=1, keepdims=True)
-
-        def weigh(source, first, base):
+        lax.fori_loop(0, new_tiles, score(new_scores, fresh, new_from, low, high), 0)
+        top[...] = jnp.broadcast_to(jnp.max(top[...], axis=1, keepdims=True), top.shape)
+
+        def weigh(scores, source, first):
+            tile = scores.shape[2]
+
             def body(t, _):
-                _, start = tile_start(source, first, t)
-                weights = jnp.exp2((scores[base + t] - highest) * (HEAD_SIZE**-0.5 * LOG2E))
-                part = weights[:, :lanes]
-                for c in range(1, tile // lanes):
-                    part = part + weights[:, c * lanes : (c + 1) * lanes]
-                total[...] += part
+                _, start = tile_start(scores, source, first, t)
+                highest = top[...]
+                weights = [
+                    jnp.exp2((scores[t, :, c : c + lanes] - highest) * (HEAD_SIZE**-0.5 * LOG2E))
+                    for c in range(0, tile, lanes)
+                ]
+                total[...] = functools.reduce(jnp.add, weights, total[...])
                 acc[...] += jnp.dot(
-                    weights.astype(jnp.bfloat16),
+                    jnp.concatenate([w.astype(jnp.bfloat16) for w in weights], axis=1),
                     source[pl.ds(start, tile), HEAD_SIZE:],
                     preferred_element_type=jnp.float32,
                 )
@@ -337,8 +347,8 @@
 
             return body
 
-        lax.fori_loop(0, cache_tiles, weigh(cache, cache_from, 0), 0)
-        lax.fori_loop(0, new_tiles, weigh(fresh, new_from, cache_tiles), 0)
+        lax.fori_loop(0, cache_tiles, weigh(old_scores, cache, cache_from), 0)
+        lax.fori_loop(0, new_tiles, weigh(new_scores, fresh, new_from), 0)
         attended = (acc[...] / jnp.sum(total[...], axis=1, keepdims=True)).astype(jnp.bfloat16)
         for h in range(heads):
             attended_rows[spots, h * HEAD_SIZE : (h + 1) * HEAD_SIZE] = attended[
@@ -353,9 +363,9 @@
 def attention(scalars, queries, cache, pieces, places, fresh, w, divisor):
     rows, width = queries.shape
     heads = width // HEAD_SIZE
-    tiles = sum(pl.cdiv(amount, KEY_TILE) for amount in (cache.shape[0], fresh))
+    sizes = [(pl.cdiv(cache.shape[0], CACHE_TILE), CACHE_TILE), (pl.cdiv(fresh, NEW_TILE), NEW_TILE)]
     sub_rows = BLOCK_ROWS
-    while sub_rows > 32 and heads * sub_rows * tiles * KEY_TILE * 4 > SCORE_BYTES:
+    while sub_rows > 32 and heads * sub_rows * 4 * sum(a * b for a, b in sizes) > SCORE_BYTES:
         sub_rows //= 2
     stacked = heads * sub_rows
     out_width = w.shape[1] // PARTS
@@ -366,7 +376,6 @@
             places=places,
             sub_rows=sub_rows,
             heads=heads,
-            tile=KEY_TILE,
             divisor=divisor,
         ),
         "attention",
@@ -377,7 +386,7 @@
         scratch=[
             pltpu.VMEM((width, out_width), jnp.bfloat16),
             pltpu.VMEM((fresh, 2 * HEAD_SIZE), jnp.bfloat16),
-            pltpu.VMEM((tiles, stacked, KEY_TILE), jnp.float32),
+            *(pltpu.VMEM((tiles, stacked, tile), jnp.float32) for tiles, tile in sizes),
             pltpu.VMEM((stacked, 128), jnp.float32),
             pltpu.VMEM((stacked, 128), jnp.float32),
             pltpu.VMEM((stacked, HEAD_SIZE), jnp.float32),

time: 119 us -> 118 us (level)
  transfers between devices with their start and end apart: 13 -> 13, of which waited for: 8 -> 8; matrix products, arithmetic and copies ran while one was open for 2% -> 2% of each run, Pallas kernels for 21% -> 22%
where the time goes in v3:
time: 118 us; the launch traced here: 116 us
  waiting for transfers between devices  63.1 us (53%)
  Pallas kernels  25.4 us (22%)
  starting transfers between devices  23.2 us (20%)
  other arithmetic  3.04 us (3%)
    ppermute x13, waiting for transfers between devices, swap(): return lax.ppermute(block, axis, pairs)  63.1 us
    pallas_call x5, Pallas kernels, resident(): pl.pallas_call(kernel, in_specs=spaces, out_specs=[pl.BlockSpec(memory_sp...  25.4 us
    ppermute x13, starting transfers between devices, swap(): return lax.ppermute(block, axis, pairs)  23.2 us
  transfers between devices with their start and end apart: 13, of which 8 were waited for; matrix products, arithmetic and copies ran while one was open for 2% of the time, Pallas kernels for 22%

profile of v3, /device:TPU:0, one launch (start us, length us, event | category | flops | bytes accessed | tf_op | source)
XLA Modules:
  0.0 116.3 jit_solution(664697399630939452)
XLA Ops:
  0.6 4.1 %collective-permute-start = (bf16[256,1280]{1,0:T(8,128)(2,1)}, bf16[256,1280]{1,0:T(8,128)(2,1)S(1)}, u32[]{:S(2)}, u32[]{:S(2)}) collective-permute-start(bf16[256,1280]{1,0:T(8,128)(2,1)} %bitcast.2.own), channel_id=1, source_target_pairs={{0,2},{3,1},{1,0},{2,3},{4,6},{7,5},{5,4},{6,7},{8,10},{11,9},{9,8... | collective-permute-start | bytes 1966088 | tf_op jit(solution)/shard_map/ppermute | solution.py:24
  4.7 1.3 %multiply_reduce_fusion = f32[256]{0:T(256)S(1)} fusion(bf16[1,256,1280]{2,1,0:T(8,128)(2,1)} %param.9), kind=kLoop, calls=%fused_computation.2 | loop fusion | flops 982784 | bytes 656384 | tf_op jit(solution)/shard_map/reduce_sum | solution.py:457
  6.0 1.4 %collective-permute-start.1 = (f32[1,256]{1,0:T(1,128)S(1)}, f32[1,256]{1,0:T(1,128)S(1)}, u32[]{:S(2)}, u32[]{:S(2)}) collective-permute-start(f32[1,256]{1,0:T(1,128)S(1)} %bitcast.21), channel_id=1, source_target_pairs={{0,3},{1,2},{2,1},{3,0},{4,7},{5,6},{6,5},{7,4},{8,11},{9,10},{10,... | collective-permute-start | bytes 3080 | tf_op jit(solution)/shard_map/ppermute | solution.py:24
  7.5 13.3 %collective-permute-done.1 = f32[1,256]{1,0:T(1,128)S(1)} collective-permute-done((f32[1,256]{1,0:T(1,128)S(1)}, f32[1,256]{1,0:T(1,128)S(1)}, u32[]{:S(2)}, u32[]{:S(2)}) %collective-permute-start.1) | collective-permute-done | bytes 1056 | tf_op jit(solution)/shard_map/ppermute | solution.py:24
  22.0 1.3 %collective-permute-start.4 = (bf16[256,1280]{1,0:T(8,128)(2,1)S(1)}, bf16[256,1280]{1,0:T(8,128)(2,1)S(1)}, u32[]{:S(2)}, u32[]{:S(2)}) collective-permute-start(bf16[256,1280]{1,0:T(8,128)(2,1)S(1)} %collective-permute-done.one), channel_id=1, source_target_pairs={{1,0},{2,3},{5,4},{6,7},{9,8},{10,11},{13,12},{14,15},{17,16},{18,... | collective-permute-start | bytes 1966088 | tf_op jit(solution)/shard_map/ppermute | solution.py:24
  23.3 1.6 %collective-permute-start.2 = (bf16[1024,256]{1,0:T(8,128)(2,1)}, bf16[1024,256]{1,0:T(8,128)(2,1)S(1)}, u32[]{:S(2)}, u32[]{:S(2)}) collective-permute-start(bf16[1024,256]{1,0:T(8,128)(2,1)} %bitcast.18), channel_id=1, source_target_pairs={{0,4},{4,0},{1,5},{5,1},{2,6},{6,2},{3,7},{7,3},{8,12},{12,8},{9,1... | collective-permute-start | bytes 1572872 | tf_op jit(solution)/shard_map/ppermute | solution.py:24
  24.9 14.7 %collective-permute-done.5.two = bf16[256,1280]{1,0:T(8,128)(2,1)S(1)} collective-permute-done((bf16[256,1280]{1,0:T(8,128)(2,1)}, bf16[256,1280]{1,0:T(8,128)(2,1)S(1)}, u32[]{:S(2)}, u32[]{:S(2)}) %collective-permute-start.5) | collective-permute-done | bytes 655392 | tf_op jit(solution)/shard_map/ppermute | solution.py:24
  40.4 8.2 %early_projection.1 = (f32[256,1024]{1,0:T(8,128)S(1)}, f32[256,256]{1,0:T(8,128)S(1)}, f32[256,128]{1,0:T(8,128)S(1)}) custom-call(bf16[256,1280]{1,0:T(8,128)(2,1)} %bitcast.2.own, bf16[256,1280]{1,0:T(8,128)(2,1)S(1)} %collective-permute-done.one, bf16[256,1280]{1,0:T(8,128)(2,1)S(1)} %collective-permute-done.5.two, ...), custom_call_target="tpu_custom_call" | custom-call | tf_op jit(solution)/shard_map/early_projection/pallas_call | solution.py:47
  48.7 2.6 %collective-permute-done.4.relayed = bf16[256,1280]{1,0:T(8,128)(2,1)S(1)} collective-permute-done((bf16[256,1280]{1,0:T(8,128)(2,1)S(1)}, bf16[256,1280]{1,0:T(8,128)(2,1)S(1)}, u32[]{:S(2)}, u32[]{:S(2)}) %collective-permute-start.4) | collective-permute-done | bytes 655392 | tf_op jit(solution)/shard_map/ppermute | solution.py:24
  51.2 1.5 %last_kv.1 = (bf16[256,256]{1,0:T(8,128)(2,1)S(1)}, bf16[256,1280]{1,0:T(8,128)(2,1)S(1)}) custom-call(bf16[256,1280]{1,0:T(8,128)(2,1)S(1)} %collective-permute-done.3.cross, bf16[256,1280]{1,0:T(8,128)(2,1)S(1)} %collective-permute-done.4.relayed, f32[256,128]{1,0:T(8,128)S(1)} %get-tuple-element.24.factor_ref, bf16[1,5120]{1,0:T(2,128)(2,1)S(1)} %copy-done, ...), custom_call_target="tpu_custom_call" | custom-call | tf_op jit(solution)/shard_map/last_kv/pallas_call | solution.py:47
  52.7 1.6 %collective-permute-start.6 = (bf16[256,256]{1,0:T(8,128)(2,1)S(1)}, bf16[256,256]{1,0:T(8,128)(2,1)S(1)}, u32[]{:S(2)}, u32[]{:S(2)}) collective-permute-start(bf16[256,256]{1,0:T(8,128)(2,1)S(1)} %get-tuple-element.26.refs_1_), channel_id=1, source_target_pairs={{0,4},{4,0},{1,5},{5,1},{2,6},{6,2},{3,7},{7,3},{8,12},{12,8},{9,1... | collective-permute-start | bytes 393224 | tf_op jit(solution)/shard_map/ppermute | solution.py:24
  54.7 2.6 %last_q.1.refs_3_ = bf16[256,1024]{1,0:T(8,128)(2,1)S(1)} custom-call(bf16[256,1280]{1,0:T(8,128)(2,1)S(1)} %get-tuple-element.27.normed, f32[256,1024]{1,0:T(8,128)S(1)} %get-tuple-element.28.acc_ref, bf16[5120,1024]{1,0:T(8,128)(2,1)} %bitcast.13), custom_call_target="tpu_custom_call" | custom-call | tf_op jit(solution)/shard_map/last_q/pallas_call | solution.py:47
  57.4 0.9 collective-permute-done.6.refs_2_
  58.2 8.4 %attention.1 = (bf16[256,1024]{1,0:T(8,128)(2,1)S(1)}, bf16[256,1280]{1,0:T(8,128)(2,1)S(1)}, f32[1,1]{1,0:T(1,128)}) custom-call(s32[1,4]{1,0:T(1,128)S(1)} %copy-done.1, s32[1,4]{1,0:T(1,128)S(1)} %copy-done.2, s32[1,4]{1,0:T(1,128)S(1)} %bitcast.11, bf16[2048,256]{1,0:T(8,128)(2,1)S(1)} %maximum_select_fusion.refs_0_, ...), custom_call_target="tpu_custom_call" | custom-call | bytes 10485760 | tf_op jit(solution)/shard_map/attention/pallas_call | solution.py:47
  66.6 2.1 %collective-permute-start.10 = (bf16[256,1280]{1,0:T(8,128)(2,1)S(1)}, bf16[256,1280]{1,0:T(8,128)(2,1)S(1)}, u32[]{:S(2)}, u32[]{:S(2)}) collective-permute-start(bf16[256,1280]{1,0:T(8,128)(2,1)S(1)} %get-tuple-element.36), channel_id=1, source_target_pairs={{0,1},{3,2},{4,5},{7,6},{8,9},{11,10},{12,13},{15,14},{16,17},{19,... | collective-permute-start | bytes 1966088 | tf_op jit(solution)/shard_map/ppermute | solution.py:24
  68.7 0.9 collective-permute-start.12
  69.6 4.7 %out_projection.1 = (bf16[256,1280]{1,0:T(8,128)(2,1)S(1)}, bf16[256,1280]{1,0:T(8,128)(2,1)S(1)}, bf16[256,1280]{1,0:T(8,128)(2,1)S(1)}) custom-call(bf16[256,1024]{1,0:T(8,128)(2,1)S(1)} %get-tuple-element.32.a_ref, bf16[1024,5120]{1,0:T(8,128)(2,1)} %bitcast.15), custom_call_target="tpu_custom_call" | custom-call | tf_op jit(solution)/shard_map/out_projection/pallas_call | solution.py:47
  74.3 2.2 %collective-permute-start.8 = (bf16[256,1280]{1,0:T(8,128)(2,1)S(1)}, bf16[256,1280]{1,0:T(8,128)(2,1)S(1)}, u32[]{:S(2)}, u32[]{:S(2)}) collective-permute-start(bf16[256,1280]{1,0:T(8,128)(2,1)S(1)} %get-tuple-element.33), channel_id=1, source_target_pairs={{0,8},{1,9},{2,10},{3,11},{8,16},{9,17},{10,18},{11,19},{16,24},{1... | collective-permute-start | bytes 1966088 | tf_op jit(solution)/shard_map/ppermute | solution.py:24
  76.5 1.5 %collective-permute-start.9 = (bf16[256,1280]{1,0:T(8,128)(2,1)S(1)}, bf16[256,1280]{1,0:T(8,128)(2,1)S(1)}, u32[]{:S(2)}, u32[]{:S(2)}) collective-permute-start(bf16[256,1280]{1,0:T(8,128)(2,1)S(1)} %get-tuple-element.34), channel_id=1, source_target_pairs={{0,10},{3,9},{1,8},{2,11},{8,18},{11,17},{9,16},{10,19},{16,26},{1... | collective-permute-start | bytes 1966088 | tf_op jit(solution)/shard_map/ppermute | solution.py:24
  78.0 4.3 %collective-permute-done.10 = bf16[256,1280]{1,0:T(8,128)(2,1)S(1)} collective-permute-done((bf16[256,1280]{1,0:T(8,128)(2,1)S(1)}, bf16[256,1280]{1,0:T(8,128)(2,1)S(1)}, u32[]{:S(2)}, u32[]{:S(2)}) %collective-permute-start.10) | collective-permute-done | bytes 655392 | tf_op jit(solution)/shard_map/ppermute | solution.py:24
  82.4 5.2 %collective-permute-start.11 = (bf16[256,1280]{1,0:T(8,128)(2,1)S(1)}, bf16[256,1280]{1,0:T(8,128)(2,1)S(1)}, u32[]{:S(2)}, u32[]{:S(2)}) collective-permute-start(bf16[256,1280]{1,0:T(8,128)(2,1)S(1)} %add_convert_fusion.1), channel_id=1, source_target_pairs={{0,9},{3,10},{1,11},{2,8},{8,17},{11,18},{9,19},{10,16},{16,25},{1... | collective-permute-start | bytes 1966088 | tf_op jit(solution)/shard_map/ppermute | solution.py:24
  87.7 8.6 %collective-permute-done.9 = bf16[256,1280]{1,0:T(8,128)(2,1)S(1)} collective-permute-done((bf16[256,1280]{1,0:T(8,128)(2,1)S(1)}, bf16[256,1280]{1,0:T(8,128)(2,1)S(1)}, u32[]{:S(2)}, u32[]{:S(2)}) %collective-permute-start.9) | collective-permute-done | bytes 655392 | tf_op jit(solution)/shard_map/ppermute | solution.py:24
  96.4 18.7 %collective-permute-done.11 = bf16[256,1280]{1,0:T(8,128)(2,1)S(1)} collective-permute-done((bf16[256,1280]{1,0:T(8,128)(2,1)S(1)}, bf16[256,1280]{1,0:T(8,128)(2,1)S(1)}, u32[]{:S(2)}, u32[]{:S(2)}) %collective-permute-start.11) | collective-permute-done | bytes 655392 | tf_op jit(solution)/shard_map/ppermute | solution.py:24
  115.0 1.3 %fusion = bf16[1,256,1280]{2,1,0:T(8,128)(2,1)} fusion(bf16[256,1280]{1,0:T(8,128)(2,1)S(1)} %collective-permute-done.12, bf16[256,1280]{1,0:T(8,128)(2,1)S(1)} %collective-permute-done.11, bf16[256,1280]{1,0:T(8,128)(2,1)S(1)} %collective-permute-done.9, bf16[256,1280]{1,0:T(8,128)(2,1)S(1)} %collective-permute-done.8, ...), kind=kLoop, calls=%fused_computation.4 | loop fusion | flops 3276800 | bytes 3932160 | tf_op jit(solution)/shard_map/broadcast_in_dim | solution.py:498
  (22 shorter events, 2.6 us)
Async XLA Ops:
  0.6 20.1 %collective-permute-start = (bf16[256,1280]{1,0:T(8,128)(2,1)}, bf16[256,1280]{1,0:T(8,128)(2,1)S(1)}, u32[]{:S(2)}, u32[]{:S(2)}) collective-permute-start(bf16[256,1280]{1,0:T(8,128)(2,1)} %bitcast.2.own), channel_id=1, source_target_pairs={{0,2},{3,1},{1,0},{2,3},{4,6},{7,5},{5,4},{6,7},{8,10},{11,9},{9,8... | collective-permute-start | bytes 1966088 | tf_op jit(solution)/shard_map/ppermute | solution.py:24
  6.0 14.7 %collective-permute-start.1 = (f32[1,256]{1,0:T(1,128)S(1)}, f32[1,256]{1,0:T(1,128)S(1)}, u32[]{:S(2)}, u32[]{:S(2)}) collective-permute-start(f32[1,256]{1,0:T(1,128)S(1)} %bitcast.21), channel_id=1, source_target_pairs={{0,3},{1,2},{2,1},{3,0},{4,7},{5,6},{6,5},{7,4},{8,11},{9,10},{10,... | collective-permute-start | bytes 3080 | tf_op jit(solution)/shard_map/ppermute | solution.py:24
  20.8 18.8 %collective-permute-start.5 = (bf16[256,1280]{1,0:T(8,128)(2,1)}, bf16[256,1280]{1,0:T(8,128)(2,1)S(1)}, u32[]{:S(2)}, u32[]{:S(2)}) collective-permute-start(bf16[256,1280]{1,0:T(8,128)(2,1)} %bitcast.2.own), channel_id=1, source_target_pairs={{0,1},{3,2},{1,3},{2,0},{4,5},{7,6},{5,7},{6,4},{8,9},{11,10},{9,1... | collective-permute-start | bytes 1966088 | tf_op jit(solution)/shard_map/ppermute | solution.py:24
  21.3 27.3 %collective-permute-start.3 = (bf16[256,1280]{1,0:T(8,128)(2,1)}, bf16[256,1280]{1,0:T(8,128)(2,1)S(1)}, u32[]{:S(2)}, u32[]{:S(2)}) collective-permute-start(bf16[256,1280]{1,0:T(8,128)(2,1)} %bitcast.2.own), channel_id=1, source_target_pairs={{1,2},{2,1},{5,6},{6,5},{9,10},{10,9},{13,14},{14,13},{17,18},{18,... | collective-permute-start | bytes 1966088 | tf_op jit(solution)/shard_map/ppermute | solution.py:24
  22.0 29.2 %collective-permute-start.4 = (bf16[256,1280]{1,0:T(8,128)(2,1)S(1)}, bf16[256,1280]{1,0:T(8,128)(2,1)S(1)}, u32[]{:S(2)}, u32[]{:S(2)}) collective-permute-start(bf16[256,1280]{1,0:T(8,128)(2,1)S(1)} %collective-permute-done.one), channel_id=1, source_target_pairs={{1,0},{2,3},{5,4},{6,7},{9,8},{10,11},{13,12},{14,15},{17,16},{18,... | collective-permute-start | bytes 1966088 | tf_op jit(solution)/shard_map/ppermute | solution.py:24
  23.3 31.0 %collective-permute-start.2 = (bf16[1024,256]{1,0:T(8,128)(2,1)}, bf16[1024,256]{1,0:T(8,128)(2,1)S(1)}, u32[]{:S(2)}, u32[]{:S(2)}) collective-permute-start(bf16[1024,256]{1,0:T(8,128)(2,1)} %bitcast.18), channel_id=1, source_target_pairs={{0,4},{4,0},{1,5},{5,1},{2,6},{6,2},{3,7},{7,3},{8,12},{12,8},{9,1... | collective-permute-start | bytes 1572872 | tf_op jit(solution)/shard_map/ppermute | solution.py:24
  39.7 0.7 copy-start
  51.2 3.1 %copy-start.4 = (bf16[1,1024,1,256]{3,1,2,0:T(8,128)(2,1)S(1)}, bf16[1,1024,1,256]{3,1,2,0:T(8,128)(2,1)}, u32[]{:S(2)}) copy-start(bf16[1,1024,1,256]{3,1,2,0:T(8,128)(2,1)} %param.14) | copy-start | bytes 1572868
  52.7 5.5 %collective-permute-start.6 = (bf16[256,256]{1,0:T(8,128)(2,1)S(1)}, bf16[256,256]{1,0:T(8,128)(2,1)S(1)}, u32[]{:S(2)}, u32[]{:S(2)}) collective-permute-start(bf16[256,256]{1,0:T(8,128)(2,1)S(1)} %get-tuple-element.26.refs_1_), channel_id=1, source_target_pairs={{0,4},{4,0},{1,5},{5,1},{2,6},{6,2},{3,7},{7,3},{8,12},{12,8},{9,1... | collective-permute-start | bytes 393224 | tf_op jit(solution)/shard_map/ppermute | solution.py:24
  54.6 15.0 %collective-permute-start.7 = (bf16[256,1280]{1,0:T(8,128)(2,1)}, bf16[256,1280]{1,0:T(8,128)(2,1)S(1)}, u32[]{:S(2)}, u32[]{:S(2)}) collective-permute-start(bf16[256,1280]{1,0:T(8,128)(2,1)} %bitcast.2.own), channel_id=1, source_target_pairs={{0,8},{1,9},{2,10},{3,11},{8,16},{9,17},{10,18},{11,19},{16,24},{1... | collective-permute-start | bytes 1966088 | tf_op jit(solution)/shard_map/ppermute | solution.py:24
  54.7 3.5 %copy-start.1 = (s32[1,4]{1,0:T(1,128)S(1)}, s32[1,4]{1,0:T(1,128)}, u32[]{:S(2)}) copy-start(s32[1,4]{1,0:T(1,128)} %row_lengths.1) | copy-start | bytes 52
  54.7 3.5 %copy-start.2 = (s32[1,4]{1,0:T(1,128)S(1)}, s32[1,4]{1,0:T(1,128)}, u32[]{:S(2)}) copy-start(s32[1,4]{1,0:T(1,128)} %cache_lengths.1) | copy-start | bytes 52
  54.7 3.5 %copy-start.3 = (s32[1,4,1]{1,2,0:T(1,128)S(1)}, s32[1,4,1]{1,2,0:T(1,128)}, u32[]{:S(2)}) copy-start(s32[1,4,1]{1,2,0:T(1,128)} %param.17) | copy-start | bytes 52
  66.6 15.7 %collective-permute-start.10 = (bf16[256,1280]{1,0:T(8,128)(2,1)S(1)}, bf16[256,1280]{1,0:T(8,128)(2,1)S(1)}, u32[]{:S(2)}, u32[]{:S(2)}) collective-permute-start(bf16[256,1280]{1,0:T(8,128)(2,1)S(1)} %get-tuple-element.36), channel_id=1, source_target_pairs={{0,1},{3,2},{4,5},{7,6},{8,9},{11,10},{12,13},{15,14},{16,17},{19,... | collective-permute-start | bytes 1966088 | tf_op jit(solution)/shard_map/ppermute | solution.py:24
  68.7 19.0 %collective-permute-start.12 = (bf16[256,1280]{1,0:T(8,128)(2,1)S(1)}, bf16[256,1280]{1,0:T(8,128)(2,1)S(1)}, u32[]{:S(2)}, u32[]{:S(2)}) collective-permute-start(bf16[256,1280]{1,0:T(8,128)(2,1)S(1)} %get-tuple-element.36), channel_id=1, source_target_pairs={{1,10},{2,9},{9,18},{10,17},{17,26},{18,25},{25,2},{26,1},{5,14},{... | collective-permute-start | bytes 1966088 | tf_op jit(solution)/shard_map/ppermute | solution.py:24
  74.3 13.5 %collective-permute-start.8 = (bf16[256,1280]{1,0:T(8,128)(2,1)S(1)}, bf16[256,1280]{1,0:T(8,128)(2,1)S(1)}, u32[]{:S(2)}, u32[]{:S(2)}) collective-permute-start(bf16[256,1280]{1,0:T(8,128)(2,1)S(1)} %get-tuple-element.33), channel_id=1, source_target_pairs={{0,8},{1,9},{2,10},{3,11},{8,16},{9,17},{10,18},{11,19},{16,24},{1... | collective-permute-start | bytes 1966088 | tf_op jit(solution)/shard_map/ppermute | solution.py:24
  76.5 19.9 %collective-permute-start.9 = (bf16[256,1280]{1,0:T(8,128)(2,1)S(1)}, bf16[256,1280]{1,0:T(8,128)(2,1)S(1)}, u32[]{:S(2)}, u32[]{:S(2)}) collective-permute-start(bf16[256,1280]{1,0:T(8,128)(2,1)S(1)} %get-tuple-element.34), channel_id=1, source_target_pairs={{0,10},{3,9},{1,8},{2,11},{8,18},{11,17},{9,16},{10,19},{16,26},{1... | collective-permute-start | bytes 1966088 | tf_op jit(solution)/shard_map/ppermute | solution.py:24
  82.4 32.6 %collective-permute-start.11 = (bf16[256,1280]{1,0:T(8,128)(2,1)S(1)}, bf16[256,1280]{1,0:T(8,128)(2,1)S(1)}, u32[]{:S(2)}, u32[]{:S(2)}) collective-permute-start(bf16[256,1280]{1,0:T(8,128)(2,1)S(1)} %add_convert_fusion.1), channel_id=1, source_target_pairs={{0,9},{3,10},{1,11},{2,8},{8,17},{11,18},{9,19},{10,16},{16,25},{1... | collective-permute-start | bytes 1966088 | tf_op jit(solution)/shard_map/ppermute | solution.py:24

commit v4 on v3

--- a/solution.py
+++ b/solution.py
@@ -16,7 +16,7 @@
 SCORE_BYTES = 13 * MIB
 PARTS = 4
 WEIGHT_CUTS = 4
-CACHE_TILE = 640
+CACHE_TILE = 768
 NEW_TILE = 512
 
 
@@ -458,8 +458,8 @@
     rest = swap(square, "tensor", xor_pairs(splits, 3))
     one, rest, late = lax.optimization_barrier((one, rest, own))
     two = swap(late, "tensor", [(0, 1), (3, 2), (1, 3), (2, 0)])
+    cross = swap(late, "tensor", inner_pairs)
     relayed = swap(one, "tensor", [(1, 0), (2, 3)])
-    cross = swap(late, "tensor", inner_pairs)
     cache = after(cache_kv.reshape(cache_rows, 2 * HEAD_SIZE), rest)
     if pair:
         other = swap(cache, "dp", pair)
@@ -487,11 +487,13 @@
     from_outer = swap(third, "tensor", [(0, 1), (3, 2)])
     from_cross = onwards(third, inner_pairs)
     attended, home = lax.optimization_barrier((attended, home))
+    from_cross, from_outer = lax.optimization_barrier((from_cross, from_outer))
     first, second, same = out_projection(attended, wo)
     from_one = onwards(first, [(0, 2), (3, 1), (1, 0), (2, 3)])
-    from_same = onwards(same, xor_pairs(splits, 0))
     summed = (second.astype(jnp.float32) + from_outer.astype(jnp.float32)).astype(jnp.bfloat16)
     from_two = onwards(summed, [(0, 1), (3, 2), (1, 3), (2, 0)])
+    from_one, same = lax.optimization_barrier((from_one, same))
+    from_same = onwards(same, xor_pairs(splits, 0))
     total = from_same.astype(jnp.float32)
     for block in (from_one, from_two, from_cross):
         total = total + block.astype(jnp.float32)

time: 118 us -> 120 us (1.017); the launches traced: 116 us -> 120 us
  starting transfers between devices: 23.2 us -> 35.3 us
  waiting for transfers between devices: 63.1 us -> 52.7 us
  Pallas kernels: 25.4 us -> 26.9 us
    ppermute x13, starting transfers between devices: 23.2 us -> 35.3 us  [swap(): return lax.ppermute(block, axis, pairs)]
    ppermute x13, waiting for transfers between devices: 63.1 us -> 52.7 us  [swap(): return lax.ppermute(block, axis, pairs)]
    pallas_call x5, Pallas kernels: 25.4 us -> 26.9 us  [resident(): pl.pallas_call(kernel, in_specs=spaces, out_specs=[pl.BlockSpec(memory_sp...]
  transfers between devices with their start and end apart: 13 -> 13, of which waited for: 8 -> 7; matrix products, arithmetic and copies ran while one was open for 2% -> 2% of each run, Pallas kernels for 22% -> 23%
where the time goes in v4:
time: 120 us
  waiting for transfers between devices  52.7 us (44%)
  starting transfers between devices  35.3 us (29%)
  Pallas kernels  26.9 us (22%)
  other arithmetic  3.05 us (3%)
    ppermute x13, waiting for transfers between devices, swap(): return lax.ppermute(block, axis, pairs)  52.7 us
    ppermute x13, starting transfers between devices, swap(): return lax.ppermute(block, axis, pairs)  35.3 us
    pallas_call x5, Pallas kernels, resident(): pl.pallas_call(kernel, in_specs=spaces, out_specs=[pl.BlockSpec(memory_sp...  26.9 us
  transfers between devices with their start and end apart: 13, of which 7 were waited for; matrix products, arithmetic and copies ran while one was open for 2% of the time, Pallas kernels for 23%

profile of v4, /device:TPU:0, one launch (start us, length us, event | category | flops | bytes accessed | tf_op | source)
XLA Modules:
  0.0 119.6 jit_solution(6252619200134387691)
XLA Ops:
  0.6 4.1 %collective-permute-start = (bf16[256,1280]{1,0:T(8,128)(2,1)}, bf16[256,1280]{1,0:T(8,128)(2,1)S(1)}, u32[]{:S(2)}, u32[]{:S(2)}) collective-permute-start(bf16[256,1280]{1,0:T(8,128)(2,1)} %bitcast.2.own), channel_id=1, source_target_pairs={{0,2},{3,1},{1,0},{2,3},{4,6},{7,5},{5,4},{6,7},{8,10},{11,9},{9,8... | collective-permute-start | bytes 1966088 | tf_op jit(solution)/shard_map/ppermute | solution.py:24
  4.7 1.3 %multiply_reduce_fusion = f32[256]{0:T(256)S(1)} fusion(bf16[1,256,1280]{2,1,0:T(8,128)(2,1)} %param.9), kind=kLoop, calls=%fused_computation.2 | loop fusion | flops 982784 | bytes 656384 | tf_op jit(solution)/shard_map/reduce_sum | solution.py:457
  6.0 1.4 %collective-permute-start.1 = (f32[1,256]{1,0:T(1,128)S(1)}, f32[1,256]{1,0:T(1,128)S(1)}, u32[]{:S(2)}, u32[]{:S(2)}) collective-permute-start(f32[1,256]{1,0:T(1,128)S(1)} %bitcast.21), channel_id=1, source_target_pairs={{0,3},{1,2},{2,1},{3,0},{4,7},{5,6},{6,5},{7,4},{8,11},{9,10},{10,... | collective-permute-start | bytes 3080 | tf_op jit(solution)/shard_map/ppermute | solution.py:24
  7.5 13.3 %collective-permute-done.1 = f32[1,256]{1,0:T(1,128)S(1)} collective-permute-done((f32[1,256]{1,0:T(1,128)S(1)}, f32[1,256]{1,0:T(1,128)S(1)}, u32[]{:S(2)}, u32[]{:S(2)}) %collective-permute-start.1) | collective-permute-done | bytes 1056 | tf_op jit(solution)/shard_map/ppermute | solution.py:24
  22.0 1.3 %collective-permute-start.4 = (bf16[256,1280]{1,0:T(8,128)(2,1)S(1)}, bf16[256,1280]{1,0:T(8,128)(2,1)S(1)}, u32[]{:S(2)}, u32[]{:S(2)}) collective-permute-start(bf16[256,1280]{1,0:T(8,128)(2,1)S(1)} %collective-permute-done.one), channel_id=1, source_target_pairs={{1,0},{2,3},{5,4},{6,7},{9,8},{10,11},{13,12},{14,15},{17,16},{18,... | collective-permute-start | bytes 1966088 | tf_op jit(solution)/shard_map/ppermute | solution.py:24
  23.3 1.6 %collective-permute-start.2 = (bf16[1024,256]{1,0:T(8,128)(2,1)}, bf16[1024,256]{1,0:T(8,128)(2,1)S(1)}, u32[]{:S(2)}, u32[]{:S(2)}) collective-permute-start(bf16[1024,256]{1,0:T(8,128)(2,1)} %bitcast.18), channel_id=1, source_target_pairs={{0,4},{4,0},{1,5},{5,1},{2,6},{6,2},{3,7},{7,3},{8,12},{12,8},{9,1... | collective-permute-start | bytes 1572872 | tf_op jit(solution)/shard_map/ppermute | solution.py:24
  24.9 14.7 %collective-permute-done.5.two = bf16[256,1280]{1,0:T(8,128)(2,1)S(1)} collective-permute-done((bf16[256,1280]{1,0:T(8,128)(2,1)}, bf16[256,1280]{1,0:T(8,128)(2,1)S(1)}, u32[]{:S(2)}, u32[]{:S(2)}) %collective-permute-start.5) | collective-permute-done | bytes 655392 | tf_op jit(solution)/shard_map/ppermute | solution.py:24
  40.4 8.2 %early_projection.1 = (f32[256,1024]{1,0:T(8,128)S(1)}, f32[256,256]{1,0:T(8,128)S(1)}, f32[256,128]{1,0:T(8,128)S(1)}) custom-call(bf16[256,1280]{1,0:T(8,128)(2,1)} %bitcast.2.own, bf16[256,1280]{1,0:T(8,128)(2,1)S(1)} %collective-permute-done.one, bf16[256,1280]{1,0:T(8,128)(2,1)S(1)} %collective-permute-done.5.two, ...), custom_call_target="tpu_custom_call" | custom-call | tf_op jit(solution)/shard_map/early_projection/pallas_call | solution.py:47
  48.7 2.6 %collective-permute-done.4.relayed = bf16[256,1280]{1,0:T(8,128)(2,1)S(1)} collective-permute-done((bf16[256,1280]{1,0:T(8,128)(2,1)S(1)}, bf16[256,1280]{1,0:T(8,128)(2,1)S(1)}, u32[]{:S(2)}, u32[]{:S(2)}) %collective-permute-start.4) | collective-permute-done | bytes 655392 | tf_op jit(solution)/shard_map/ppermute | solution.py:24
  51.2 1.5 %last_kv.1 = (bf16[256,256]{1,0:T(8,128)(2,1)S(1)}, bf16[256,1280]{1,0:T(8,128)(2,1)S(1)}) custom-call(bf16[256,1280]{1,0:T(8,128)(2,1)S(1)} %collective-permute-done.3.cross, bf16[256,1280]{1,0:T(8,128)(2,1)S(1)} %collective-permute-done.4.relayed, f32[256,128]{1,0:T(8,128)S(1)} %get-tuple-element.28.factor_ref, bf16[1,5120]{1,0:T(2,128)(2,1)S(1)} %copy-done, ...), custom_call_target="tpu_custom_call" | custom-call | tf_op jit(solution)/shard_map/last_kv/pallas_call | solution.py:47
  52.7 1.6 %collective-permute-start.6 = (bf16[256,256]{1,0:T(8,128)(2,1)S(1)}, bf16[256,256]{1,0:T(8,128)(2,1)S(1)}, u32[]{:S(2)}, u32[]{:S(2)}) collective-permute-start(bf16[256,256]{1,0:T(8,128)(2,1)S(1)} %get-tuple-element.30.refs_1_), channel_id=1, source_target_pairs={{0,4},{4,0},{1,5},{5,1},{2,6},{6,2},{3,7},{7,3},{8,12},{12,8},{9,1... | collective-permute-start | bytes 393224 | tf_op jit(solution)/shard_map/ppermute | solution.py:24
  54.7 2.6 %last_q.1.refs_3_ = bf16[256,1024]{1,0:T(8,128)(2,1)S(1)} custom-call(bf16[256,1280]{1,0:T(8,128)(2,1)S(1)} %get-tuple-element.31.normed, f32[256,1024]{1,0:T(8,128)S(1)} %get-tuple-element.32.acc_ref, bf16[5120,1024]{1,0:T(8,128)(2,1)} %bitcast.13), custom_call_target="tpu_custom_call" | custom-call | tf_op jit(solution)/shard_map/last_q/pallas_call | solution.py:47
  57.3 0.9 collective-permute-done.6.refs_2_
  58.2 10.0 %attention.1 = (bf16[256,1024]{1,0:T(8,128)(2,1)S(1)}, bf16[256,1280]{1,0:T(8,128)(2,1)S(1)}, f32[1,1]{1,0:T(1,128)}) custom-call(s32[1,4]{1,0:T(1,128)S(1)} %copy-done.1, s32[1,4]{1,0:T(1,128)S(1)} %copy-done.2, s32[1,4]{1,0:T(1,128)S(1)} %bitcast.11, bf16[2048,256]{1,0:T(8,128)(2,1)S(1)} %maximum_select_fusion.refs_0_, ...), custom_call_target="tpu_custom_call" | custom-call | bytes 10485760 | tf_op jit(solution)/shard_map/attention/pallas_call | solution.py:47
  68.2 2.1 %collective-permute-start.11 = (bf16[256,1280]{1,0:T(8,128)(2,1)S(1)}, bf16[256,1280]{1,0:T(8,128)(2,1)S(1)}, u32[]{:S(2)}, u32[]{:S(2)}) collective-permute-start(bf16[256,1280]{1,0:T(8,128)(2,1)S(1)} %get-tuple-element.42), channel_id=1, source_target_pairs={{0,1},{3,2},{4,5},{7,6},{8,9},{11,10},{12,13},{15,14},{16,17},{19,... | collective-permute-start | bytes 1966088 | tf_op jit(solution)/shard_map/ppermute | solution.py:24
  70.3 0.9 collective-permute-start.10
  71.2 4.6 %out_projection.1 = (bf16[256,1280]{1,0:T(8,128)(2,1)S(1)}, bf16[256,1280]{1,0:T(8,128)(2,1)S(1)}, bf16[256,1280]{1,0:T(8,128)(2,1)S(1)}) custom-call(bf16[256,1024]{1,0:T(8,128)(2,1)S(1)} %get-tuple-element.36.a_ref, bf16[1024,5120]{1,0:T(8,128)(2,1)} %bitcast.15), custom_call_target="tpu_custom_call" | custom-call | tf_op jit(solution)/shard_map/out_projection/pallas_call | solution.py:47
  75.9 2.7 %collective-permute-start.8 = (bf16[256,1280]{1,0:T(8,128)(2,1)S(1)}, bf16[256,1280]{1,0:T(8,128)(2,1)S(1)}, u32[]{:S(2)}, u32[]{:S(2)}) collective-permute-start(bf16[256,1280]{1,0:T(8,128)(2,1)S(1)} %get-tuple-element.37), channel_id=1, source_target_pairs={{0,10},{3,9},{1,8},{2,11},{8,18},{11,17},{9,16},{10,19},{16,26},{1... | collective-permute-start | bytes 1966088 | tf_op jit(solution)/shard_map/ppermute | solution.py:24
  78.6 6.9 %collective-permute-done.11 = bf16[256,1280]{1,0:T(8,128)(2,1)S(1)} collective-permute-done((bf16[256,1280]{1,0:T(8,128)(2,1)S(1)}, bf16[256,1280]{1,0:T(8,128)(2,1)S(1)}, u32[]{:S(2)}, u32[]{:S(2)}) %collective-permute-start.11) | collective-permute-done | bytes 655392 | tf_op jit(solution)/shard_map/ppermute | solution.py:24
  85.6 16.4 %collective-permute-start.12 = (bf16[256,1280]{1,0:T(8,128)(2,1)S(1)}, bf16[256,1280]{1,0:T(8,128)(2,1)S(1)}, u32[]{:S(2)}, u32[]{:S(2)}) collective-permute-start(bf16[256,1280]{1,0:T(8,128)(2,1)S(1)} %add_convert_fusion.1), channel_id=1, source_target_pairs={{0,9},{3,10},{1,11},{2,8},{8,17},{11,18},{9,19},{10,16},{16,25},{1... | collective-permute-start | bytes 1966088 | tf_op jit(solution)/shard_map/ppermute | solution.py:24
  102.0 2.0 %collective-permute-start.9 = (bf16[256,1280]{1,0:T(8,128)(2,1)S(1)}, bf16[256,1280]{1,0:T(8,128)(2,1)S(1)}, u32[]{:S(2)}, u32[]{:S(2)}) collective-permute-start(bf16[256,1280]{1,0:T(8,128)(2,1)S(1)} %get-tuple-element.39), channel_id=1, source_target_pairs={{0,8},{1,9},{2,10},{3,11},{8,16},{9,17},{10,18},{11,19},{16,24},{1... | collective-permute-start | bytes 1966088 | tf_op jit(solution)/shard_map/ppermute | solution.py:24
  104.0 12.6 %collective-permute-done.12 = bf16[256,1280]{1,0:T(8,128)(2,1)S(1)} collective-permute-done((bf16[256,1280]{1,0:T(8,128)(2,1)S(1)}, bf16[256,1280]{1,0:T(8,128)(2,1)S(1)}, u32[]{:S(2)}, u32[]{:S(2)}) %collective-permute-start.12) | collective-permute-done | bytes 655392 | tf_op jit(solution)/shard_map/ppermute | solution.py:24
  116.6 1.7 %collective-permute-done.9 = bf16[256,1280]{1,0:T(8,128)(2,1)S(1)} collective-permute-done((bf16[256,1280]{1,0:T(8,128)(2,1)S(1)}, bf16[256,1280]{1,0:T(8,128)(2,1)S(1)}, u32[]{:S(2)}, u32[]{:S(2)}) %collective-permute-start.9) | collective-permute-done | bytes 655392 | tf_op jit(solution)/shard_map/ppermute | solution.py:24
  118.3 1.3 %fusion = bf16[1,256,1280]{2,1,0:T(8,128)(2,1)} fusion(bf16[256,1280]{1,0:T(8,128)(2,1)S(1)} %collective-permute-done.10, bf16[256,1280]{1,0:T(8,128)(2,1)S(1)} %collective-permute-done.12, bf16[256,1280]{1,0:T(8,128)(2,1)S(1)} %collective-permute-done.8, bf16[256,1280]{1,0:T(8,128)(2,1)S(1)} %collective-permute-done.9, ...), kind=kLoop, calls=%fused_computation.4 | loop fusion | flops 3276800 | bytes 3932160 | tf_op jit(solution)/shard_map/broadcast_in_dim | solution.py:500
  (22 shorter events, 2.5 us)
Async XLA Ops:
  0.6 20.1 %collective-permute-start = (bf16[256,1280]{1,0:T(8,128)(2,1)}, bf16[256,1280]{1,0:T(8,128)(2,1)S(1)}, u32[]{:S(2)}, u32[]{:S(2)}) collective-permute-start(bf16[256,1280]{1,0:T(8,128)(2,1)} %bitcast.2.own), channel_id=1, source_target_pairs={{0,2},{3,1},{1,0},{2,3},{4,6},{7,5},{5,4},{6,7},{8,10},{11,9},{9,8... | collective-permute-start | bytes 1966088 | tf_op jit(solution)/shard_map/ppermute | solution.py:24
  6.0 14.7 %collective-permute-start.1 = (f32[1,256]{1,0:T(1,128)S(1)}, f32[1,256]{1,0:T(1,128)S(1)}, u32[]{:S(2)}, u32[]{:S(2)}) collective-permute-start(f32[1,256]{1,0:T(1,128)S(1)} %bitcast.21), channel_id=1, source_target_pairs={{0,3},{1,2},{2,1},{3,0},{4,7},{5,6},{6,5},{7,4},{8,11},{9,10},{10,... | collective-permute-start | bytes 3080 | tf_op jit(solution)/shard_map/ppermute | solution.py:24
  20.8 18.8 %collective-permute-start.5 = (bf16[256,1280]{1,0:T(8,128)(2,1)}, bf16[256,1280]{1,0:T(8,128)(2,1)S(1)}, u32[]{:S(2)}, u32[]{:S(2)}) collective-permute-start(bf16[256,1280]{1,0:T(8,128)(2,1)} %bitcast.2.own), channel_id=1, source_target_pairs={{0,1},{3,2},{1,3},{2,0},{4,5},{7,6},{5,7},{6,4},{8,9},{11,10},{9,1... | collective-permute-start | bytes 1966088 | tf_op jit(solution)/shard_map/ppermute | solution.py:24
  21.3 27.3 %collective-permute-start.3 = (bf16[256,1280]{1,0:T(8,128)(2,1)}, bf16[256,1280]{1,0:T(8,128)(2,1)S(1)}, u32[]{:S(2)}, u32[]{:S(2)}) collective-permute-start(bf16[256,1280]{1,0:T(8,128)(2,1)} %bitcast.2.own), channel_id=1, source_target_pairs={{1,2},{2,1},{5,6},{6,5},{9,10},{10,9},{13,14},{14,13},{17,18},{18,... | collective-permute-start | bytes 1966088 | tf_op jit(solution)/shard_map/ppermute | solution.py:24
  22.0 29.2 %collective-permute-start.4 = (bf16[256,1280]{1,0:T(8,128)(2,1)S(1)}, bf16[256,1280]{1,0:T(8,128)(2,1)S(1)}, u32[]{:S(2)}, u32[]{:S(2)}) collective-permute-start(bf16[256,1280]{1,0:T(8,128)(2,1)S(1)} %collective-permute-done.one), channel_id=1, source_target_pairs={{1,0},{2,3},{5,4},{6,7},{9,8},{10,11},{13,12},{14,15},{17,16},{18,... | collective-permute-start | bytes 1966088 | tf_op jit(solution)/shard_map/ppermute | solution.py:24
  23.3 31.0 %collective-permute-start.2 = (bf16[1024,256]{1,0:T(8,128)(2,1)}, bf16[1024,256]{1,0:T(8,128)(2,1)S(1)}, u32[]{:S(2)}, u32[]{:S(2)}) collective-permute-start(bf16[1024,256]{1,0:T(8,128)(2,1)} %bitcast.18), channel_id=1, source_target_pairs={{0,4},{4,0},{1,5},{5,1},{2,6},{6,2},{3,7},{7,3},{8,12},{12,8},{9,1... | collective-permute-start | bytes 1572872 | tf_op jit(solution)/shard_map/ppermute | solution.py:24
  39.7 0.7 copy-start
  51.2 3.1 %copy-start.4 = (bf16[1,1024,1,256]{3,1,2,0:T(8,128)(2,1)S(1)}, bf16[1,1024,1,256]{3,1,2,0:T(8,128)(2,1)}, u32[]{:S(2)}) copy-start(bf16[1,1024,1,256]{3,1,2,0:T(8,128)(2,1)} %param.14) | copy-start | bytes 1572868
  52.7 5.5 %collective-permute-start.6 = (bf16[256,256]{1,0:T(8,128)(2,1)S(1)}, bf16[256,256]{1,0:T(8,128)(2,1)S(1)}, u32[]{:S(2)}, u32[]{:S(2)}) collective-permute-start(bf16[256,256]{1,0:T(8,128)(2,1)S(1)} %get-tuple-element.30.refs_1_), channel_id=1, source_target_pairs={{0,4},{4,0},{1,5},{5,1},{2,6},{6,2},{3,7},{7,3},{8,12},{12,8},{9,1... | collective-permute-start | bytes 393224 | tf_op jit(solution)/shard_map/ppermute | solution.py:24
  54.3 16.9 %collective-permute-start.7 = (bf16[256,1280]{1,0:T(8,128)(2,1)}, bf16[256,1280]{1,0:T(8,128)(2,1)S(1)}, u32[]{:S(2)}, u32[]{:S(2)}) collective-permute-start(bf16[256,1280]{1,0:T(8,128)(2,1)} %bitcast.2.own), channel_id=1, source_target_pairs={{0,8},{1,9},{2,10},{3,11},{8,16},{9,17},{10,18},{11,19},{16,24},{1... | collective-permute-start | bytes 1966088 | tf_op jit(solution)/shard_map/ppermute | solution.py:24
  54.6 3.6 %copy-start.1 = (s32[1,4]{1,0:T(1,128)S(1)}, s32[1,4]{1,0:T(1,128)}, u32[]{:S(2)}) copy-start(s32[1,4]{1,0:T(1,128)} %row_lengths.1) | copy-start | bytes 52
  54.6 3.6 %copy-start.2 = (s32[1,4]{1,0:T(1,128)S(1)}, s32[1,4]{1,0:T(1,128)}, u32[]{:S(2)}) copy-start(s32[1,4]{1,0:T(1,128)} %cache_lengths.1) | copy-start | bytes 52
  54.6 3.6 %copy-start.3 = (s32[1,4,1]{1,2,0:T(1,128)S(1)}, s32[1,4,1]{1,2,0:T(1,128)}, u32[]{:S(2)}) copy-start(s32[1,4,1]{1,2,0:T(1,128)} %param.17) | copy-start | bytes 52
  68.2 17.2 %collective-permute-start.11 = (bf16[256,1280]{1,0:T(8,128)(2,1)S(1)}, bf16[256,1280]{1,0:T(8,128)(2,1)S(1)}, u32[]{:S(2)}, u32[]{:S(2)}) collective-permute-start(bf16[256,1280]{1,0:T(8,128)(2,1)S(1)} %get-tuple-element.42), channel_id=1, source_target_pairs={{0,1},{3,2},{4,5},{7,6},{8,9},{11,10},{12,13},{15,14},{16,17},{19,... | collective-permute-start | bytes 1966088 | tf_op jit(solution)/shard_map/ppermute | solution.py:24
  70.3 15.1 %collective-permute-start.10 = (bf16[256,1280]{1,0:T(8,128)(2,1)S(1)}, bf16[256,1280]{1,0:T(8,128)(2,1)S(1)}, u32[]{:S(2)}, u32[]{:S(2)}) collective-permute-start(bf16[256,1280]{1,0:T(8,128)(2,1)S(1)} %get-tuple-element.42), channel_id=1, source_target_pairs={{1,10},{2,9},{9,18},{10,17},{17,26},{18,25},{25,2},{26,1},{5,14},{... | collective-permute-start | bytes 1966088 | tf_op jit(solution)/shard_map/ppermute | solution.py:24
  75.9 26.1 %collective-permute-start.8 = (bf16[256,1280]{1,0:T(8,128)(2,1)S(1)}, bf16[256,1280]{1,0:T(8,128)(2,1)S(1)}, u32[]{:S(2)}, u32[]{:S(2)}) collective-permute-start(bf16[256,1280]{1,0:T(8,128)(2,1)S(1)} %get-tuple-element.37), channel_id=1, source_target_pairs={{0,10},{3,9},{1,8},{2,11},{8,18},{11,17},{9,16},{10,19},{16,26},{1... | collective-permute-start | bytes 1966088 | tf_op jit(solution)/shard_map/ppermute | solution.py:24
  85.6 31.0 %collective-permute-start.12 = (bf16[256,1280]{1,0:T(8,128)(2,1)S(1)}, bf16[256,1280]{1,0:T(8,128)(2,1)S(1)}, u32[]{:S(2)}, u32[]{:S(2)}) collective-permute-start(bf16[256,1280]{1,0:T(8,128)(2,1)S(1)} %add_convert_fusion.1), channel_id=1, source_target_pairs={{0,9},{3,10},{1,11},{2,8},{8,17},{11,18},{9,19},{10,16},{16,25},{1... | collective-permute-start | bytes 1966088 | tf_op jit(solution)/shard_map/ppermute | solution.py:24
  102.0 16.3 %collective-permute-start.9 = (bf16[256,1280]{1,0:T(8,128)(2,1)S(1)}, bf16[256,1280]{1,0:T(8,128)(2,1)S(1)}, u32[]{:S(2)}, u32[]{:S(2)}) collective-permute-start(bf16[256,1280]{1,0:T(8,128)(2,1)S(1)} %get-tuple-element.39), channel_id=1, source_target_pairs={{0,8},{1,9},{2,10},{3,11},{8,16},{9,17},{10,18},{11,19},{16,24},{1... | collective-permute-start | bytes 1966088 | tf_op jit(solution)/shard_map/ppermute | solution.py:24

commit v5 on v3

--- a/solution.py
+++ b/solution.py
@@ -16,7 +16,7 @@
 SCORE_BYTES = 13 * MIB
 PARTS = 4
 WEIGHT_CUTS = 4
-CACHE_TILE = 640
+CACHE_TILE = 768
 NEW_TILE = 512
 
 
@@ -30,10 +30,6 @@
 
 def after(value, *others):
     return lax.optimization_barrier((value, *others))[0]
-
-
-def in_vmem(x):
-    return pltpu.with_memory_space_constraint(x, pltpu.VMEM)
 
 
 def in_hbm(x):
@@ -48,15 +44,12 @@
         kernel,
         in_specs=spaces,
         out_specs=[pl.BlockSpec(memory_space=pltpu.VMEM)] * len(outs),
-        out_shape=[
-            jax.ShapeDtypeStruct(shape, dtype) if shape == (1, 1) else pltpu.VMEM(shape, dtype)
-            for shape, dtype in outs
-        ],
+        out_shape=[jax.ShapeDtypeStruct(shape, dtype) for shape, dtype in outs],
         scratch_shapes=list(scratch),
         compiler_params=pltpu.CompilerParams(vmem_limit_bytes=limit * MIB),
         cost_estimate=pl.CostEstimate(flops=0, bytes_accessed=moved, transcendentals=0),
         name=name,
-    )(*scalars, *[in_vmem(x) for x in args], *[in_hbm(w) for w in weights])
+    )(*scalars, *args, *[in_hbm(w) for w in weights])
 
 
 def start_copies(copies):
@@ -492,10 +485,11 @@
     from_same = onwards(same, xor_pairs(splits, 0))
     summed = (second.astype(jnp.float32) + from_outer.astype(jnp.float32)).astype(jnp.bfloat16)
     from_two = onwards(summed, [(0, 1), (3, 2), (1, 3), (2, 0)])
-    total = from_same.astype(jnp.float32)
-    for block in (from_one, from_two, from_cross):
+    total = home.astype(jnp.float32)
+    for block in (from_same, from_one, from_cross):
         total = total + block.astype(jnp.float32)
-    handed = (home.astype(jnp.float32) + total).astype(jnp.bfloat16)[None]
+    total = lax.optimization_barrier(total)
+    handed = (total + from_two.astype(jnp.float32)).astype(jnp.bfloat16)[None]
     return handed, blocks_held
 
 

time: 118 us -> 118 us (level); the launches traced: 116 us -> 118 us
  waiting for transfers between devices: 63.1 us -> 66.1 us
    ppermute x13, waiting for transfers between devices: 63.1 us -> 66.1 us  [swap(): return lax.ppermute(block, axis, pairs)]
  transfers between devices with their start and end apart: 13 -> 13, of which waited for: 8 -> 8; matrix products, arithmetic and copies ran while one was open for 2% -> 2% of each run, Pallas kernels for 22% -> 21%
where the time goes in v5:
time: 118 us
  waiting for transfers between devices  66.1 us (56%)
  Pallas kernels  24.4 us (21%)
  starting transfers between devices  22.5 us (19%)
  other arithmetic  3.1 us (3%)
    ppermute x13, waiting for transfers between devices, swap(): return lax.ppermute(block, axis, pairs)  66.1 us
    pallas_call x5, Pallas kernels, resident(): pl.pallas_call(kernel, in_specs=spaces, out_specs=[pl.BlockSpec(memory_sp...  24.4 us
    ppermute x13, starting transfers between devices, swap(): return lax.ppermute(block, axis, pairs)  22.5 us
  transfers between devices with their start and end apart: 13, of which 8 were waited for; matrix products, arithmetic and copies ran while one was open for 2% of the time, Pallas kernels for 21%

profile of v5, /device:TPU:0, one launch (start us, length us, event | category | flops | bytes accessed | tf_op | source)
XLA Modules:
  0.0 117.7 jit_solution(13332952469409002220)
XLA Ops:
  0.6 4.1 %collective-permute-start = (bf16[256,1280]{1,0:T(8,128)(2,1)}, bf16[256,1280]{1,0:T(8,128)(2,1)S(1)}, u32[]{:S(2)}, u32[]{:S(2)}) collective-permute-start(bf16[256,1280]{1,0:T(8,128)(2,1)} %bitcast.2.own), channel_id=1, source_target_pairs={{0,2},{3,1},{1,0},{2,3},{4,6},{7,5},{5,4},{6,7},{8,10},{11,9},{9,8... | collective-permute-start | bytes 1966088 | tf_op jit(solution)/shard_map/ppermute | solution.py:24
  4.7 1.3 %multiply_reduce_fusion = f32[256]{0:T(256)S(1)} fusion(bf16[1,256,1280]{2,1,0:T(8,128)(2,1)} %param.9), kind=kLoop, calls=%fused_computation.3 | loop fusion | flops 982784 | bytes 656384 | tf_op jit(solution)/shard_map/reduce_sum | solution.py:450
  6.0 1.4 %collective-permute-start.1 = (f32[1,256]{1,0:T(1,128)S(1)}, f32[1,256]{1,0:T(1,128)S(1)}, u32[]{:S(2)}, u32[]{:S(2)}) collective-permute-start(f32[1,256]{1,0:T(1,128)S(1)} %bitcast.21), channel_id=1, source_target_pairs={{0,3},{1,2},{2,1},{3,0},{4,7},{5,6},{6,5},{7,4},{8,11},{9,10},{10,... | collective-permute-start | bytes 3080 | tf_op jit(solution)/shard_map/ppermute | solution.py:24
  7.5 13.3 %collective-permute-done.1 = f32[1,256]{1,0:T(1,128)S(1)} collective-permute-done((f32[1,256]{1,0:T(1,128)S(1)}, f32[1,256]{1,0:T(1,128)S(1)}, u32[]{:S(2)}, u32[]{:S(2)}) %collective-permute-start.1) | collective-permute-done | bytes 1056 | tf_op jit(solution)/shard_map/ppermute | solution.py:24
  22.0 1.3 %collective-permute-start.4 = (bf16[256,1280]{1,0:T(8,128)(2,1)S(1)}, bf16[256,1280]{1,0:T(8,128)(2,1)S(1)}, u32[]{:S(2)}, u32[]{:S(2)}) collective-permute-start(bf16[256,1280]{1,0:T(8,128)(2,1)S(1)} %collective-permute-done.one), channel_id=1, source_target_pairs={{1,0},{2,3},{5,4},{6,7},{9,8},{10,11},{13,12},{14,15},{17,16},{18,... | collective-permute-start | bytes 1966088 | tf_op jit(solution)/shard_map/ppermute | solution.py:24
  23.3 1.6 %collective-permute-start.2 = (bf16[1024,256]{1,0:T(8,128)(2,1)}, bf16[1024,256]{1,0:T(8,128)(2,1)S(1)}, u32[]{:S(2)}, u32[]{:S(2)}) collective-permute-start(bf16[1024,256]{1,0:T(8,128)(2,1)} %bitcast.18), channel_id=1, source_target_pairs={{0,4},{4,0},{1,5},{5,1},{2,6},{6,2},{3,7},{7,3},{8,12},{12,8},{9,1... | collective-permute-start | bytes 1572872 | tf_op jit(solution)/shard_map/ppermute | solution.py:24
  24.9 14.7 %collective-permute-done.5.two = bf16[256,1280]{1,0:T(8,128)(2,1)S(1)} collective-permute-done((bf16[256,1280]{1,0:T(8,128)(2,1)}, bf16[256,1280]{1,0:T(8,128)(2,1)S(1)}, u32[]{:S(2)}, u32[]{:S(2)}) %collective-permute-start.5) | collective-permute-done | bytes 655392 | tf_op jit(solution)/shard_map/ppermute | solution.py:24
  40.4 8.2 %early_projection.1 = (f32[256,1024]{1,0:T(8,128)S(1)}, f32[256,256]{1,0:T(8,128)S(1)}, f32[256,128]{1,0:T(8,128)S(1)}) custom-call(bf16[256,1280]{1,0:T(8,128)(2,1)} %bitcast.2.own, bf16[256,1280]{1,0:T(8,128)(2,1)S(1)} %collective-permute-done.one, bf16[256,1280]{1,0:T(8,128)(2,1)S(1)} %collective-permute-done.5.two, ...), custom_call_target="tpu_custom_call" | custom-call | tf_op jit(solution)/shard_map/early_projection/pallas_call | solution.py:43
  48.7 2.6 %collective-permute-done.4.relayed = bf16[256,1280]{1,0:T(8,128)(2,1)S(1)} collective-permute-done((bf16[256,1280]{1,0:T(8,128)(2,1)S(1)}, bf16[256,1280]{1,0:T(8,128)(2,1)S(1)}, u32[]{:S(2)}, u32[]{:S(2)}) %collective-permute-start.4) | collective-permute-done | bytes 655392 | tf_op jit(solution)/shard_map/ppermute | solution.py:24
  51.2 1.5 %last_kv.1 = (bf16[256,256]{1,0:T(8,128)(2,1)S(1)}, bf16[256,1280]{1,0:T(8,128)(2,1)S(1)}) custom-call(bf16[256,1280]{1,0:T(8,128)(2,1)S(1)} %collective-permute-done.3.cross, bf16[256,1280]{1,0:T(8,128)(2,1)S(1)} %collective-permute-done.4.relayed, f32[256,128]{1,0:T(8,128)S(1)} %get-tuple-element.24.factor_ref, bf16[1,5120]{1,0:T(2,128)(2,1)S(1)} %copy-done, ...), custom_call_target="tpu_custom_call" | custom-call | tf_op jit(solution)/shard_map/last_kv/pallas_call | solution.py:43
  52.7 1.6 %collective-permute-start.6 = (bf16[256,256]{1,0:T(8,128)(2,1)S(1)}, bf16[256,256]{1,0:T(8,128)(2,1)S(1)}, u32[]{:S(2)}, u32[]{:S(2)}) collective-permute-start(bf16[256,256]{1,0:T(8,128)(2,1)S(1)} %get-tuple-element.26.refs_1_), channel_id=1, source_target_pairs={{0,4},{4,0},{1,5},{5,1},{2,6},{6,2},{3,7},{7,3},{8,12},{12,8},{9,1... | collective-permute-start | bytes 393224 | tf_op jit(solution)/shard_map/ppermute | solution.py:24
  54.7 2.6 %last_q.1.refs_3_ = bf16[256,1024]{1,0:T(8,128)(2,1)S(1)} custom-call(bf16[256,1280]{1,0:T(8,128)(2,1)S(1)} %get-tuple-element.27.normed, f32[256,1024]{1,0:T(8,128)S(1)} %get-tuple-element.28.acc_ref, bf16[5120,1024]{1,0:T(8,128)(2,1)} %bitcast.13), custom_call_target="tpu_custom_call" | custom-call | tf_op jit(solution)/shard_map/last_q/pallas_call | solution.py:43
  57.3 0.9 collective-permute-done.6.refs_2_
  58.2 7.4 %attention.1 = (bf16[256,1024]{1,0:T(8,128)(2,1)S(1)}, bf16[256,1280]{1,0:T(8,128)(2,1)S(1)}, f32[1,1]{1,0:T(1,128)}) custom-call(s32[1,4]{1,0:T(1,128)S(1)} %copy-done.1, s32[1,4]{1,0:T(1,128)S(1)} %copy-done.2, s32[1,4]{1,0:T(1,128)S(1)} %bitcast.11, bf16[2048,256]{1,0:T(8,128)(2,1)S(1)} %maximum_select_fusion.refs_0_, ...), custom_call_target="tpu_custom_call" | custom-call | bytes 10485760 | tf_op jit(solution)/shard_map/attention/pallas_call | solution.py:43
  65.6 2.1 %collective-permute-start.11 = (bf16[256,1280]{1,0:T(8,128)(2,1)S(1)}, bf16[256,1280]{1,0:T(8,128)(2,1)S(1)}, u32[]{:S(2)}, u32[]{:S(2)}) collective-permute-start(bf16[256,1280]{1,0:T(8,128)(2,1)S(1)} %get-tuple-element.35), channel_id=1, source_target_pairs={{0,1},{3,2},{4,5},{7,6},{8,9},{11,10},{12,13},{15,14},{16,17},{19,... | collective-permute-start | bytes 1966088 | tf_op jit(solution)/shard_map/ppermute | solution.py:24
  68.6 4.7 %out_projection.1 = (bf16[256,1280]{1,0:T(8,128)(2,1)S(1)}, bf16[256,1280]{1,0:T(8,128)(2,1)S(1)}, bf16[256,1280]{1,0:T(8,128)(2,1)S(1)}) custom-call(bf16[256,1024]{1,0:T(8,128)(2,1)S(1)} %get-tuple-element.32.a_ref, bf16[1024,5120]{1,0:T(8,128)(2,1)} %bitcast.15), custom_call_target="tpu_custom_call" | custom-call | tf_op jit(solution)/shard_map/out_projection/pallas_call | solution.py:43
  73.3 0.9 collective-permute-start.8
  74.2 4.7 %collective-permute-start.9 = (bf16[256,1280]{1,0:T(8,128)(2,1)S(1)}, bf16[256,1280]{1,0:T(8,128)(2,1)S(1)}, u32[]{:S(2)}, u32[]{:S(2)}) collective-permute-start(bf16[256,1280]{1,0:T(8,128)(2,1)S(1)} %get-tuple-element.34), channel_id=1, source_target_pairs={{0,10},{3,9},{1,8},{2,11},{8,18},{11,17},{9,16},{10,19},{16,26},{1... | collective-permute-start | bytes 1966088 | tf_op jit(solution)/shard_map/ppermute | solution.py:24
  79.0 3.7 %collective-permute-done.11 = bf16[256,1280]{1,0:T(8,128)(2,1)S(1)} collective-permute-done((bf16[256,1280]{1,0:T(8,128)(2,1)S(1)}, bf16[256,1280]{1,0:T(8,128)(2,1)S(1)}, u32[]{:S(2)}, u32[]{:S(2)}) %collective-permute-start.11) | collective-permute-done | bytes 655392 | tf_op jit(solution)/shard_map/ppermute | solution.py:24
  82.8 2.6 %collective-permute-start.12 = (bf16[256,1280]{1,0:T(8,128)(2,1)S(1)}, bf16[256,1280]{1,0:T(8,128)(2,1)S(1)}, u32[]{:S(2)}, u32[]{:S(2)}) collective-permute-start(bf16[256,1280]{1,0:T(8,128)(2,1)S(1)} %add_convert_fusion.1), channel_id=1, source_target_pairs={{0,9},{3,10},{1,11},{2,8},{8,17},{11,18},{9,19},{10,16},{16,25},{1... | collective-permute-start | bytes 1966088 | tf_op jit(solution)/shard_map/ppermute | solution.py:24
  85.4 6.8 %collective-permute-done.8 = bf16[256,1280]{1,0:T(8,128)(2,1)S(1)} collective-permute-done((bf16[256,1280]{1,0:T(8,128)(2,1)S(1)}, bf16[256,1280]{1,0:T(8,128)(2,1)S(1)}, u32[]{:S(2)}, u32[]{:S(2)}) %collective-permute-start.8) | collective-permute-done | bytes 655392 | tf_op jit(solution)/shard_map/ppermute | solution.py:24
  92.2 4.5 %collective-permute-done.9 = bf16[256,1280]{1,0:T(8,128)(2,1)S(1)} collective-permute-done((bf16[256,1280]{1,0:T(8,128)(2,1)S(1)}, bf16[256,1280]{1,0:T(8,128)(2,1)S(1)}, u32[]{:S(2)}, u32[]{:S(2)}) %collective-permute-start.9) | collective-permute-done | bytes 655392 | tf_op jit(solution)/shard_map/ppermute | solution.py:24
  97.0 19.7 %collective-permute-done.12 = bf16[256,1280]{1,0:T(8,128)(2,1)S(1)} collective-permute-done((bf16[256,1280]{1,0:T(8,128)(2,1)S(1)}, bf16[256,1280]{1,0:T(8,128)(2,1)S(1)}, u32[]{:S(2)}, u32[]{:S(2)}) %collective-permute-start.12) | collective-permute-done | bytes 655392 | tf_op jit(solution)/shard_map/ppermute | solution.py:24
  116.7 1.0 fusion
  (23 shorter events, 3.8 us)
Async XLA Ops:
  0.6 20.1 %collective-permute-start = (bf16[256,1280]{1,0:T(8,128)(2,1)}, bf16[256,1280]{1,0:T(8,128)(2,1)S(1)}, u32[]{:S(2)}, u32[]{:S(2)}) collective-permute-start(bf16[256,1280]{1,0:T(8,128)(2,1)} %bitcast.2.own), channel_id=1, source_target_pairs={{0,2},{3,1},{1,0},{2,3},{4,6},{7,5},{5,4},{6,7},{8,10},{11,9},{9,8... | collective-permute-start | bytes 1966088 | tf_op jit(solution)/shard_map/ppermute | solution.py:24
  6.0 14.7 %collective-permute-start.1 = (f32[1,256]{1,0:T(1,128)S(1)}, f32[1,256]{1,0:T(1,128)S(1)}, u32[]{:S(2)}, u32[]{:S(2)}) collective-permute-start(f32[1,256]{1,0:T(1,128)S(1)} %bitcast.21), channel_id=1, source_target_pairs={{0,3},{1,2},{2,1},{3,0},{4,7},{5,6},{6,5},{7,4},{8,11},{9,10},{10,... | collective-permute-start | bytes 3080 | tf_op jit(solution)/shard_map/ppermute | solution.py:24
  20.8 18.8 %collective-permute-start.5 = (bf16[256,1280]{1,0:T(8,128)(2,1)}, bf16[256,1280]{1,0:T(8,128)(2,1)S(1)}, u32[]{:S(2)}, u32[]{:S(2)}) collective-permute-start(bf16[256,1280]{1,0:T(8,128)(2,1)} %bitcast.2.own), channel_id=1, source_target_pairs={{0,1},{3,2},{1,3},{2,0},{4,5},{7,6},{5,7},{6,4},{8,9},{11,10},{9,1... | collective-permute-start | bytes 1966088 | tf_op jit(solution)/shard_map/ppermute | solution.py:24
  21.3 27.3 %collective-permute-start.3 = (bf16[256,1280]{1,0:T(8,128)(2,1)}, bf16[256,1280]{1,0:T(8,128)(2,1)S(1)}, u32[]{:S(2)}, u32[]{:S(2)}) collective-permute-start(bf16[256,1280]{1,0:T(8,128)(2,1)} %bitcast.2.own), channel_id=1, source_target_pairs={{1,2},{2,1},{5,6},{6,5},{9,10},{10,9},{13,14},{14,13},{17,18},{18,... | collective-permute-start | bytes 1966088 | tf_op jit(solution)/shard_map/ppermute | solution.py:24
  22.0 29.2 %collective-permute-start.4 = (bf16[256,1280]{1,0:T(8,128)(2,1)S(1)}, bf16[256,1280]{1,0:T(8,128)(2,1)S(1)}, u32[]{:S(2)}, u32[]{:S(2)}) collective-permute-start(bf16[256,1280]{1,0:T(8,128)(2,1)S(1)} %collective-permute-done.one), channel_id=1, source_target_pairs={{1,0},{2,3},{5,4},{6,7},{9,8},{10,11},{13,12},{14,15},{17,16},{18,... | collective-permute-start | bytes 1966088 | tf_op jit(solution)/shard_map/ppermute | solution.py:24
  23.3 31.0 %collective-permute-start.2 = (bf16[1024,256]{1,0:T(8,128)(2,1)}, bf16[1024,256]{1,0:T(8,128)(2,1)S(1)}, u32[]{:S(2)}, u32[]{:S(2)}) collective-permute-start(bf16[1024,256]{1,0:T(8,128)(2,1)} %bitcast.18), channel_id=1, source_target_pairs={{0,4},{4,0},{1,5},{5,1},{2,6},{6,2},{3,7},{7,3},{8,12},{12,8},{9,1... | collective-permute-start | bytes 1572872 | tf_op jit(solution)/shard_map/ppermute | solution.py:24
  39.7 0.7 copy-start
  51.2 3.1 %copy-start.4 = (bf16[1,1024,1,256]{3,1,2,0:T(8,128)(2,1)S(1)}, bf16[1,1024,1,256]{3,1,2,0:T(8,128)(2,1)}, u32[]{:S(2)}) copy-start(bf16[1,1024,1,256]{3,1,2,0:T(8,128)(2,1)} %param.14) | copy-start | bytes 1572868
  52.7 5.5 %collective-permute-start.6 = (bf16[256,256]{1,0:T(8,128)(2,1)S(1)}, bf16[256,256]{1,0:T(8,128)(2,1)S(1)}, u32[]{:S(2)}, u32[]{:S(2)}) collective-permute-start(bf16[256,256]{1,0:T(8,128)(2,1)S(1)} %get-tuple-element.26.refs_1_), channel_id=1, source_target_pairs={{0,4},{4,0},{1,5},{5,1},{2,6},{6,2},{3,7},{7,3},{8,12},{12,8},{9,1... | collective-permute-start | bytes 393224 | tf_op jit(solution)/shard_map/ppermute | solution.py:24
  54.3 14.3 %collective-permute-start.7 = (bf16[256,1280]{1,0:T(8,128)(2,1)}, bf16[256,1280]{1,0:T(8,128)(2,1)S(1)}, u32[]{:S(2)}, u32[]{:S(2)}) collective-permute-start(bf16[256,1280]{1,0:T(8,128)(2,1)} %bitcast.2.own), channel_id=1, source_target_pairs={{0,8},{1,9},{2,10},{3,11},{8,16},{9,17},{10,18},{11,19},{16,24},{1... | collective-permute-start | bytes 1966088 | tf_op jit(solution)/shard_map/ppermute | solution.py:24
  54.6 3.6 %copy-start.1 = (s32[1,4]{1,0:T(1,128)S(1)}, s32[1,4]{1,0:T(1,128)}, u32[]{:S(2)}) copy-start(s32[1,4]{1,0:T(1,128)} %row_lengths.1) | copy-start | bytes 52
  54.6 3.6 %copy-start.2 = (s32[1,4]{1,0:T(1,128)S(1)}, s32[1,4]{1,0:T(1,128)}, u32[]{:S(2)}) copy-start(s32[1,4]{1,0:T(1,128)} %cache_lengths.1) | copy-start | bytes 52
  54.6 3.6 %copy-start.3 = (s32[1,4,1]{1,2,0:T(1,128)S(1)}, s32[1,4,1]{1,2,0:T(1,128)}, u32[]{:S(2)}) copy-start(s32[1,4,1]{1,2,0:T(1,128)} %param.17) | copy-start | bytes 52
  65.6 17.0 %collective-permute-start.11 = (bf16[256,1280]{1,0:T(8,128)(2,1)S(1)}, bf16[256,1280]{1,0:T(8,128)(2,1)S(1)}, u32[]{:S(2)}, u32[]{:S(2)}) collective-permute-start(bf16[256,1280]{1,0:T(8,128)(2,1)S(1)} %get-tuple-element.35), channel_id=1, source_target_pairs={{0,1},{3,2},{4,5},{7,6},{8,9},{11,10},{12,13},{15,14},{16,17},{19,... | collective-permute-start | bytes 1966088 | tf_op jit(solution)/shard_map/ppermute | solution.py:24
  67.7 17.7 %collective-permute-start.10 = (bf16[256,1280]{1,0:T(8,128)(2,1)S(1)}, bf16[256,1280]{1,0:T(8,128)(2,1)S(1)}, u32[]{:S(2)}, u32[]{:S(2)}) collective-permute-start(bf16[256,1280]{1,0:T(8,128)(2,1)S(1)} %get-tuple-element.35), channel_id=1, source_target_pairs={{1,10},{2,9},{9,18},{10,17},{17,26},{18,25},{25,2},{26,1},{5,14},{... | collective-permute-start | bytes 1966088 | tf_op jit(solution)/shard_map/ppermute | solution.py:24
  73.3 18.9 %collective-permute-start.8 = (bf16[256,1280]{1,0:T(8,128)(2,1)S(1)}, bf16[256,1280]{1,0:T(8,128)(2,1)S(1)}, u32[]{:S(2)}, u32[]{:S(2)}) collective-permute-start(bf16[256,1280]{1,0:T(8,128)(2,1)S(1)} %get-tuple-element.33), channel_id=1, source_target_pairs={{0,8},{1,9},{2,10},{3,11},{8,16},{9,17},{10,18},{11,19},{16,24},{1... | collective-permute-start | bytes 1966088 | tf_op jit(solution)/shard_map/ppermute | solution.py:24
  74.2 22.5 %collective-permute-start.9 = (bf16[256,1280]{1,0:T(8,128)(2,1)S(1)}, bf16[256,1280]{1,0:T(8,128)(2,1)S(1)}, u32[]{:S(2)}, u32[]{:S(2)}) collective-permute-start(bf16[256,1280]{1,0:T(8,128)(2,1)S(1)} %get-tuple-element.34), channel_id=1, source_target_pairs={{0,10},{3,9},{1,8},{2,11},{8,18},{11,17},{9,16},{10,19},{16,26},{1... | collective-permute-start | bytes 1966088 | tf_op jit(solution)/shard_map/ppermute | solution.py:24
  82.8 33.9 %collective-permute-start.12 = (bf16[256,1280]{1,0:T(8,128)(2,1)S(1)}, bf16[256,1280]{1,0:T(8,128)(2,1)S(1)}, u32[]{:S(2)}, u32[]{:S(2)}) collective-permute-start(bf16[256,1280]{1,0:T(8,128)(2,1)S(1)} %add_convert_fusion.1), channel_id=1, source_target_pairs={{0,9},{3,10},{1,11},{2,8},{8,17},{11,18},{9,19},{10,16},{16,25},{1... | collective-permute-start | bytes 1966088 | tf_op jit(solution)/shard_map/ppermute | solution.py:24

commit v6 on v5

--- a/solution.py
+++ b/solution.py
@@ -482,14 +482,15 @@
     attended, home = lax.optimization_barrier((attended, home))
     first, second, same = out_projection(attended, wo)
     from_one = onwards(first, [(0, 2), (3, 1), (1, 0), (2, 3)])
-    from_same = onwards(same, xor_pairs(splits, 0))
     summed = (second.astype(jnp.float32) + from_outer.astype(jnp.float32)).astype(jnp.bfloat16)
     from_two = onwards(summed, [(0, 1), (3, 2), (1, 3), (2, 0)])
+    same = lax.optimization_barrier((same, summed))[0]
+    from_same = onwards(same, xor_pairs(splits, 0))
     total = home.astype(jnp.float32)
-    for block in (from_same, from_one, from_cross):
+    for block in (from_one, from_cross, from_two):
         total = total + block.astype(jnp.float32)
     total = lax.optimization_barrier(total)
-    handed = (total + from_two.astype(jnp.float32)).astype(jnp.bfloat16)[None]
+    handed = (total + from_same.astype(jnp.float32)).astype(jnp.bfloat16)[None]
     return handed, blocks_held
 
 

time: 118 us -> 119 us (level); the launches traced: 118 us -> 117 us
  waiting for transfers between devices: 66.1 us -> 59.1 us
  starting transfers between devices: 22.5 us -> 28.6 us
    ppermute x13, waiting for transfers between devices: 66.1 us -> 59.1 us  [swap(): return lax.ppermute(block, axis, pairs)]
    ppermute x13, starting transfers between devices: 22.5 us -> 28.6 us  [swap(): return lax.ppermute(block, axis, pairs)]
  transfers between devices with their start and end apart: 13 -> 13, of which waited for: 8 -> 6; matrix products, arithmetic and copies ran while one was open for 2% -> 2% of each run, Pallas kernels for 21% -> 21%
where the time goes in v6:
time: 119 us; the launch traced here: 117 us
  waiting for transfers between devices  59.1 us (50%)
  starting transfers between devices  28.6 us (24%)
  Pallas kernels  24.4 us (21%)
  other arithmetic  3.08 us (3%)
    ppermute x13, waiting for transfers between devices, swap(): return lax.ppermute(block, axis, pairs)  59.1 us
    ppermute x13, starting transfers between devices, swap(): return lax.ppermute(block, axis, pairs)  28.6 us
    pallas_call x5, Pallas kernels, resident(): pl.pallas_call(kernel, in_specs=spaces, out_specs=[pl.BlockSpec(memory_sp...  24.4 us
  transfers between devices with their start and end apart: 13, of which 6 were waited for; matrix products, arithmetic and copies ran while one was open for 2% of the time, Pallas kernels for 21%

profile of v6, /device:TPU:0, one launch (start us, length us, event | category | flops | bytes accessed | tf_op | source)
XLA Modules:
  0.0 116.8 jit_solution(2586883821384439323)
XLA Ops:
  0.6 4.1 %collective-permute-start = (bf16[256,1280]{1,0:T(8,128)(2,1)}, bf16[256,1280]{1,0:T(8,128)(2,1)S(1)}, u32[]{:S(2)}, u32[]{:S(2)}) collective-permute-start(bf16[256,1280]{1,0:T(8,128)(2,1)} %bitcast.2.own), channel_id=1, source_target_pairs={{0,2},{3,1},{1,0},{2,3},{4,6},{7,5},{5,4},{6,7},{8,10},{11,9},{9,8... | collective-permute-start | bytes 1966088 | tf_op jit(solution)/shard_map/ppermute | solution.py:24
  4.7 1.3 %multiply_reduce_fusion = f32[256]{0:T(256)S(1)} fusion(bf16[1,256,1280]{2,1,0:T(8,128)(2,1)} %param.9), kind=kLoop, calls=%fused_computation.3 | loop fusion | flops 982784 | bytes 656384 | tf_op jit(solution)/shard_map/reduce_sum | solution.py:450
  6.0 1.4 %collective-permute-start.1 = (f32[1,256]{1,0:T(1,128)S(1)}, f32[1,256]{1,0:T(1,128)S(1)}, u32[]{:S(2)}, u32[]{:S(2)}) collective-permute-start(f32[1,256]{1,0:T(1,128)S(1)} %bitcast.21), channel_id=1, source_target_pairs={{0,3},{1,2},{2,1},{3,0},{4,7},{5,6},{6,5},{7,4},{8,11},{9,10},{10,... | collective-permute-start | bytes 3080 | tf_op jit(solution)/shard_map/ppermute | solution.py:24
  7.5 13.3 %collective-permute-done.1 = f32[1,256]{1,0:T(1,128)S(1)} collective-permute-done((f32[1,256]{1,0:T(1,128)S(1)}, f32[1,256]{1,0:T(1,128)S(1)}, u32[]{:S(2)}, u32[]{:S(2)}) %collective-permute-start.1) | collective-permute-done | bytes 1056 | tf_op jit(solution)/shard_map/ppermute | solution.py:24
  21.3 0.7 collective-permute-start.3
  22.0 1.3 %collective-permute-start.4 = (bf16[256,1280]{1,0:T(8,128)(2,1)S(1)}, bf16[256,1280]{1,0:T(8,128)(2,1)S(1)}, u32[]{:S(2)}, u32[]{:S(2)}) collective-permute-start(bf16[256,1280]{1,0:T(8,128)(2,1)S(1)} %collective-permute-done.one), channel_id=1, source_target_pairs={{1,0},{2,3},{5,4},{6,7},{9,8},{10,11},{13,12},{14,15},{17,16},{18,... | collective-permute-start | bytes 1966088 | tf_op jit(solution)/shard_map/ppermute | solution.py:24
  23.3 1.6 %collective-permute-start.2 = (bf16[1024,256]{1,0:T(8,128)(2,1)}, bf16[1024,256]{1,0:T(8,128)(2,1)S(1)}, u32[]{:S(2)}, u32[]{:S(2)}) collective-permute-start(bf16[1024,256]{1,0:T(8,128)(2,1)} %bitcast.18), channel_id=1, source_target_pairs={{0,4},{4,0},{1,5},{5,1},{2,6},{6,2},{3,7},{7,3},{8,12},{12,8},{9,1... | collective-permute-start | bytes 1572872 | tf_op jit(solution)/shard_map/ppermute | solution.py:24
  24.9 14.7 %collective-permute-done.5.two = bf16[256,1280]{1,0:T(8,128)(2,1)S(1)} collective-permute-done((bf16[256,1280]{1,0:T(8,128)(2,1)}, bf16[256,1280]{1,0:T(8,128)(2,1)S(1)}, u32[]{:S(2)}, u32[]{:S(2)}) %collective-permute-start.5) | collective-permute-done | bytes 655392 | tf_op jit(solution)/shard_map/ppermute | solution.py:24
  39.7 0.7 copy-done
  40.4 8.2 %early_projection.1 = (f32[256,1024]{1,0:T(8,128)S(1)}, f32[256,256]{1,0:T(8,128)S(1)}, f32[256,128]{1,0:T(8,128)S(1)}) custom-call(bf16[256,1280]{1,0:T(8,128)(2,1)} %bitcast.2.own, bf16[256,1280]{1,0:T(8,128)(2,1)S(1)} %collective-permute-done.one, bf16[256,1280]{1,0:T(8,128)(2,1)S(1)} %collective-permute-done.5.two, ...), custom_call_target="tpu_custom_call" | custom-call | tf_op jit(solution)/shard_map/early_projection/pallas_call | solution.py:43
  48.7 2.6 %collective-permute-done.4.relayed = bf16[256,1280]{1,0:T(8,128)(2,1)S(1)} collective-permute-done((bf16[256,1280]{1,0:T(8,128)(2,1)S(1)}, bf16[256,1280]{1,0:T(8,128)(2,1)S(1)}, u32[]{:S(2)}, u32[]{:S(2)}) %collective-permute-start.4) | collective-permute-done | bytes 655392 | tf_op jit(solution)/shard_map/ppermute | solution.py:24
  51.2 1.5 %last_kv.1 = (bf16[256,256]{1,0:T(8,128)(2,1)S(1)}, bf16[256,1280]{1,0:T(8,128)(2,1)S(1)}) custom-call(bf16[256,1280]{1,0:T(8,128)(2,1)S(1)} %collective-permute-done.3.cross, bf16[256,1280]{1,0:T(8,128)(2,1)S(1)} %collective-permute-done.4.relayed, f32[256,128]{1,0:T(8,128)S(1)} %get-tuple-element.25.factor_ref, bf16[1,5120]{1,0:T(2,128)(2,1)S(1)} %copy-done, ...), custom_call_target="tpu_custom_call" | custom-call | tf_op jit(solution)/shard_map/last_kv/pallas_call | solution.py:43
  52.7 1.6 %collective-permute-start.6 = (bf16[256,256]{1,0:T(8,128)(2,1)S(1)}, bf16[256,256]{1,0:T(8,128)(2,1)S(1)}, u32[]{:S(2)}, u32[]{:S(2)}) collective-permute-start(bf16[256,256]{1,0:T(8,128)(2,1)S(1)} %get-tuple-element.27.refs_1_), channel_id=1, source_target_pairs={{0,4},{4,0},{1,5},{5,1},{2,6},{6,2},{3,7},{7,3},{8,12},{12,8},{9,1... | collective-permute-start | bytes 393224 | tf_op jit(solution)/shard_map/ppermute | solution.py:24
  54.7 2.6 %last_q.1.refs_3_ = bf16[256,1024]{1,0:T(8,128)(2,1)S(1)} custom-call(bf16[256,1280]{1,0:T(8,128)(2,1)S(1)} %get-tuple-element.28.normed, f32[256,1024]{1,0:T(8,128)S(1)} %get-tuple-element.29.acc_ref, bf16[5120,1024]{1,0:T(8,128)(2,1)} %bitcast.13), custom_call_target="tpu_custom_call" | custom-call | tf_op jit(solution)/shard_map/last_q/pallas_call | solution.py:43
  57.4 0.9 collective-permute-done.6.refs_2_
  58.2 7.4 %attention.1 = (bf16[256,1024]{1,0:T(8,128)(2,1)S(1)}, bf16[256,1280]{1,0:T(8,128)(2,1)S(1)}, f32[1,1]{1,0:T(1,128)}) custom-call(s32[1,4]{1,0:T(1,128)S(1)} %copy-done.1, s32[1,4]{1,0:T(1,128)S(1)} %copy-done.2, s32[1,4]{1,0:T(1,128)S(1)} %bitcast.11, bf16[2048,256]{1,0:T(8,128)(2,1)S(1)} %maximum_select_fusion.refs_0_, ...), custom_call_target="tpu_custom_call" | custom-call | bytes 10485760 | tf_op jit(solution)/shard_map/attention/pallas_call | solution.py:43
  65.6 2.1 %collective-permute-start.10 = (bf16[256,1280]{1,0:T(8,128)(2,1)S(1)}, bf16[256,1280]{1,0:T(8,128)(2,1)S(1)}, u32[]{:S(2)}, u32[]{:S(2)}) collective-permute-start(bf16[256,1280]{1,0:T(8,128)(2,1)S(1)} %get-tuple-element.35), channel_id=1, source_target_pairs={{0,1},{3,2},{4,5},{7,6},{8,9},{11,10},{12,13},{15,14},{16,17},{19,... | collective-permute-start | bytes 1966088 | tf_op jit(solution)/shard_map/ppermute | solution.py:24
  67.7 0.9 collective-permute-start.9
  68.6 4.7 %out_projection.1 = (bf16[256,1280]{1,0:T(8,128)(2,1)S(1)}, bf16[256,1280]{1,0:T(8,128)(2,1)S(1)}, bf16[256,1280]{1,0:T(8,128)(2,1)S(1)}) custom-call(bf16[256,1024]{1,0:T(8,128)(2,1)S(1)} %get-tuple-element.33.a_ref, bf16[1024,5120]{1,0:T(8,128)(2,1)} %bitcast.15), custom_call_target="tpu_custom_call" | custom-call | tf_op jit(solution)/shard_map/out_projection/pallas_call | solution.py:43
  73.3 6.3 %collective-permute-start.8 = (bf16[256,1280]{1,0:T(8,128)(2,1)S(1)}, bf16[256,1280]{1,0:T(8,128)(2,1)S(1)}, u32[]{:S(2)}, u32[]{:S(2)}) collective-permute-start(bf16[256,1280]{1,0:T(8,128)(2,1)S(1)} %get-tuple-element.34), channel_id=1, source_target_pairs={{0,10},{3,9},{1,8},{2,11},{8,18},{11,17},{9,16},{10,19},{16,26},{1... | collective-permute-start | bytes 1966088 | tf_op jit(solution)/shard_map/ppermute | solution.py:24
  79.8 7.5 %collective-permute-start.11 = (bf16[256,1280]{1,0:T(8,128)(2,1)S(1)}, bf16[256,1280]{1,0:T(8,128)(2,1)S(1)}, u32[]{:S(2)}, u32[]{:S(2)}) collective-permute-start(bf16[256,1280]{1,0:T(8,128)(2,1)S(1)} %add_convert_fusion.1), channel_id=1, source_target_pairs={{0,9},{3,10},{1,11},{2,8},{8,17},{11,18},{9,19},{10,16},{16,25},{1... | collective-permute-start | bytes 1966088 | tf_op jit(solution)/shard_map/ppermute | solution.py:24
  87.8 7.1 %collective-permute-done.8 = bf16[256,1280]{1,0:T(8,128)(2,1)S(1)} collective-permute-done((bf16[256,1280]{1,0:T(8,128)(2,1)S(1)}, bf16[256,1280]{1,0:T(8,128)(2,1)S(1)}, u32[]{:S(2)}, u32[]{:S(2)}) %collective-permute-start.8) | collective-permute-done | bytes 655392 | tf_op jit(solution)/shard_map/ppermute | solution.py:24
  94.8 20.6 %collective-permute-done.11 = bf16[256,1280]{1,0:T(8,128)(2,1)S(1)} collective-permute-done((bf16[256,1280]{1,0:T(8,128)(2,1)S(1)}, bf16[256,1280]{1,0:T(8,128)(2,1)S(1)}, u32[]{:S(2)}, u32[]{:S(2)}) %collective-permute-start.11) | collective-permute-done | bytes 655392 | tf_op jit(solution)/shard_map/ppermute | solution.py:24
  115.8 1.0 fusion
  (23 shorter events, 2.1 us)
Async XLA Ops:
  0.6 20.1 %collective-permute-start = (bf16[256,1280]{1,0:T(8,128)(2,1)}, bf16[256,1280]{1,0:T(8,128)(2,1)S(1)}, u32[]{:S(2)}, u32[]{:S(2)}) collective-permute-start(bf16[256,1280]{1,0:T(8,128)(2,1)} %bitcast.2.own), channel_id=1, source_target_pairs={{0,2},{3,1},{1,0},{2,3},{4,6},{7,5},{5,4},{6,7},{8,10},{11,9},{9,8... | collective-permute-start | bytes 1966088 | tf_op jit(solution)/shard_map/ppermute | solution.py:24
  6.0 14.7 %collective-permute-start.1 = (f32[1,256]{1,0:T(1,128)S(1)}, f32[1,256]{1,0:T(1,128)S(1)}, u32[]{:S(2)}, u32[]{:S(2)}) collective-permute-start(f32[1,256]{1,0:T(1,128)S(1)} %bitcast.21), channel_id=1, source_target_pairs={{0,3},{1,2},{2,1},{3,0},{4,7},{5,6},{6,5},{7,4},{8,11},{9,10},{10,... | collective-permute-start | bytes 3080 | tf_op jit(solution)/shard_map/ppermute | solution.py:24
  20.8 18.8 %collective-permute-start.5 = (bf16[256,1280]{1,0:T(8,128)(2,1)}, bf16[256,1280]{1,0:T(8,128)(2,1)S(1)}, u32[]{:S(2)}, u32[]{:S(2)}) collective-permute-start(bf16[256,1280]{1,0:T(8,128)(2,1)} %bitcast.2.own), channel_id=1, source_target_pairs={{0,1},{3,2},{1,3},{2,0},{4,5},{7,6},{5,7},{6,4},{8,9},{11,10},{9,1... | collective-permute-start | bytes 1966088 | tf_op jit(solution)/shard_map/ppermute | solution.py:24
  21.3 27.3 %collective-permute-start.3 = (bf16[256,1280]{1,0:T(8,128)(2,1)}, bf16[256,1280]{1,0:T(8,128)(2,1)S(1)}, u32[]{:S(2)}, u32[]{:S(2)}) collective-permute-start(bf16[256,1280]{1,0:T(8,128)(2,1)} %bitcast.2.own), channel_id=1, source_target_pairs={{1,2},{2,1},{5,6},{6,5},{9,10},{10,9},{13,14},{14,13},{17,18},{18,... | collective-permute-start | bytes 1966088 | tf_op jit(solution)/shard_map/ppermute | solution.py:24
  22.0 29.2 %collective-permute-start.4 = (bf16[256,1280]{1,0:T(8,128)(2,1)S(1)}, bf16[256,1280]{1,0:T(8,128)(2,1)S(1)}, u32[]{:S(2)}, u32[]{:S(2)}) collective-permute-start(bf16[256,1280]{1,0:T(8,128)(2,1)S(1)} %collective-permute-done.one), channel_id=1, source_target_pairs={{1,0},{2,3},{5,4},{6,7},{9,8},{10,11},{13,12},{14,15},{17,16},{18,... | collective-permute-start | bytes 1966088 | tf_op jit(solution)/shard_map/ppermute | solution.py:24
  23.3 31.0 %collective-permute-start.2 = (bf16[1024,256]{1,0:T(8,128)(2,1)}, bf16[1024,256]{1,0:T(8,128)(2,1)S(1)}, u32[]{:S(2)}, u32[]{:S(2)}) collective-permute-start(bf16[1024,256]{1,0:T(8,128)(2,1)} %bitcast.18), channel_id=1, source_target_pairs={{0,4},{4,0},{1,5},{5,1},{2,6},{6,2},{3,7},{7,3},{8,12},{12,8},{9,1... | collective-permute-start | bytes 1572872 | tf_op jit(solution)/shard_map/ppermute | solution.py:24
  39.7 0.7 copy-start
  51.2 3.1 %copy-start.4 = (bf16[1,1024,1,256]{3,1,2,0:T(8,128)(2,1)S(1)}, bf16[1,1024,1,256]{3,1,2,0:T(8,128)(2,1)}, u32[]{:S(2)}) copy-start(bf16[1,1024,1,256]{3,1,2,0:T(8,128)(2,1)} %param.14) | copy-start | bytes 1572868
  52.7 5.5 %collective-permute-start.6 = (bf16[256,256]{1,0:T(8,128)(2,1)S(1)}, bf16[256,256]{1,0:T(8,128)(2,1)S(1)}, u32[]{:S(2)}, u32[]{:S(2)}) collective-permute-start(bf16[256,256]{1,0:T(8,128)(2,1)S(1)} %get-tuple-element.27.refs_1_), channel_id=1, source_target_pairs={{0,4},{4,0},{1,5},{5,1},{2,6},{6,2},{3,7},{7,3},{8,12},{12,8},{9,1... | collective-permute-start | bytes 393224 | tf_op jit(solution)/shard_map/ppermute | solution.py:24
  54.6 14.0 %collective-permute-start.7 = (bf16[256,1280]{1,0:T(8,128)(2,1)}, bf16[256,1280]{1,0:T(8,128)(2,1)S(1)}, u32[]{:S(2)}, u32[]{:S(2)}) collective-permute-start(bf16[256,1280]{1,0:T(8,128)(2,1)} %bitcast.2.own), channel_id=1, source_target_pairs={{0,8},{1,9},{2,10},{3,11},{8,16},{9,17},{10,18},{11,19},{16,24},{1... | collective-permute-start | bytes 1966088 | tf_op jit(solution)/shard_map/ppermute | solution.py:24
  54.7 3.5 %copy-start.1 = (s32[1,4]{1,0:T(1,128)S(1)}, s32[1,4]{1,0:T(1,128)}, u32[]{:S(2)}) copy-start(s32[1,4]{1,0:T(1,128)} %row_lengths.1) | copy-start | bytes 52
  54.7 3.5 %copy-start.2 = (s32[1,4]{1,0:T(1,128)S(1)}, s32[1,4]{1,0:T(1,128)}, u32[]{:S(2)}) copy-start(s32[1,4]{1,0:T(1,128)} %cache_lengths.1) | copy-start | bytes 52
  54.7 3.5 %copy-start.3 = (s32[1,4,1]{1,2,0:T(1,128)S(1)}, s32[1,4,1]{1,2,0:T(1,128)}, u32[]{:S(2)}) copy-start(s32[1,4,1]{1,2,0:T(1,128)} %param.17) | copy-start | bytes 52
  65.6 14.0 %collective-permute-start.10 = (bf16[256,1280]{1,0:T(8,128)(2,1)S(1)}, bf16[256,1280]{1,0:T(8,128)(2,1)S(1)}, u32[]{:S(2)}, u32[]{:S(2)}) collective-permute-start(bf16[256,1280]{1,0:T(8,128)(2,1)S(1)} %get-tuple-element.35), channel_id=1, source_target_pairs={{0,1},{3,2},{4,5},{7,6},{8,9},{11,10},{12,13},{15,14},{16,17},{19,... | collective-permute-start | bytes 1966088 | tf_op jit(solution)/shard_map/ppermute | solution.py:24
  67.7 20.1 %collective-permute-start.9 = (bf16[256,1280]{1,0:T(8,128)(2,1)S(1)}, bf16[256,1280]{1,0:T(8,128)(2,1)S(1)}, u32[]{:S(2)}, u32[]{:S(2)}) collective-permute-start(bf16[256,1280]{1,0:T(8,128)(2,1)S(1)} %get-tuple-element.35), channel_id=1, source_target_pairs={{1,10},{2,9},{9,18},{10,17},{17,26},{18,25},{25,2},{26,1},{5,14},{... | collective-permute-start | bytes 1966088 | tf_op jit(solution)/shard_map/ppermute | solution.py:24
  73.3 21.6 %collective-permute-start.8 = (bf16[256,1280]{1,0:T(8,128)(2,1)S(1)}, bf16[256,1280]{1,0:T(8,128)(2,1)S(1)}, u32[]{:S(2)}, u32[]{:S(2)}) collective-permute-start(bf16[256,1280]{1,0:T(8,128)(2,1)S(1)} %get-tuple-element.34), channel_id=1, source_target_pairs={{0,10},{3,9},{1,8},{2,11},{8,18},{11,17},{9,16},{10,19},{16,26},{1... | collective-permute-start | bytes 1966088 | tf_op jit(solution)/shard_map/ppermute | solution.py:24
  79.8 35.7 %collective-permute-start.11 = (bf16[256,1280]{1,0:T(8,128)(2,1)S(1)}, bf16[256,1280]{1,0:T(8,128)(2,1)S(1)}, u32[]{:S(2)}, u32[]{:S(2)}) collective-permute-start(bf16[256,1280]{1,0:T(8,128)(2,1)S(1)} %add_convert_fusion.1), channel_id=1, source_target_pairs={{0,9},{3,10},{1,11},{2,8},{8,17},{11,18},{9,19},{10,16},{16,25},{1... | collective-permute-start | bytes 1966088 | tf_op jit(solution)/shard_map/ppermute | solution.py:24
  87.2 28.6 %collective-permute-start.12 = (bf16[256,1280]{1,0:T(8,128)(2,1)S(1)}, bf16[256,1280]{1,0:T(8,128)(2,1)S(1)}, u32[]{:S(2)}, u32[]{:S(2)}) collective-permute-start(bf16[256,1280]{1,0:T(8,128)(2,1)S(1)} %get-tuple-element.38), channel_id=1, source_target_pairs={{0,8},{1,9},{2,10},{3,11},{8,16},{9,17},{10,18},{11,19},{16,24},{1... | collective-permute-start | bytes 1966088 | tf_op jit(solution)/shard_map/ppermute | solution.py:24
